TPU v7x, 32 devices: a whole 2x2x4 slice. The times are simulated.
32 devices in a mesh: dp: 16 (over z, x, core), seq: 2 (over y).
Axes of the slice: x: 2, y: 2, z: 4, core: 2. Of those that a mesh axis runs over, the one named last changes fastest.
Arguments:
- query_rows: bfloat16 [18432, 2048], P(('dp', 'seq')), may hold values from -500 to 500
- key_rows: bfloat16 [18432, 2048], P(('dp', 'seq')), may hold values from -5 to 5
- value_rows: bfloat16 [18432, 2048], P(('dp', 'seq')), may hold values from -6 to 6
- windows: int32 [16, 3], replicated, may hold values from 1 to 3, as said below
- out_weight: bfloat16 [2048, 3072], P('dp', 'seq'), may hold values from -0.125 to 0.125
- gate_scale: bfloat16 [16, 3072], P('dp', 'seq'), may hold values from 0.5 to 1.5
- out_grad: bfloat16 [18432, 3072], P('dp', 'seq'), may hold values from -0.046875 to 0.046875
Outputs:
- block_out: bfloat16 [18432, 3072], P('dp', 'seq')
- weight_grad: float32 [2048, 3072], P('dp', 'seq')
Inputs may be any that keep to these rules, and one draw needn't show every extreme that they name: `windows`: one head has extent 3 along all three dimensions.
All inputs are finite; a program needn't handle non-finite values.
Results may differ from a plain program's by a relative error of at most 0.0057.
Values may be sent and summed in bfloat16 or wider, within the bound.
No kernel may reach another device: no remote copies, remote signals or barrier semaphores. Data moves between devices by JAX's collectives and lax.ppermute only.
A program may use at most 192 MiB of HBM per device.

v0:
```python
import functools
import math

import jax
import jax.numpy as jnp
import numpy as np
from jax import lax
from jax.experimental import pallas as pl
from jax.experimental.pallas import tpu as pltpu
from jax.sharding import PartitionSpec as P

HEADS = 16
HEAD_DIM = 128
GH = 3
GW = 4
GT = 2
TILE = 48
NT = 24
CLIP_TOK = NT * TILE
Q_ROWS = GW * TILE
LOG2_SCALE = math.log2(math.e) / math.sqrt(HEAD_DIM)
VMEM_LIMIT = 16 * 1024 * 1024
VMEM_GRADIENT = 20 * 1024 * 1024
VMEM_PROJECT = 24 * 1024 * 1024
PROJECT_STEPS = 6
GRADIENT_STEPS = 3
JOIN_STEPS = 4
SEQ, CORE, X, LOW, HIGH = range(5)
VMEM_WHOLE = 60 * 1024 * 1024
VMEM_SMALL = 12 * 1024 * 1024
SMALL_COST = pl.CostEstimate(flops=1, bytes_accessed=1, transcendentals=0)
LONG_COST = pl.CostEstimate(flops=2 * 10**10, bytes_accessed=2 * 10**7, transcendentals=0)


def window_bias(windows):
    tile_id = np.arange(NT)
    coords = np.stack([tile_id // (GH * GW), tile_id // GW % GH, tile_id % GW]).astype(np.int32)
    token_coords = np.repeat(coords, TILE, axis=1)
    inside = None
    for axis_no, limit in enumerate((GT, GH, GW)):
        extent = jnp.minimum(windows[:, axis_no], limit)[:, None]
        start = jnp.clip(coords[axis_no][None, :] - (extent - 1) // 2, 0, limit - extent)
        column = token_coords[axis_no][None, None, :]
        here = (column >= start[:, :, None]) & (column < (start + extent)[:, :, None])
        inside = here if inside is None else inside & here
    return jnp.where(inside, 0.0, -jnp.inf).astype(jnp.float32)


def attend_rows(queries, first_tile, bias_ref, keys, values):
    count = queries.shape[0]
    tiles = count // TILE
    scores = lax.dot_general(
        queries, keys, (((1,), (1,)), ((), ())), preferred_element_type=jnp.float32
    )
    bias = bias_ref[0, first_tile : first_tile + tiles, :]
    scores = (scores.reshape(tiles, TILE, CLIP_TOK) + bias[:, None, :]).reshape(count, CLIP_TOK)
    peak = jnp.max(scores, axis=-1, keepdims=True)
    weights = jnp.exp2((scores - peak) * LOG2_SCALE).astype(jnp.bfloat16)
    blended = jnp.dot(weights, values, preferred_element_type=jnp.float32)
    return (blended[:, :HEAD_DIM] / blended[:, HEAD_DIM:]).astype(jnp.bfloat16)


def fill_values(values_ref, parts):
    at = 0
    for part in parts:
        rows = part.shape[0]
        values_ref[at : at + rows, :HEAD_DIM] = part
        at += rows
    values_ref[:, HEAD_DIM:] = jnp.ones((CLIP_TOK, HEAD_DIM), jnp.bfloat16)


def pair_kernel(place_ref, q_ref, k_ref, v_ref, other_ref, bias_ref, *rest):
    out_ref, keys_ref, values_ref = rest[-3:]
    half = CLIP_TOK // 2
    keys_ref[:half, :] = k_ref[...]
    keys_ref[half:, :] = other_ref[1]
    fill_values(values_ref, (v_ref[...], other_ref[2]))
    keys = keys_ref[...]
    values = values_ref[...]
    for side in range(2):
        base = pl.multiple_of((place_ref[0] if side == 0 else 1 - place_ref[0]) * half, half)
        for at in range(0, half, Q_ROWS):
            queries = q_ref[at : at + Q_ROWS, :] if side == 0 else other_ref[0, at : at + Q_ROWS, :]
            first_tile = (side * half + at) // TILE
            out_ref[pl.ds(base + at, Q_ROWS), :] = attend_rows(
                queries, first_tile, bias_ref, keys, values
            )


def whole_kernel(place_ref, q_ref, k_ref, v_ref, bias_ref, out_ref, values_ref):
    fill_values(values_ref, (v_ref[...],))
    keys = k_ref[...]
    values = values_ref[...]
    for at in range(0, CLIP_TOK, Q_ROWS):
        out_ref[at : at + Q_ROWS, :] = attend_rows(
            q_ref[at : at + Q_ROWS, :], at // TILE, bias_ref, keys, values
        )


def attention_cost(heads):
    pairs = heads * CLIP_TOK * CLIP_TOK
    return pl.CostEstimate(
        flops=pairs * HEAD_DIM * 6,
        bytes_accessed=heads * CLIP_TOK * HEAD_DIM * 8,
        transcendentals=pairs,
    )


def attend_pair(place, local_heads, call, query, key, value, other, bias, earlier, limit):
    half = CLIP_TOK // 2
    count = 2

    def head(i, place_ref):
        return place_ref[SEQ] * local_heads + local_head(call, place_ref[SEQ], i)

    own = pl.BlockSpec((half, HEAD_DIM), lambda i, p: (0, head(i, p)))
    return pl.pallas_call(
        pair_kernel,
        grid_spec=pltpu.PrefetchScalarGridSpec(
            num_scalar_prefetch=1,
            grid=(count,),
            in_specs=[
                own,
                own,
                own,
                pl.BlockSpec((3, half, HEAD_DIM), lambda i, p: (0, 0, i)),
                pl.BlockSpec((1, NT, CLIP_TOK), lambda i, p: (head(i, p), 0, 0)),
            ]
            + [pl.BlockSpec(memory_space=pl.ANY)] * len(earlier),
            out_specs=pl.BlockSpec((CLIP_TOK, HEAD_DIM), lambda i, p: (0, i)),
            scratch_shapes=[
                pltpu.VMEM((CLIP_TOK, HEAD_DIM), jnp.bfloat16),
                pltpu.VMEM((CLIP_TOK, 2 * HEAD_DIM), jnp.bfloat16),
            ],
        ),
        out_shape=jax.ShapeDtypeStruct((CLIP_TOK, count * HEAD_DIM), jnp.bfloat16),
        compiler_params=pltpu.CompilerParams(vmem_limit_bytes=limit),
        cost_estimate=SMALL_COST,
    )(place, query, key, value, other, bias, *earlier)


def attend_whole(place, query, key, value, bias):
    local_heads = query.shape[1] // HEAD_DIM
    column = pl.BlockSpec((CLIP_TOK, HEAD_DIM), lambda i, p: (0, i))
    return pl.pallas_call(
        whole_kernel,
        grid_spec=pltpu.PrefetchScalarGridSpec(
            num_scalar_prefetch=1,
            grid=(local_heads,),
            in_specs=[
                column,
                column,
                column,
                pl.BlockSpec((1, NT, CLIP_TOK), lambda i, p: (p[0] * local_heads + i, 0, 0)),
            ],
            out_specs=column,
            scratch_shapes=[pltpu.VMEM((CLIP_TOK, 2 * HEAD_DIM), jnp.bfloat16)],
        ),
        out_shape=jax.ShapeDtypeStruct(query.shape, jnp.bfloat16),
        compiler_params=pltpu.CompilerParams(vmem_limit_bytes=VMEM_LIMIT),
        cost_estimate=attention_cost(local_heads),
    )(place, query, key, value, bias)


def pack_kernel(place_ref, q_ref, k_ref, v_ref, *rest):
    out_ref = rest[-1]
    out_ref[0] = q_ref[...]
    out_ref[1] = k_ref[...]
    out_ref[2] = v_ref[...]


def local_head(call, side, part):
    first, by_side, step = call
    return first + by_side * side + step * part


def pack_partner(place, local_heads, call, query, key, value, earlier, limit):
    rows = query.shape[0]
    count = 2

    def head(i, place_ref):
        side = 1 - place_ref[SEQ]
        return side * local_heads + local_head(call, side, i)

    column = pl.BlockSpec((rows, HEAD_DIM), lambda i, p: (0, head(i, p)))
    return pl.pallas_call(
        pack_kernel,
        grid_spec=pltpu.PrefetchScalarGridSpec(
            num_scalar_prefetch=1,
            grid=(count,),
            in_specs=[column, column, column]
            + [pl.BlockSpec(memory_space=pl.ANY)] * len(earlier),
            out_specs=pl.BlockSpec((3, rows, HEAD_DIM), lambda i, p: (0, 0, i)),
        ),
        out_shape=jax.ShapeDtypeStruct((3, rows, count * HEAD_DIM), jnp.bfloat16),
        compiler_params=pltpu.CompilerParams(vmem_limit_bytes=limit),
        cost_estimate=SMALL_COST,
    )(place, query, key, value, *earlier)


def whole_block(shape):
    return pl.BlockSpec(shape, lambda i, p: (0,) * len(shape), pipeline_mode=pl.Buffered(1))


def gradient_kernel(place_ref, *refs, by_call):
    count = 4 if by_call else 2
    grad_ref = refs[count]
    sent_ref, kept_ref, rows_ref = refs[-3:]
    first_core = place_ref[CORE] == 0
    sides = (place_ref[SEQ], 1 - place_ref[SEQ])

    @pl.when(pl.program_id(0) == 0)
    def _():
        sent, kept = [], []
        for n in range(2):
            if by_call:
                one, two = refs[2 + n][...], refs[n][...]
            else:
                one, two = refs[n][:, :HEAD_DIM], refs[n][:, HEAD_DIM:]
            sent.append(jnp.where(first_core, one, two))
            kept.append(jnp.where(first_core, two, one))
        rows_ref[...] = jnp.concatenate(sent + kept, axis=1).T

    each = 2 if by_call else 1
    product = jnp.dot(rows_ref[...], grad_ref[...], preferred_element_type=jnp.float32)
    product = product.astype(jnp.bfloat16).reshape(4 * each, HEAD_DIM, grad_ref.shape[1])
    for n, side in enumerate(sides):
        sent_ref[pl.ds(each * side, each)] = product[each * n : each * (n + 1)]
        kept_ref[pl.ds(each * side, each)] = product[each * (2 + n) : each * (3 + n)]


def batch_gradient(place, sources, grad_proj, earlier=(), cost=SMALL_COST):
    by_call = len(sources) == 4
    heads = len(sources)
    rows, columns = grad_proj.shape
    step = columns // GRADIENT_STEPS
    out = pl.BlockSpec((heads, HEAD_DIM, step), lambda i, p: (0, 0, i))
    result = jax.ShapeDtypeStruct((heads, HEAD_DIM, columns), jnp.bfloat16)
    return pl.pallas_call(
        functools.partial(gradient_kernel, by_call=by_call),
        grid_spec=pltpu.PrefetchScalarGridSpec(
            num_scalar_prefetch=1,
            grid=(GRADIENT_STEPS,),
            in_specs=[whole_block(each.shape) for each in sources]
            + [pl.BlockSpec((rows, step), lambda i, p: (0, i))]
            + [pl.BlockSpec(memory_space=pl.ANY)] * len(earlier),
            out_specs=[out, out],
            scratch_shapes=[pltpu.VMEM((2 * heads * HEAD_DIM, rows), jnp.bfloat16)],
        ),
        out_shape=[result, result],
        compiler_params=pltpu.CompilerParams(vmem_limit_bytes=VMEM_GRADIENT),
        cost_estimate=cost,
    )(place, *sources, grad_proj, *earlier)


def sum_of(blocks):
    total = blocks[0].astype(jnp.float32)
    for block in blocks[1:]:
        total = total + block.astype(jnp.float32)
    return total


def level_step(place, bit, terms, earlier=(), cost=SMALL_COST):
    count = len(terms)
    pairs = terms[0].shape[0] // 2
    shape = (pairs,) + terms[0].shape[1:]
    block = (1,) + terms[0].shape[1:]
    keep = pl.BlockSpec(block, lambda i, p: (2 * i + p[bit], 0, 0))
    send = pl.BlockSpec(block, lambda i, p: (2 * i + 1 - p[bit], 0, 0))
    out = pl.BlockSpec(block, lambda i, p: (i, 0, 0))

    def kernel(place_ref, *refs):
        kept_ref, sent_ref = refs[-2:]
        kept_ref[...] = sum_of([ref[...] for ref in refs[:count]])
        sent_ref[...] = sum_of([ref[...] for ref in refs[count : 2 * count]]).astype(jnp.bfloat16)

    return pl.pallas_call(
        kernel,
        grid_spec=pltpu.PrefetchScalarGridSpec(
            num_scalar_prefetch=1,
            grid=(pairs,),
            in_specs=[keep] * count
            + [send] * count
            + [pl.BlockSpec(memory_space=pl.ANY)] * len(earlier),
            out_specs=[out, out],
        ),
        out_shape=[
            jax.ShapeDtypeStruct(shape, jnp.float32),
            jax.ShapeDtypeStruct(shape, jnp.bfloat16),
        ],
        compiler_params=pltpu.CompilerParams(vmem_limit_bytes=VMEM_SMALL),
        cost_estimate=cost,
    )(place, *terms, *terms, *earlier)


def reach_step(place, terms, earlier=()):
    count = len(terms)
    block = (1,) + terms[0].shape[1:]
    near = pl.BlockSpec(block, lambda i, p: (p[HIGH], 0, 0))
    far = pl.BlockSpec(block, lambda i, p: (1 - p[HIGH], 0, 0))

    def kernel(place_ref, *refs):
        kept_ref, near_ref, far_ref = refs[-3:]
        total = sum_of([ref[...] for ref in refs[:count]])
        kept_ref[...] = total
        near_ref[...] = total.astype(jnp.bfloat16)
        far_ref[...] = sum_of([ref[...] for ref in refs[count : 2 * count]]).astype(jnp.bfloat16)

    return pl.pallas_call(
        kernel,
        grid_spec=pltpu.PrefetchScalarGridSpec(
            num_scalar_prefetch=1,
            grid=(1,),
            in_specs=[near] * count
            + [far] * count
            + [pl.BlockSpec(memory_space=pl.ANY)] * len(earlier),
            out_specs=[whole_block(block)] * 3,
        ),
        out_shape=[
            jax.ShapeDtypeStruct(block, kind) for kind in (jnp.float32, jnp.bfloat16, jnp.bfloat16)
        ],
        compiler_params=pltpu.CompilerParams(vmem_limit_bytes=VMEM_SMALL),
        cost_estimate=SMALL_COST,
    )(place, *terms, *terms, *earlier)


def total_step(terms, earlier=(), kind=jnp.bfloat16):
    block = pl.BlockSpec((1,) + terms[0].shape[1:], lambda i: (i, 0, 0))

    def kernel(*refs):
        refs[-1][...] = sum_of([ref[...] for ref in refs[: len(terms)]]).astype(kind)

    return pl.pallas_call(
        kernel,
        grid=(terms[0].shape[0],),
        in_specs=[block] * len(terms) + [pl.BlockSpec(memory_space=pl.ANY)] * len(earlier),
        out_specs=block,
        out_shape=jax.ShapeDtypeStruct(terms[0].shape, kind),
        compiler_params=pltpu.CompilerParams(vmem_limit_bytes=VMEM_SMALL),
        cost_estimate=SMALL_COST,
    )(*terms, *earlier)


def choose_owned(place, *batches):
    block = batches[0][0].shape
    terms = [term for batch in batches for term in batch]

    def kernel(place_ref, *refs):
        alike = place_ref[CORE] == place_ref[X]
        outer = place_ref[LOW] == place_ref[HIGH]
        owned = (alike, ~alike & outer, ~alike & ~outer)
        at = 0
        for batch, mine in zip(batches, owned):
            chosen = refs[at : at + len(batch)]
            at += len(batch)

            @pl.when(mine)
            def _():
                refs[-1][...] = sum_of([ref[0] for ref in chosen])

    return pl.pallas_call(
        kernel,
        grid_spec=pltpu.PrefetchScalarGridSpec(
            num_scalar_prefetch=1,
            grid=(1,),
            in_specs=[whole_block(block)] * len(terms),
            out_specs=whole_block(block[1:]),
        ),
        out_shape=jax.ShapeDtypeStruct(block[1:], jnp.float32),
        compiler_params=pltpu.CompilerParams(vmem_limit_bytes=VMEM_GRADIENT),
        cost_estimate=SMALL_COST,
    )(place, *terms)


def join_columns(place, sources, calls, local_heads, earlier, cost):
    rows = sources[0].shape[0]
    step = rows // JOIN_STEPS
    shape = (rows, HEADS * HEAD_DIM)

    def kernel(place_ref, *refs):
        out_ref, done_ref = refs[-2:]
        done_ref[...] = jnp.zeros_like(done_ref)
        for n, source in enumerate(refs[: len(sources)]):
            side = place_ref[SEQ] if n % 2 == 0 else 1 - place_ref[SEQ]
            for part in range(2):
                head = side * local_heads + local_head(calls[n // 2], side, part)
                at = pl.multiple_of(head * HEAD_DIM, HEAD_DIM)
                out_ref[:, pl.ds(at, HEAD_DIM)] = source[:, part * HEAD_DIM : (part + 1) * HEAD_DIM]

    return pl.pallas_call(
        kernel,
        grid_spec=pltpu.PrefetchScalarGridSpec(
            num_scalar_prefetch=1,
            grid=(JOIN_STEPS,),
            in_specs=[pl.BlockSpec((step, each.shape[1]), lambda i, p: (i, 0)) for each in sources]
            + [pl.BlockSpec(memory_space=pl.ANY)] * len(earlier),
            out_specs=[
                pl.BlockSpec((step, shape[1]), lambda i, p: (i, 0)),
                pl.BlockSpec((8, HEAD_DIM), lambda i, p: (0, 0)),
            ],
        ),
        out_shape=[
            jax.ShapeDtypeStruct(shape, jnp.bfloat16),
            jax.ShapeDtypeStruct((8, HEAD_DIM), jnp.float32),
        ],
        compiler_params=pltpu.CompilerParams(vmem_limit_bytes=VMEM_SMALL),
        cost_estimate=cost,
    )(place, *sources, *earlier)


def project(attention, weight, gate, span, filled=(), earlier=(), cost=SMALL_COST):
    rows, depth = attention.shape
    columns = weight.shape[1]
    step = columns // PROJECT_STEPS
    first, steps = span[0], len(span)

    def kernel(attention_ref, weight_ref, gate_ref, *refs):
        out_ref, done_ref = refs[-2:]
        done_ref[...] = jnp.zeros_like(done_ref)
        total = jnp.dot(attention_ref[...], weight_ref[...], preferred_element_type=jnp.float32)
        out_ref[...] = (total * gate_ref[...]).astype(out_ref.dtype)

    return pl.pallas_call(
        kernel,
        grid=(steps,),
        in_specs=[
            pl.BlockSpec((rows, depth), lambda i: (0, 0), pipeline_mode=pl.Buffered(1)),
            pl.BlockSpec((depth, step), lambda i: (0, first + i)),
            pl.BlockSpec((1, step), lambda i: (0, first + i)),
        ]
        + [pl.BlockSpec(memory_space=pl.ANY)] * (len(filled) + len(earlier)),
        out_specs=[
            pl.BlockSpec((rows, step), lambda i: (0, first + i)),
            pl.BlockSpec((8, HEAD_DIM), lambda i: (0, 0)),
        ],
        out_shape=[
            jax.ShapeDtypeStruct((rows, columns), jnp.bfloat16),
            jax.ShapeDtypeStruct((8, HEAD_DIM), jnp.float32),
        ],
        input_output_aliases={3: 0} if filled else {},
        compiler_params=pltpu.CompilerParams(vmem_limit_bytes=VMEM_PROJECT),
        cost_estimate=cost,
    )(attention, weight, gate, *filled, *earlier)


def contract_tokens(columns, grad_proj, kind):
    return lax.dot_general(
        columns, grad_proj, (((0,), (0,)), ((), ())), preferred_element_type=jnp.float32
    ).astype(kind)


def after(value, *earlier):
    return lax.optimization_barrier((value,) + earlier)[0]


def dp_send(value, flip, sender):
    return lax.ppermute(value, "dp", [(i, i ^ flip) for i in range(HEADS) if sender(i)])


def same_bits(i):
    return (i >> 1 ^ i) & 1 == 0


def paired_device(query_rows, key_rows, value_rows, windows, out_weight, gate_scale, out_grad):
    index = lax.axis_index("dp")
    place = jnp.stack([lax.axis_index("seq")] + [index >> bit & 1 for bit in range(4)])
    place = lax.optimization_barrier(place.astype(jnp.int32))
    local_heads = HEADS // 2
    swap = [(0, 1), (1, 0)]
    calls = [(0, 0, 4), (3, 0, 4), (1, 4, 1), (5, -4, 1)]
    bias = window_bias(windows)
    weight = lax.all_gather(out_weight, "dp", axis=0, tiled=True)
    gate_row = gate_scale[0].astype(jnp.float32)
    grad_proj = (out_grad.astype(jnp.float32) * gate_row).astype(jnp.bfloat16)
    sources = (query_rows, key_rows, value_rows)

    def pack(n, limit, *earlier):
        return pack_partner(place, local_heads, calls[n], *sources, earlier, limit)

    def attention(n, other, *earlier, limit=VMEM_LIMIT):
        return attend_pair(place, local_heads, calls[n], *sources, other, bias, earlier, limit)

    def exchange(mine):
        return lax.ppermute(mine, "seq", swap)

    def core_step(*operands):
        sent, kept = batch_gradient(place, operands[:4], operands[4])
        return total_step([kept, dp_send(sent, 1, lambda i: True)])

    def apart(step, *operands):
        shapes = jax.eval_shape(step, *operands)
        return lax.cond(
            windows[0, 0] > 0,
            step,
            lambda *_: jax.tree.map(lambda leaf: jnp.zeros(leaf.shape, leaf.dtype), shapes),
            *operands,
        )

    packed0 = pack(0, VMEM_WHOLE)
    packed1 = pack(1, VMEM_WHOLE, packed0)
    packed2 = pack(2, VMEM_LIMIT, packed1)
    other0 = exchange(packed0)
    other1 = exchange(packed1)
    other2 = exchange(packed2)
    mine0 = attention(0, other0, packed2)
    theirs0 = exchange(mine0)
    mine1 = attention(1, other1, mine0)
    theirs1 = exchange(mine1)
    packed3 = pack(3, VMEM_LIMIT, mine1)
    other3 = exchange(packed3)
    mine2 = attention(2, other2, mine1, packed3)
    theirs2 = exchange(mine2)

    def unlike(i):
        return not same_bits(i)

    def outer(i):
        return unlike(i) and (i >> 2 ^ i >> 3) & 1 == 0

    def inner(i):
        return unlike(i) and (i >> 2 ^ i >> 3) & 1 == 1

    first = (mine0, theirs0, mine1, theirs1)
    total_a = apart(core_step, after(mine0, mine2, weight), *first[1:], grad_proj)
    across_a = dp_send(total_a, 2, unlike)
    mine3 = attention(3, other3, total_a, limit=VMEM_WHOLE)
    theirs3 = exchange(mine3)
    sent_b, kept_b = batch_gradient(place, (mine2, theirs2), grad_proj, (mine3,), LONG_COST)
    came_b = dp_send(sent_b, 1, lambda i: True)
    kept_a, sent_a = level_step(place, LOW, [total_a, across_a], (sent_b,), LONG_COST)
    low_a = dp_send(sent_a, 4, same_bits)
    total_b = total_step([kept_b, came_b], (sent_a,))
    across_b = dp_send(total_b, 2, same_bits)
    sent_c, kept_c = batch_gradient(place, (mine3, theirs3), grad_proj, (total_b,))
    came_c = dp_send(sent_c, 1, lambda i: True)
    results = (*first, mine2, theirs2, mine3, theirs3)
    columns, done = join_columns(place, results, calls, local_heads, (sent_c,), LONG_COST)
    total_c = total_step([kept_c, came_c], (done,))
    across_c = dp_send(total_c, 2, same_bits)
    kept_a, sent_a = level_step(place, HIGH, [kept_a, low_a], (total_c,))
    high_a = dp_send(sent_a, 8, same_bits)
    sent_b = total_step([total_b, across_b], (sent_a,))
    low_b = dp_send(sent_b, 4, inner)
    gate = gate_row[None]
    out, done = project(columns, weight, gate, range(3), (), (sent_b,))
    kept_c, near_c, far_c = reach_step(place, [total_c, across_c], (done,))
    reached_c = dp_send(far_c, 8, outer), dp_send(far_c, 12, inner), dp_send(near_c, 4, outer)
    kept_b, sent_b = level_step(place, HIGH, [total_b, across_b, low_b], (near_c,))
    high_b = dp_send(sent_b, 12, outer)
    block_out, done = project(columns, weight, gate, range(3, PROJECT_STEPS), (out,), (sent_b,))
    final_a = total_step([kept_a, high_a], (done,), jnp.float32)
    weight_grad = choose_owned(place, (final_a,), (kept_b, high_b), (kept_c, *reached_c))
    return (block_out, weight_grad)


def general_device(query_rows, key_rows, value_rows, windows, out_weight, gate_scale, out_grad):
    query, key, value = (
        lax.all_to_all(rows, "seq", split_axis=1, concat_axis=0, tiled=True)
        for rows in (query_rows, key_rows, value_rows)
    )
    place = lax.axis_index("seq").reshape(1).astype(jnp.int32)
    mine = attend_whole(place, query, key, value, window_bias(windows))
    columns = lax.all_gather(mine, "seq", axis=1, tiled=True)
    weight = lax.all_gather(out_weight, "dp", axis=0, tiled=True)
    gate_row = gate_scale[0].astype(jnp.float32)
    projected = jnp.dot(columns, weight, preferred_element_type=jnp.float32)
    block_out = (projected * gate_row).astype(jnp.bfloat16)
    grad_proj = (out_grad.astype(jnp.float32) * gate_row).astype(jnp.bfloat16)
    weight_grad = lax.psum_scatter(
        contract_tokens(columns, grad_proj, jnp.float32), "dp", scatter_dimension=0, tiled=True
    )
    return (block_out, weight_grad)


def solution(mesh):
    paired = mesh.shape["seq"] == 2 and mesh.shape["dp"] == HEADS
    return jax.shard_map(
        paired_device if paired else general_device,
        mesh=mesh,
        in_specs=(
            P(("dp", "seq"), None),
            P(("dp", "seq"), None),
            P(("dp", "seq"), None),
            P(),
            P("dp", "seq"),
            P("dp", "seq"),
            P("dp", "seq"),
        ),
        out_specs=(P("dp", "seq"), P("dp", "seq")),
        check_vma=False,
    )
```

profile of v0, /device:TPU:2, one launch (start us, length us, event | category | flops | bytes accessed | tf_op | source)
XLA Modules:
  0.0 198.9 jit_solution(17548296737706396987)
XLA Ops:
  8.0 2.6 %shard_map.140.rest_0_ = bf16[3,576,256]{2,1,0:T(8,128)(2,1)} custom-call(s32[5]{0:T(128)S(1)} %stack.23.place_ref, bf16[576,2048]{1,0:T(8,128)(2,1)} %q_ref.15, bf16[576,2048]{1,0:T(8,128)(2,1)} %k_ref.15, bf16[576,2048]{1,0:T(8,128)(2,1)} %v_ref.15), custom_call_target="tpu_custom_call" | custom-call | flops 1 | bytes 1 | tf_op jit(solution)/shard_map/pallas_call | solution.py:186
  12.1 2.7 %shard_map.141.rest_0_ = bf16[3,576,256]{2,1,0:T(8,128)(2,1)} custom-call(s32[5]{0:T(128)S(1)} %stack.23.place_ref, bf16[576,2048]{1,0:T(8,128)(2,1)} %q_ref.15, bf16[576,2048]{1,0:T(8,128)(2,1)} %k_ref.15, bf16[576,2048]{1,0:T(8,128)(2,1)} %v_ref.15, bf16[3,576,256]{2,1,0:T(8,128)(2,1)} %shard_map.140.rest_0_), custom_call_target="tpu_custom_call" | custom-call | flops 1 | bytes 1 | tf_op jit(solution)/shard_map/pallas_call | solution.py:186
  15.4 1.7 copy-done.1
  17.0 1.7 copy-done.2
  21.1 1.6 collective-permute-start.5
  23.7 9.6 %collective-permute-done.1.other_ref = bf16[3,576,256]{2,1,0:T(8,128)(2,1)S(1)} collective-permute-done((bf16[3,576,256]{2,1,0:T(8,128)(2,1)}, bf16[3,576,256]{2,1,0:T(8,128)(2,1)S(1)}, u32[]{:S(2)}, u32[]{:S(2)}) %collective-permute-start.1) | collective-permute-done | bytes 884768 | tf_op jit(solution)/shard_map/ppermute | solution.py:484
  33.4 7.3 %shard_map.143.rest_0_.refs_0_ = bf16[1152,256]{1,0:T(8,128)(2,1)} custom-call(s32[5]{0:T(128)S(1)} %stack.23.place_ref, bf16[576,2048]{1,0:T(8,128)(2,1)S(1)} %copy-done, bf16[576,2048]{1,0:T(8,128)(2,1)S(1)} %copy-done.1, bf16[576,2048]{1,0:T(8,128)(2,1)S(1)} %copy-done.2, bf16[3,576,256]{2,1,0:T(8,128)(2,1)S(1)} %collective-permute-done.1.other_ref, ...), custom_call_target="tpu_custom_call" | custom-call | flops 1 | bytes 1 | tf_op jit(solution)/shard_map/pallas_call | solution.py:117
  40.6 11.7 %collective-permute-done.3.other_ref = bf16[3,576,256]{2,1,0:T(8,128)(2,1)S(1)} collective-permute-done((bf16[3,576,256]{2,1,0:T(8,128)(2,1)}, bf16[3,576,256]{2,1,0:T(8,128)(2,1)S(1)}, u32[]{:S(2)}, u32[]{:S(2)}) %collective-permute-start.3) | collective-permute-done | bytes 884768 | tf_op jit(solution)/shard_map/ppermute | solution.py:484
  52.3 7.3 %shard_map.144.rest_0_.refs_2_ = bf16[1152,256]{1,0:T(8,128)(2,1)} custom-call(s32[5]{0:T(128)S(1)} %stack.23.place_ref, bf16[576,2048]{1,0:T(8,128)(2,1)S(1)} %copy-done, bf16[576,2048]{1,0:T(8,128)(2,1)S(1)} %copy-done.1, bf16[576,2048]{1,0:T(8,128)(2,1)S(1)} %copy-done.2, bf16[3,576,256]{2,1,0:T(8,128)(2,1)S(1)} %collective-permute-done.3.other_ref, ...), custom_call_target="tpu_custom_call" | custom-call | flops 1 | bytes 1 | tf_op jit(solution)/shard_map/pallas_call | solution.py:117
  64.4 6.9 %collective-permute-done.5.other_ref = bf16[3,576,256]{2,1,0:T(8,128)(2,1)S(1)} collective-permute-done((bf16[3,576,256]{2,1,0:T(8,128)(2,1)S(1)}, bf16[3,576,256]{2,1,0:T(8,128)(2,1)S(1)}, u32[]{:S(2)}, u32[]{:S(2)}) %collective-permute-start.5) | collective-permute-done | bytes 884768 | tf_op jit(solution)/shard_map/ppermute | solution.py:484
  71.3 7.3 %shard_map.146.refs_0_.refs_4_ = bf16[1152,256]{1,0:T(8,128)(2,1)} custom-call(s32[5]{0:T(128)S(1)} %stack.23.place_ref, bf16[576,2048]{1,0:T(8,128)(2,1)S(1)} %copy-done, bf16[576,2048]{1,0:T(8,128)(2,1)S(1)} %copy-done.1, bf16[576,2048]{1,0:T(8,128)(2,1)S(1)} %copy-done.2, bf16[3,576,256]{2,1,0:T(8,128)(2,1)S(1)} %collective-permute-done.5.other_ref, ...), custom_call_target="tpu_custom_call" | custom-call | flops 1 | bytes 1 | tf_op jit(solution)/shard_map/pallas_call | solution.py:117
  80.1 2.6 %multiply_convert_fusion.refs_2_ = bf16[1152,1536]{1,0:T(8,128)(2,1)} fusion(bf16[1152,1536]{1,0:T(8,128)(2,1)S(1)} %copy-done.8, f32[1536]{0:T(1024)S(1)} %convert_reduce_fusion), kind=kLoop, calls=%fused_computation | loop fusion | flops 5308416 | bytes 7084032 | tf_op jit(solution)/shard_map/convert_element_type | solution.py:474
  84.0 12.6 %collective-permute-done.2.refs_1_ = bf16[1152,256]{1,0:T(8,128)(2,1)} collective-permute-done((bf16[1152,256]{1,0:T(8,128)(2,1)}, bf16[1152,256]{1,0:T(8,128)(2,1)}, u32[]{:S(2)}, u32[]{:S(2)}) %collective-permute-start.2) | collective-permute-done | bytes 589856 | tf_op jit(solution)/shard_map/ppermute | solution.py:484
  96.7 13.3 %conditional.1 = (bf16[4,128,1536]{2,1,0:T(8,128)(2,1)}) conditional(s32[]{:T(128)} %bitcast.14, () %tuple.15, (s32[5]{0:T(128)S(1)}, bf16[1152,256]{1,0:T(8,128)(2,1)}, bf16[1152,256]{1,0:T(8,128)(2,1)}, bf16[1152,256]{1,0:T(8,128)(2,1)}, bf16[1152,256]{1,0:T(8,128)(2,1)}, /*index=5*/bf16[1152,1536]{1,0:T(8,128)(2,1)}) %tuple.17), branch_computations={%region_0.1_spmd, %region_1.2_spmd} | conditional | flops 2 | bytes 6291506 | solution.py:492
  96.7 8.0 %branch_1_fun.2 = (bf16[4,128,1536]{2,1,0:T(8,128)(2,1)S(1)}, bf16[4,128,1536]{2,1,0:T(8,128)(2,1)S(1)}) custom-call(s32[5]{0:T(128)S(1)} %get-tuple-element.5.place_ref, bf16[1152,256]{1,0:T(8,128)(2,1)} %get-tuple-element.16.refs_0_, bf16[1152,256]{1,0:T(8,128)(2,1)} %get-tuple-element.17.refs_1_, bf16[1152,256]{1,0:T(8,128)(2,1)} %get-tuple-element.18.refs_2_, ...), custom_call_target="tpu_custom_call" | custom-call | flops 1 | bytes 1 | tf_op jit(solution)/shard_map/cond/branch_1_fun/pallas_call | solution.py:239
  104.8 3.4 %collective-permute-done.refs_1_ = bf16[4,128,1536]{2,1,0:T(8,128)(2,1)S(1)} collective-permute-done((bf16[4,128,1536]{2,1,0:T(8,128)(2,1)S(1)}, bf16[4,128,1536]{2,1,0:T(8,128)(2,1)S(1)}, u32[]{:S(2)}, u32[]{:S(2)}) %collective-permute-start) | collective-permute-done | bytes 1572896 | tf_op jit(solution)/shard_map/cond/branch_1_fun/ppermute | solution.py:457
  108.1 1.9 branch_1_fun.3
  110.0 2.0 %collective-permute-start.10 = (bf16[4,128,1536]{2,1,0:T(8,128)(2,1)}, bf16[4,128,1536]{2,1,0:T(8,128)(2,1)S(1)}, u32[]{:S(2)}, u32[]{:S(2)}) collective-permute-start(bf16[4,128,1536]{2,1,0:T(8,128)(2,1)} %get-tuple-element.82.rest_0_.refs_0_.refs_2_), channel_id=1, source_target_pairs={{2,6},{4,0},{10,14},{12,8},{18,22},{20,16},{26,30},{28,24},{3,7},{... | collective-permute-start | bytes 4718600 | tf_op jit(solution)/shard_map/ppermute | solution.py:457
  112.0 3.6 %collective-permute-done.7.other_ref = bf16[3,576,256]{2,1,0:T(8,128)(2,1)} collective-permute-done((bf16[3,576,256]{2,1,0:T(8,128)(2,1)S(1)}, bf16[3,576,256]{2,1,0:T(8,128)(2,1)}, u32[]{:S(2)}, u32[]{:S(2)}) %collective-permute-start.7) | collective-permute-done | bytes 884768 | tf_op jit(solution)/shard_map/ppermute | solution.py:484
  115.6 8.1 %shard_map.147.refs_3_.refs_0_.refs_6_ = bf16[1152,256]{1,0:T(8,128)(2,1)} custom-call(s32[5]{0:T(128)S(1)} %stack.23.place_ref, bf16[576,2048]{1,0:T(8,128)(2,1)} %q_ref.15, bf16[576,2048]{1,0:T(8,128)(2,1)} %k_ref.15, bf16[576,2048]{1,0:T(8,128)(2,1)} %v_ref.15, bf16[3,576,256]{2,1,0:T(8,128)(2,1)} %collective-permute-done.7.other_ref, ...), custom_call_target="tpu_custom_call" | custom-call | flops 1 | bytes 1 | tf_op jit(solution)/shard_map/pallas_call | solution.py:117
  125.2 2.9 %collective-permute-done.6.refs_1_.refs_5_ = bf16[1152,256]{1,0:T(8,128)(2,1)S(1)} collective-permute-done((bf16[1152,256]{1,0:T(8,128)(2,1)}, bf16[1152,256]{1,0:T(8,128)(2,1)S(1)}, u32[]{:S(2)}, u32[]{:S(2)}) %collective-permute-start.6) | collective-permute-done | bytes 589856 | tf_op jit(solution)/shard_map/ppermute | solution.py:484
  129.2 5.4 %shard_map.148 = (bf16[2,128,1536]{2,1,0:T(8,128)(2,1)S(1)}, bf16[2,128,1536]{2,1,0:T(8,128)(2,1)S(1)}) custom-call(s32[5]{0:T(128)S(1)} %stack.23.place_ref, bf16[1152,256]{1,0:T(8,128)(2,1)} %shard_map.146.refs_0_.refs_4_, bf16[1152,256]{1,0:T(8,128)(2,1)S(1)} %collective-permute-done.6.refs_1_.refs_5_, bf16[1152,1536]{1,0:T(8,128)(2,1)} %multiply_convert_fusion.refs_2_, ...), custom_call_target="tpu_custom_call" | custom-call | flops 20000000000 | bytes 20000000 | tf_op jit(solution)/shard_map/pallas_call | solution.py:239
  134.7 2.4 %shard_map.149 = (f32[2,128,1536]{2,1,0:T(8,128)S(1)}, bf16[2,128,1536]{2,1,0:T(8,128)(2,1)S(1)}) custom-call(s32[5]{0:T(128)S(1)} %stack.23.place_ref, bf16[4,128,1536]{2,1,0:T(8,128)(2,1)} %get-tuple-element.82.rest_0_.refs_0_.refs_2_, bf16[4,128,1536]{2,1,0:T(8,128)(2,1)S(1)} %collective-permute-done.10.refs_1_.refs_3_, ...), custom_call_target="tpu_custom_call" | custom-call | flops 20000000000 | bytes 20000000 | tf_op jit(solution)/shard_map/pallas_call | solution.py:277
  139.7 3.8 %shard_map.151 = (bf16[2,128,1536]{2,1,0:T(8,128)(2,1)S(1)}, bf16[2,128,1536]{2,1,0:T(8,128)(2,1)S(1)}) custom-call(s32[5]{0:T(128)S(1)} %stack.23.place_ref, bf16[1152,256]{1,0:T(8,128)(2,1)S(1)} %copy-done.6, bf16[1152,256]{1,0:T(8,128)(2,1)S(1)} %collective-permute-done.8.refs_1_.refs_7_, bf16[1152,1536]{1,0:T(8,128)(2,1)S(1)} %copy-done.7, ...), custom_call_target="tpu_custom_call" | custom-call | flops 1 | bytes 1 | tf_op jit(solution)/shard_map/pallas_call | solution.py:239
  143.5 3.0 %collective-permute-start.13 = (bf16[2,128,1536]{2,1,0:T(8,128)(2,1)S(1)}, bf16[2,128,1536]{2,1,0:T(8,128)(2,1)S(1)}, u32[]{:S(2)}, u32[]{:S(2)}) collective-permute-start(bf16[2,128,1536]{2,1,0:T(8,128)(2,1)S(1)} %get-tuple-element.49.refs_8_), channel_id=1, source_target_pairs={{0,2},{2,0},{4,6},{6,4},{8,10},{10,8},{12,14},{14,12},{16,18},{18,... | collective-permute-start | bytes 2359304 | tf_op jit(solution)/shard_map/ppermute | solution.py:457
  146.5 4.0 %shard_map.152 = (bf16[1152,2048]{1,0:T(8,128)(2,1)S(1)}, f32[8,128]{1,0:T(8,128)S(1)}) custom-call(s32[5]{0:T(128)S(1)} %stack.23.place_ref, bf16[1152,256]{1,0:T(8,128)(2,1)} %shard_map.143.rest_0_.refs_0_, bf16[1152,256]{1,0:T(8,128)(2,1)} %collective-permute-done.2.refs_1_, bf16[1152,256]{1,0:T(8,128)(2,1)} %shard_map.144.rest_0_.refs_2_, ...), custom_call_target="tpu_custom_call" | custom-call | flops 20000000000 | bytes 20000000 | tf_op jit(solution)/shard_map/pallas_call | solution.py:390
  155.0 5.3 %shard_map.156 = (bf16[1152,1536]{1,0:T(8,128)(2,1)}, f32[8,128]{1,0:T(8,128)S(1)}) custom-call(bf16[1152,2048]{1,0:T(8,128)(2,1)S(1)} %get-tuple-element.50.attention_ref, bf16[2048,1536]{1,0:T(8,128)(2,1)S(1)} %bitcast.25, f32[1,1536]{1,0:T(1,128)S(1)} %convert_element_type.19.gate_ref, bf16[2,128,1536]{2,1,0:T(8,128)(2,1)S(1)} %shard_map.155.refs_0_), custom_call_target="tpu_custom_call" | custom-call | flops 1 | bytes 1 | tf_op jit(solution)/shard_map/pallas_call | solution.py:423
  160.3 4.3 %collective-permute-done.15.refs_1_.refs_3_ = bf16[2,128,1536]{2,1,0:T(8,128)(2,1)S(1)} collective-permute-done((bf16[2,128,1536]{2,1,0:T(8,128)(2,1)S(1)}, bf16[2,128,1536]{2,1,0:T(8,128)(2,1)S(1)}, u32[]{:S(2)}, u32[]{:S(2)}) %collective-permute-start.15) | collective-permute-done | bytes 786464 | tf_op jit(solution)/shard_map/ppermute | solution.py:457
  165.3 5.7 %collective-permute-done.14.refs_2_.refs_5_ = bf16[2,128,1536]{2,1,0:T(8,128)(2,1)S(1)} collective-permute-done((bf16[2,128,1536]{2,1,0:T(8,128)(2,1)S(1)}, bf16[2,128,1536]{2,1,0:T(8,128)(2,1)S(1)}, u32[]{:S(2)}, u32[]{:S(2)}) %collective-permute-start.14) | collective-permute-done | bytes 786464 | tf_op jit(solution)/shard_map/ppermute | solution.py:457
  171.9 4.8 %collective-permute-start.17 = (bf16[1,128,1536]{2,1,0:T(8,128)(2,1)S(1)}, bf16[1,128,1536]{2,1,0:T(8,128)(2,1)S(1)}, u32[]{:S(2)}, u32[]{:S(2)}) collective-permute-start(bf16[1,128,1536]{2,1,0:T(8,128)(2,1)S(1)} %get-tuple-element.58.refs_1_), channel_id=1, source_target_pairs={{2,26},{4,28},{26,2},{28,4},{3,27},{5,29},{27,3},{29,5}} | collective-permute-start | bytes 1179656 | tf_op jit(solution)/shard_map/ppermute | solution.py:457
  180.1 5.3 %shard_map.159 = (bf16[1152,1536]{1,0:T(8,128)(2,1)}, f32[8,128]{1,0:T(8,128)S(1)}) custom-call(bf16[1152,2048]{1,0:T(8,128)(2,1)S(1)} %get-tuple-element.50.attention_ref, bf16[2048,1536]{1,0:T(8,128)(2,1)S(1)} %bitcast.25, f32[1,1536]{1,0:T(1,128)S(1)} %convert_element_type.19.gate_ref, ...), custom_call_target="tpu_custom_call", output_to_operand_aliasing={{0}: (3, {})} | custom-call | flops 1 | bytes 1 | tf_op jit(solution)/shard_map/pallas_call | solution.py:423
  186.3 4.2 %collective-permute-done.20.refs_6_ = bf16[1,128,1536]{2,1,0:T(8,128)(2,1)S(1)} collective-permute-done((bf16[1,128,1536]{2,1,0:T(8,128)(2,1)S(1)}, bf16[1,128,1536]{2,1,0:T(8,128)(2,1)S(1)}, u32[]{:S(2)}, u32[]{:S(2)}) %collective-permute-start.20) | collective-permute-done | bytes 393248 | tf_op jit(solution)/shard_map/ppermute | solution.py:457
  (86 shorter events, 30.2 us)
Async XLA Ops:
  7.2 76.7 %all-gather.2.cloned.1.call-start = ((), (), s32[]{:S(2)}) async-start(), calls=%async_computation | async-start | bytes 6684672 | tf_op jit(solution)/shard_map/all_gather | solution.py:472
  10.6 4.7 %copy-start = (bf16[576,2048]{1,0:T(8,128)(2,1)S(1)}, bf16[576,2048]{1,0:T(8,128)(2,1)}, u32[]{:S(2)}) copy-start(bf16[576,2048]{1,0:T(8,128)(2,1)} %q_ref.15) | copy-start | bytes 7077892
  10.6 22.7 %collective-permute-start.1 = (bf16[3,576,256]{2,1,0:T(8,128)(2,1)}, bf16[3,576,256]{2,1,0:T(8,128)(2,1)S(1)}, u32[]{:S(2)}, u32[]{:S(2)}) collective-permute-start(bf16[3,576,256]{2,1,0:T(8,128)(2,1)} %shard_map.140.rest_0_), channel_id=1, source_target_pairs={{0,1},{1,0},{2,3},{3,2},{4,5},{5,4},{6,7},{7,6},{8,9},{9,8},{10,11... | collective-permute-start | bytes 2654216 | tf_op jit(solution)/shard_map/ppermute | solution.py:484
  14.9 37.5 %collective-permute-start.3 = (bf16[3,576,256]{2,1,0:T(8,128)(2,1)}, bf16[3,576,256]{2,1,0:T(8,128)(2,1)S(1)}, u32[]{:S(2)}, u32[]{:S(2)}) collective-permute-start(bf16[3,576,256]{2,1,0:T(8,128)(2,1)} %shard_map.141.rest_0_), channel_id=1, source_target_pairs={{0,1},{1,0},{2,3},{3,2},{4,5},{5,4},{6,7},{7,6},{8,9},{9,8},{10,11... | collective-permute-start | bytes 2654216 | tf_op jit(solution)/shard_map/ppermute | solution.py:484
  19.9 3.0 %copy-start.10 = (s32[1152]{0:T(1024)S(1)}, s32[1152]{0:T(1024)}, u32[]{:S(2)}) copy-start(s32[1152]{0:T(1024)} %constant.80) | copy-start | bytes 13828
  19.9 3.0 %copy-start.11 = (s32[1152]{0:T(1024)S(1)}, s32[1152]{0:T(1024)}, u32[]{:S(2)}) copy-start(s32[1152]{0:T(1024)} %constant.82) | copy-start | bytes 13828
  19.9 3.0 %copy-start.12 = (s32[1152]{0:T(1024)S(1)}, s32[1152]{0:T(1024)}, u32[]{:S(2)}) copy-start(s32[1152]{0:T(1024)} %constant.84) | copy-start | bytes 13828
  21.1 50.2 %collective-permute-start.5 = (bf16[3,576,256]{2,1,0:T(8,128)(2,1)S(1)}, bf16[3,576,256]{2,1,0:T(8,128)(2,1)S(1)}, u32[]{:S(2)}, u32[]{:S(2)}) collective-permute-start(bf16[3,576,256]{2,1,0:T(8,128)(2,1)S(1)} %shard_map.142.rest_0_), channel_id=1, source_target_pairs={{0,1},{1,0},{2,3},{3,2},{4,5},{5,4},{6,7},{7,6},{8,9},{9,8},{10,11... | collective-permute-start | bytes 2654216 | tf_op jit(solution)/shard_map/ppermute | solution.py:484
  23.7 47.6 %copy-start.3 = (f32[16,24,1152]{2,1,0:T(8,128)}, f32[16,24,1152]{2,1,0:T(8,128)S(1)}, u32[]{:S(2)}) copy-start(f32[16,24,1152]{2,1,0:T(8,128)S(1)} %and_select_fusion.bias_ref) | copy-start | bytes 5308420
  40.6 19.0 %copy-start.9 = (bf16[1,1536]{1,0:T(2,128)(2,1)S(1)}, bf16[1,1536]{1,0:T(2,128)(2,1)}, u32[]{:S(2)}) copy-start(bf16[1,1536]{1,0:T(2,128)(2,1)} %param.20) | copy-start | bytes 9220
  60.8 23.3 %collective-permute-start.4 = (bf16[1152,256]{1,0:T(8,128)(2,1)}, bf16[1152,256]{1,0:T(8,128)(2,1)}, u32[]{:S(2)}, u32[]{:S(2)}) collective-permute-start(bf16[1152,256]{1,0:T(8,128)(2,1)} %shard_map.144.rest_0_.refs_2_), channel_id=1, source_target_pairs={{0,1},{1,0},{2,3},{3,2},{4,5},{5,4},{6,7},{7,6},{8,9},{9,8},{10,11... | collective-permute-start | bytes 1769480 | tf_op jit(solution)/shard_map/ppermute | solution.py:484
  62.4 34.3 %collective-permute-start.2 = (bf16[1152,256]{1,0:T(8,128)(2,1)}, bf16[1152,256]{1,0:T(8,128)(2,1)}, u32[]{:S(2)}, u32[]{:S(2)}) collective-permute-start(bf16[1152,256]{1,0:T(8,128)(2,1)} %shard_map.143.rest_0_.refs_0_), channel_id=1, source_target_pairs={{0,1},{1,0},{2,3},{3,2},{4,5},{5,4},{6,7},{7,6},{8,9},{9,8},{10,11... | collective-permute-start | bytes 1769480 | tf_op jit(solution)/shard_map/ppermute | solution.py:484
  62.9 52.8 %collective-permute-start.7 = (bf16[3,576,256]{2,1,0:T(8,128)(2,1)S(1)}, bf16[3,576,256]{2,1,0:T(8,128)(2,1)}, u32[]{:S(2)}, u32[]{:S(2)}) collective-permute-start(bf16[3,576,256]{2,1,0:T(8,128)(2,1)S(1)} %shard_map.145.rest_1_), channel_id=1, source_target_pairs={{0,1},{1,0},{2,3},{3,2},{4,5},{5,4},{6,7},{7,6},{8,9},{9,8},{10,11... | collective-permute-start | bytes 2654216 | tf_op jit(solution)/shard_map/ppermute | solution.py:484
  71.3 8.8 %copy-start.8 = (bf16[1152,1536]{1,0:T(8,128)(2,1)S(1)}, bf16[1152,1536]{1,0:T(8,128)(2,1)}, u32[]{:S(2)}) copy-start(bf16[1152,1536]{1,0:T(8,128)(2,1)} %param.21) | copy-start | bytes 10616836
  78.6 49.6 %collective-permute-start.6 = (bf16[1152,256]{1,0:T(8,128)(2,1)}, bf16[1152,256]{1,0:T(8,128)(2,1)S(1)}, u32[]{:S(2)}, u32[]{:S(2)}) collective-permute-start(bf16[1152,256]{1,0:T(8,128)(2,1)} %shard_map.146.refs_0_.refs_4_), channel_id=1, source_target_pairs={{0,1},{1,0},{2,3},{3,2},{4,5},{5,4},{6,7},{7,6},{8,9},{9,8},{10,11... | collective-permute-start | bytes 1769480 | tf_op jit(solution)/shard_map/ppermute | solution.py:484
  104.7 3.5 %collective-permute-start = (bf16[4,128,1536]{2,1,0:T(8,128)(2,1)S(1)}, bf16[4,128,1536]{2,1,0:T(8,128)(2,1)S(1)}, u32[]{:S(2)}, u32[]{:S(2)}) collective-permute-start(bf16[4,128,1536]{2,1,0:T(8,128)(2,1)S(1)} %get-tuple-element.22), channel_id=1, source_target_pairs={{0,2},{2,0},{4,6},{6,4},{8,10},{10,8},{12,14},{14,12},{16,18},{18,... | collective-permute-start | bytes 4718600 | tf_op jit(solution)/shard_map/cond/branch_1_fun/ppermute | solution.py:457
  110.0 24.7 %collective-permute-start.10 = (bf16[4,128,1536]{2,1,0:T(8,128)(2,1)}, bf16[4,128,1536]{2,1,0:T(8,128)(2,1)S(1)}, u32[]{:S(2)}, u32[]{:S(2)}) collective-permute-start(bf16[4,128,1536]{2,1,0:T(8,128)(2,1)} %get-tuple-element.82.rest_0_.refs_0_.refs_2_), channel_id=1, source_target_pairs={{2,6},{4,0},{10,14},{12,8},{18,22},{20,16},{26,30},{28,24},{3,7},{... | collective-permute-start | bytes 4718600 | tf_op jit(solution)/shard_map/ppermute | solution.py:457
  123.7 16.0 %collective-permute-start.8 = (bf16[1152,256]{1,0:T(8,128)(2,1)}, bf16[1152,256]{1,0:T(8,128)(2,1)S(1)}, u32[]{:S(2)}, u32[]{:S(2)}) collective-permute-start(bf16[1152,256]{1,0:T(8,128)(2,1)} %shard_map.147.refs_3_.refs_0_.refs_6_), channel_id=1, source_target_pairs={{0,1},{1,0},{2,3},{3,2},{4,5},{5,4},{6,7},{7,6},{8,9},{9,8},{10,11... | collective-permute-start | bytes 1769480 | tf_op jit(solution)/shard_map/ppermute | solution.py:484
  134.6 3.4 %collective-permute-start.9 = (bf16[2,128,1536]{2,1,0:T(8,128)(2,1)S(1)}, bf16[2,128,1536]{2,1,0:T(8,128)(2,1)S(1)}, u32[]{:S(2)}, u32[]{:S(2)}) collective-permute-start(bf16[2,128,1536]{2,1,0:T(8,128)(2,1)S(1)} %get-tuple-element.47.refs_4_), channel_id=1, source_target_pairs={{0,2},{2,0},{4,6},{6,4},{8,10},{10,8},{12,14},{14,12},{16,18},{18,... | collective-permute-start | bytes 2359304 | tf_op jit(solution)/shard_map/ppermute | solution.py:457
  134.7 5.0 %copy-start.7 = (bf16[1152,1536]{1,0:T(8,128)(2,1)S(1)}, bf16[1152,1536]{1,0:T(8,128)(2,1)}, u32[]{:S(2)}) copy-start(bf16[1152,1536]{1,0:T(8,128)(2,1)} %multiply_convert_fusion.refs_2_) | copy-start | bytes 10616836
  137.1 14.9 %collective-permute-start.12 = (bf16[2,128,1536]{2,1,0:T(8,128)(2,1)S(1)}, bf16[2,128,1536]{2,1,0:T(8,128)(2,1)S(1)}, u32[]{:S(2)}, u32[]{:S(2)}) collective-permute-start(bf16[2,128,1536]{2,1,0:T(8,128)(2,1)S(1)} %get-tuple-element.48.refs_2_), channel_id=1, source_target_pairs={{0,8},{6,14},{8,0},{14,6},{16,24},{22,30},{24,16},{30,22},{1,9},{7... | collective-permute-start | bytes 2359304 | tf_op jit(solution)/shard_map/ppermute | solution.py:457
  138.2 14.6 %collective-permute-start.11 = (bf16[2,128,1536]{2,1,0:T(8,128)(2,1)S(1)}, bf16[2,128,1536]{2,1,0:T(8,128)(2,1)S(1)}, u32[]{:S(2)}, u32[]{:S(2)}) collective-permute-start(bf16[2,128,1536]{2,1,0:T(8,128)(2,1)S(1)} %shard_map.150.refs_3_.refs_0_), channel_id=1, source_target_pairs={{0,4},{6,2},{8,12},{14,10},{16,20},{22,18},{24,28},{30,26},{1,5},{... | collective-permute-start | bytes 2359304 | tf_op jit(solution)/shard_map/ppermute | solution.py:457
  139.7 15.3 %slice-start = ((s8[6291456]{0:T(1024)(128)(4,1)}), s8[4194304]{0:T(1024)(128)(4,1)S(1)}, s32[]{:S(2)}) async-start(s8[6291456]{0:T(1024)(128)(4,1)} %bitcast.24), calls=%async_computation.1 | async-start | bytes 8388608
  143.5 11.5 %slice-start.1 = ((s8[6291456]{0:T(1024)(128)(4,1)}), s8[2097152]{0:T(1024)(128)(4,1)S(1)}, s32[]{:S(2)}) async-start(s8[6291456]{0:T(1024)(128)(4,1)} %bitcast.24), calls=%async_computation.2 | async-start | bytes 4194304
  143.5 6.9 %collective-permute-start.13 = (bf16[2,128,1536]{2,1,0:T(8,128)(2,1)S(1)}, bf16[2,128,1536]{2,1,0:T(8,128)(2,1)S(1)}, u32[]{:S(2)}, u32[]{:S(2)}) collective-permute-start(bf16[2,128,1536]{2,1,0:T(8,128)(2,1)S(1)} %get-tuple-element.49.refs_8_), channel_id=1, source_target_pairs={{0,2},{2,0},{4,6},{6,4},{8,10},{10,8},{12,14},{14,12},{16,18},{18,... | collective-permute-start | bytes 2359304 | tf_op jit(solution)/shard_map/ppermute | solution.py:457
  150.7 13.9 %collective-permute-start.15 = (bf16[2,128,1536]{2,1,0:T(8,128)(2,1)S(1)}, bf16[2,128,1536]{2,1,0:T(8,128)(2,1)S(1)}, u32[]{:S(2)}, u32[]{:S(2)}) collective-permute-start(bf16[2,128,1536]{2,1,0:T(8,128)(2,1)S(1)} %shard_map.153.refs_4_.refs_0_.refs_2_), channel_id=1, source_target_pairs={{0,4},{6,2},{8,12},{14,10},{16,20},{22,18},{24,28},{30,26},{1,5},{... | collective-permute-start | bytes 2359304 | tf_op jit(solution)/shard_map/ppermute | solution.py:457
  153.0 18.1 %collective-permute-start.14 = (bf16[2,128,1536]{2,1,0:T(8,128)(2,1)S(1)}, bf16[2,128,1536]{2,1,0:T(8,128)(2,1)S(1)}, u32[]{:S(2)}, u32[]{:S(2)}) collective-permute-start(bf16[2,128,1536]{2,1,0:T(8,128)(2,1)S(1)} %shard_map.155.refs_0_), channel_id=1, source_target_pairs={{10,2},{12,4},{18,26},{20,28},{11,3},{13,5},{19,27},{21,29}} | collective-permute-start | bytes 2359304 | tf_op jit(solution)/shard_map/ppermute | solution.py:457
  154.3 31.1 %collective-permute-start.16 = (bf16[1,128,1536]{2,1,0:T(8,128)(2,1)S(1)}, bf16[1,128,1536]{2,1,0:T(8,128)(2,1)S(1)}, u32[]{:S(2)}, u32[]{:S(2)}) collective-permute-start(bf16[1,128,1536]{2,1,0:T(8,128)(2,1)S(1)} %get-tuple-element.54.refs_2_), channel_id=1, source_target_pairs={{0,16},{6,22},{8,24},{14,30},{16,0},{22,6},{24,8},{30,14},{1,17},{... | collective-permute-start | bytes 1179656 | tf_op jit(solution)/shard_map/ppermute | solution.py:457
  171.9 13.5 %collective-permute-start.17 = (bf16[1,128,1536]{2,1,0:T(8,128)(2,1)S(1)}, bf16[1,128,1536]{2,1,0:T(8,128)(2,1)S(1)}, u32[]{:S(2)}, u32[]{:S(2)}) collective-permute-start(bf16[1,128,1536]{2,1,0:T(8,128)(2,1)S(1)} %get-tuple-element.58.refs_1_), channel_id=1, source_target_pairs={{2,26},{4,28},{26,2},{28,4},{3,27},{5,29},{27,3},{29,5}} | collective-permute-start | bytes 1179656 | tf_op jit(solution)/shard_map/ppermute | solution.py:457
  176.7 9.5 %collective-permute-start.18 = (bf16[1,128,1536]{2,1,0:T(8,128)(2,1)S(1)}, bf16[1,128,1536]{2,1,0:T(8,128)(2,1)S(1)}, u32[]{:S(2)}, u32[]{:S(2)}) collective-permute-start(bf16[1,128,1536]{2,1,0:T(8,128)(2,1)S(1)} %get-tuple-element.64), channel_id=1, source_target_pairs={{2,18},{4,20},{26,10},{28,12},{3,19},{5,21},{27,11},{29,13}} | collective-permute-start | bytes 1179656 | tf_op jit(solution)/shard_map/ppermute | solution.py:457
  178.1 8.2 %collective-permute-start.19 = (bf16[1,128,1536]{2,1,0:T(8,128)(2,1)S(1)}, bf16[1,128,1536]{2,1,0:T(8,128)(2,1)S(1)}, u32[]{:S(2)}, u32[]{:S(2)}) collective-permute-start(bf16[1,128,1536]{2,1,0:T(8,128)(2,1)S(1)} %get-tuple-element.64), channel_id=1, source_target_pairs={{10,18},{12,20},{18,10},{20,12},{11,19},{13,21},{19,11},{21,13}} | collective-permute-start | bytes 1179656 | tf_op jit(solution)/shard_map/ppermute | solution.py:457
  178.8 11.7 %collective-permute-start.20 = (bf16[1,128,1536]{2,1,0:T(8,128)(2,1)S(1)}, bf16[1,128,1536]{2,1,0:T(8,128)(2,1)S(1)}, u32[]{:S(2)}, u32[]{:S(2)}) collective-permute-start(bf16[1,128,1536]{2,1,0:T(8,128)(2,1)S(1)} %get-tuple-element.57.refs_6_), channel_id=1, source_target_pairs={{2,10},{4,12},{26,18},{28,20},{3,11},{5,13},{27,19},{29,21}} | collective-permute-start | bytes 1179656 | tf_op jit(solution)/shard_map/ppermute | solution.py:457
  (9 other events, 19.5 us)
Sparse Core Ops, SparseCore 0:
  10.3 62.1 all-gather.1
where the time goes:
time: 200 us; the launch traced here: 199 us
  Pallas kernels  77.9 us (39%)
  waiting for transfers between devices  67.1 us (34%)
  starting transfers between devices  29 us (14%)
  between operations  15 us (8%)
  local copies, waits for them, and re-layouts  6.27 us (3%)
  other arithmetic  3.61 us (2%)
    ppermute x8, waiting for transfers between devices, exchange(): return lax.ppermute(mine, 'seq', swap)  47.8 us
    pallas_call x4, Pallas kernels, attend_pair(): pl.pallas_call(pair_kernel, grid_spec=pltpu.PrefetchScalarGridSpec(num_sc...  29.9 us
    ppermute x13, starting transfers between devices, dp_send(): lax.ppermute(value, 'dp', [(i, i ^ flip) for i in range(HEADS) if sender(...  18.7 us
    ppermute x13, waiting for transfers between devices, dp_send(): lax.ppermute(value, 'dp', [(i, i ^ flip) for i in range(HEADS) if sender(...  18.6 us
    pallas_call x3, Pallas kernels, batch_gradient(): pl.pallas_call(functools.partial(gradient_kernel, by_call=by_call), grid_...  17.2 us
    pallas_call x2, Pallas kernels, project(): pl.pallas_call(kernel, grid=(steps,), in_specs=[pl.BlockSpec((rows, depth...  10.5 us
    ppermute x8, starting transfers between devices, exchange(): return lax.ppermute(mine, 'seq', swap)  10.3 us
    pallas_call x4, Pallas kernels, pack_partner(): pl.pallas_call(pack_kernel, grid_spec=pltpu.PrefetchScalarGridSpec(num_sc...  7.59 us
  transfers between devices with their start and end apart: 22, of which 14 were waited for; matrix products, arithmetic and copies ran while one was open for 2% of the time, Pallas kernels for 38%

commit v1 on v0

--- a/solution.py
+++ b/solution.py
@@ -547,7 +547,8 @@
     reached_c = dp_send(far_c, 8, outer), dp_send(far_c, 12, inner), dp_send(near_c, 4, outer)
     kept_b, sent_b = level_step(place, HIGH, [total_b, across_b, low_b], (near_c,))
     high_b = dp_send(sent_b, 12, outer)
-    block_out, done = project(columns, weight, gate, range(3, PROJECT_STEPS), (out,), (sent_b,))
+    last = range(3, PROJECT_STEPS)
+    block_out, done = project(columns, weight, gate, last, (out,), (sent_b,), LONG_COST)
     final_a = total_step([kept_a, high_a], (done,), jnp.float32)
     weight_grad = choose_owned(place, (final_a,), (kept_b, high_b), (kept_c, *reached_c))
     return (block_out, weight_grad)

time: 200 us -> 195 us (0.975)
  waiting for transfers between devices: 67.1 us -> 59.6 us
  starting transfers between devices: 29 us -> 31.9 us
    ppermute x13, waiting for transfers between devices: 18.6 us -> 11.1 us  [dp_send(): lax.ppermute(value, 'dp', [(i, i ^ flip) for i in range(HEADS) if sender(...]
    ppermute x13, starting transfers between devices: 18.7 us -> 21.6 us  [dp_send(): lax.ppermute(value, 'dp', [(i, i ^ flip) for i in range(HEADS) if sender(...]
  transfers between devices with their start and end apart: 22 -> 22, of which waited for: 14 -> 12; matrix products, arithmetic and copies ran while one was open for 2% -> 2% of each run, Pallas kernels for 38% -> 39%
where the time goes in v1:
time: 195 us; the launch traced here: 194 us
  Pallas kernels  77.9 us (40%)
  waiting for transfers between devices  59.6 us (31%)
  starting transfers between devices  31.9 us (16%)
  between operations  15 us (8%)
  local copies, waits for them, and re-layouts  6.27 us (3%)
  other arithmetic  3.61 us (2%)
    ppermute x8, waiting for transfers between devices, exchange(): return lax.ppermute(mine, 'seq', swap)  47.8 us
    pallas_call x4, Pallas kernels, attend_pair(): pl.pallas_call(pair_kernel, grid_spec=pltpu.PrefetchScalarGridSpec(num_sc...  29.9 us
    ppermute x13, starting transfers between devices, dp_send(): lax.ppermute(value, 'dp', [(i, i ^ flip) for i in range(HEADS) if sender(...  21.6 us
    pallas_call x3, Pallas kernels, batch_gradient(): pl.pallas_call(functools.partial(gradient_kernel, by_call=by_call), grid_...  17.2 us
    ppermute x13, waiting for transfers between devices, dp_send(): lax.ppermute(value, 'dp', [(i, i ^ flip) for i in range(HEADS) if sender(...  11.1 us
    pallas_call x2, Pallas kernels, project(): pl.pallas_call(kernel, grid=(steps,), in_specs=[pl.BlockSpec((rows, depth...  10.5 us
    ppermute x8, starting transfers between devices, exchange(): return lax.ppermute(mine, 'seq', swap)  10.3 us
    pallas_call x4, Pallas kernels, pack_partner(): pl.pallas_call(pack_kernel, grid_spec=pltpu.PrefetchScalarGridSpec(num_sc...  7.59 us
  transfers between devices with their start and end apart: 22, of which 12 were waited for; matrix products, arithmetic and copies ran while one was open for 2% of the time, Pallas kernels for 39%

profile of v1, /device:TPU:2, one launch (start us, length us, event | category | flops | bytes accessed | tf_op | source)
XLA Modules:
  0.0 194.3 jit_solution(3953080673714052695)
XLA Ops:
  8.0 2.6 %shard_map.140.rest_0_ = bf16[3,576,256]{2,1,0:T(8,128)(2,1)} custom-call(s32[5]{0:T(128)S(1)} %stack.23.place_ref, bf16[576,2048]{1,0:T(8,128)(2,1)} %q_ref.15, bf16[576,2048]{1,0:T(8,128)(2,1)} %k_ref.15, bf16[576,2048]{1,0:T(8,128)(2,1)} %v_ref.15), custom_call_target="tpu_custom_call" | custom-call | flops 1 | bytes 1 | tf_op jit(solution)/shard_map/pallas_call | solution.py:186
  12.1 2.7 %shard_map.141.rest_0_ = bf16[3,576,256]{2,1,0:T(8,128)(2,1)} custom-call(s32[5]{0:T(128)S(1)} %stack.23.place_ref, bf16[576,2048]{1,0:T(8,128)(2,1)} %q_ref.15, bf16[576,2048]{1,0:T(8,128)(2,1)} %k_ref.15, bf16[576,2048]{1,0:T(8,128)(2,1)} %v_ref.15, bf16[3,576,256]{2,1,0:T(8,128)(2,1)} %shard_map.140.rest_0_), custom_call_target="tpu_custom_call" | custom-call | flops 1 | bytes 1 | tf_op jit(solution)/shard_map/pallas_call | solution.py:186
  15.4 1.7 copy-done.1
  17.0 1.7 copy-done.2
  23.7 9.6 %collective-permute-done.1.other_ref = bf16[3,576,256]{2,1,0:T(8,128)(2,1)S(1)} collective-permute-done((bf16[3,576,256]{2,1,0:T(8,128)(2,1)}, bf16[3,576,256]{2,1,0:T(8,128)(2,1)S(1)}, u32[]{:S(2)}, u32[]{:S(2)}) %collective-permute-start.1) | collective-permute-done | bytes 884768 | tf_op jit(solution)/shard_map/ppermute | solution.py:484
  33.4 7.3 %shard_map.143.rest_0_.refs_0_ = bf16[1152,256]{1,0:T(8,128)(2,1)} custom-call(s32[5]{0:T(128)S(1)} %stack.23.place_ref, bf16[576,2048]{1,0:T(8,128)(2,1)S(1)} %copy-done, bf16[576,2048]{1,0:T(8,128)(2,1)S(1)} %copy-done.1, bf16[576,2048]{1,0:T(8,128)(2,1)S(1)} %copy-done.2, bf16[3,576,256]{2,1,0:T(8,128)(2,1)S(1)} %collective-permute-done.1.other_ref, ...), custom_call_target="tpu_custom_call" | custom-call | flops 1 | bytes 1 | tf_op jit(solution)/shard_map/pallas_call | solution.py:117
  40.6 11.7 %collective-permute-done.3.other_ref = bf16[3,576,256]{2,1,0:T(8,128)(2,1)S(1)} collective-permute-done((bf16[3,576,256]{2,1,0:T(8,128)(2,1)}, bf16[3,576,256]{2,1,0:T(8,128)(2,1)S(1)}, u32[]{:S(2)}, u32[]{:S(2)}) %collective-permute-start.3) | collective-permute-done | bytes 884768 | tf_op jit(solution)/shard_map/ppermute | solution.py:484
  52.3 7.3 %shard_map.144.rest_0_.refs_2_ = bf16[1152,256]{1,0:T(8,128)(2,1)} custom-call(s32[5]{0:T(128)S(1)} %stack.23.place_ref, bf16[576,2048]{1,0:T(8,128)(2,1)S(1)} %copy-done, bf16[576,2048]{1,0:T(8,128)(2,1)S(1)} %copy-done.1, bf16[576,2048]{1,0:T(8,128)(2,1)S(1)} %copy-done.2, bf16[3,576,256]{2,1,0:T(8,128)(2,1)S(1)} %collective-permute-done.3.other_ref, ...), custom_call_target="tpu_custom_call" | custom-call | flops 1 | bytes 1 | tf_op jit(solution)/shard_map/pallas_call | solution.py:117
  64.4 6.9 %collective-permute-done.5.other_ref = bf16[3,576,256]{2,1,0:T(8,128)(2,1)S(1)} collective-permute-done((bf16[3,576,256]{2,1,0:T(8,128)(2,1)S(1)}, bf16[3,576,256]{2,1,0:T(8,128)(2,1)S(1)}, u32[]{:S(2)}, u32[]{:S(2)}) %collective-permute-start.5) | collective-permute-done | bytes 884768 | tf_op jit(solution)/shard_map/ppermute | solution.py:484
  71.3 7.3 %shard_map.146.refs_0_.refs_4_ = bf16[1152,256]{1,0:T(8,128)(2,1)} custom-call(s32[5]{0:T(128)S(1)} %stack.23.place_ref, bf16[576,2048]{1,0:T(8,128)(2,1)S(1)} %copy-done, bf16[576,2048]{1,0:T(8,128)(2,1)S(1)} %copy-done.1, bf16[576,2048]{1,0:T(8,128)(2,1)S(1)} %copy-done.2, bf16[3,576,256]{2,1,0:T(8,128)(2,1)S(1)} %collective-permute-done.5.other_ref, ...), custom_call_target="tpu_custom_call" | custom-call | flops 1 | bytes 1 | tf_op jit(solution)/shard_map/pallas_call | solution.py:117
  80.1 2.6 %multiply_convert_fusion.refs_2_ = bf16[1152,1536]{1,0:T(8,128)(2,1)} fusion(bf16[1152,1536]{1,0:T(8,128)(2,1)S(1)} %copy-done.8, f32[1536]{0:T(1024)S(1)} %convert_reduce_fusion), kind=kLoop, calls=%fused_computation | loop fusion | flops 5308416 | bytes 7084032 | tf_op jit(solution)/shard_map/convert_element_type | solution.py:474
  84.0 12.6 %collective-permute-done.2.refs_1_ = bf16[1152,256]{1,0:T(8,128)(2,1)} collective-permute-done((bf16[1152,256]{1,0:T(8,128)(2,1)}, bf16[1152,256]{1,0:T(8,128)(2,1)}, u32[]{:S(2)}, u32[]{:S(2)}) %collective-permute-start.2) | collective-permute-done | bytes 589856 | tf_op jit(solution)/shard_map/ppermute | solution.py:484
  96.7 13.3 %conditional.1 = (bf16[4,128,1536]{2,1,0:T(8,128)(2,1)}) conditional(s32[]{:T(128)} %bitcast.14, () %tuple.15, (s32[5]{0:T(128)S(1)}, bf16[1152,256]{1,0:T(8,128)(2,1)}, bf16[1152,256]{1,0:T(8,128)(2,1)}, bf16[1152,256]{1,0:T(8,128)(2,1)}, bf16[1152,256]{1,0:T(8,128)(2,1)}, /*index=5*/bf16[1152,1536]{1,0:T(8,128)(2,1)}) %tuple.17), branch_computations={%region_0.1_spmd, %region_1.2_spmd} | conditional | flops 2 | bytes 6291506 | solution.py:492
  96.7 8.0 %branch_1_fun.2 = (bf16[4,128,1536]{2,1,0:T(8,128)(2,1)S(1)}, bf16[4,128,1536]{2,1,0:T(8,128)(2,1)S(1)}) custom-call(s32[5]{0:T(128)S(1)} %get-tuple-element.5.place_ref, bf16[1152,256]{1,0:T(8,128)(2,1)} %get-tuple-element.16.refs_0_, bf16[1152,256]{1,0:T(8,128)(2,1)} %get-tuple-element.17.refs_1_, bf16[1152,256]{1,0:T(8,128)(2,1)} %get-tuple-element.18.refs_2_, ...), custom_call_target="tpu_custom_call" | custom-call | flops 1 | bytes 1 | tf_op jit(solution)/shard_map/cond/branch_1_fun/pallas_call | solution.py:239
  104.8 3.4 %collective-permute-done.refs_1_ = bf16[4,128,1536]{2,1,0:T(8,128)(2,1)S(1)} collective-permute-done((bf16[4,128,1536]{2,1,0:T(8,128)(2,1)S(1)}, bf16[4,128,1536]{2,1,0:T(8,128)(2,1)S(1)}, u32[]{:S(2)}, u32[]{:S(2)}) %collective-permute-start) | collective-permute-done | bytes 1572896 | tf_op jit(solution)/shard_map/cond/branch_1_fun/ppermute | solution.py:457
  108.1 1.9 branch_1_fun.3
  110.0 2.0 %collective-permute-start.10 = (bf16[4,128,1536]{2,1,0:T(8,128)(2,1)}, bf16[4,128,1536]{2,1,0:T(8,128)(2,1)S(1)}, u32[]{:S(2)}, u32[]{:S(2)}) collective-permute-start(bf16[4,128,1536]{2,1,0:T(8,128)(2,1)} %get-tuple-element.82.rest_0_.refs_0_.refs_2_), channel_id=1, source_target_pairs={{2,6},{4,0},{10,14},{12,8},{18,22},{20,16},{26,30},{28,24},{3,7},{... | collective-permute-start | bytes 4718600 | tf_op jit(solution)/shard_map/ppermute | solution.py:457
  112.0 3.6 %collective-permute-done.7.other_ref = bf16[3,576,256]{2,1,0:T(8,128)(2,1)} collective-permute-done((bf16[3,576,256]{2,1,0:T(8,128)(2,1)S(1)}, bf16[3,576,256]{2,1,0:T(8,128)(2,1)}, u32[]{:S(2)}, u32[]{:S(2)}) %collective-permute-start.7) | collective-permute-done | bytes 884768 | tf_op jit(solution)/shard_map/ppermute | solution.py:484
  115.6 8.1 %shard_map.147.refs_3_.refs_0_.refs_6_ = bf16[1152,256]{1,0:T(8,128)(2,1)} custom-call(s32[5]{0:T(128)S(1)} %stack.23.place_ref, bf16[576,2048]{1,0:T(8,128)(2,1)} %q_ref.15, bf16[576,2048]{1,0:T(8,128)(2,1)} %k_ref.15, bf16[576,2048]{1,0:T(8,128)(2,1)} %v_ref.15, bf16[3,576,256]{2,1,0:T(8,128)(2,1)} %collective-permute-done.7.other_ref, ...), custom_call_target="tpu_custom_call" | custom-call | flops 1 | bytes 1 | tf_op jit(solution)/shard_map/pallas_call | solution.py:117
  125.2 2.9 %collective-permute-done.6.refs_1_.refs_5_ = bf16[1152,256]{1,0:T(8,128)(2,1)S(1)} collective-permute-done((bf16[1152,256]{1,0:T(8,128)(2,1)}, bf16[1152,256]{1,0:T(8,128)(2,1)S(1)}, u32[]{:S(2)}, u32[]{:S(2)}) %collective-permute-start.6) | collective-permute-done | bytes 589856 | tf_op jit(solution)/shard_map/ppermute | solution.py:484
  129.2 5.4 %shard_map.148 = (bf16[2,128,1536]{2,1,0:T(8,128)(2,1)S(1)}, bf16[2,128,1536]{2,1,0:T(8,128)(2,1)S(1)}) custom-call(s32[5]{0:T(128)S(1)} %stack.23.place_ref, bf16[1152,256]{1,0:T(8,128)(2,1)} %shard_map.146.refs_0_.refs_4_, bf16[1152,256]{1,0:T(8,128)(2,1)S(1)} %collective-permute-done.6.refs_1_.refs_5_, bf16[1152,1536]{1,0:T(8,128)(2,1)} %multiply_convert_fusion.refs_2_, ...), custom_call_target="tpu_custom_call" | custom-call | flops 20000000000 | bytes 20000000 | tf_op jit(solution)/shard_map/pallas_call | solution.py:239
  134.7 2.4 %shard_map.149 = (f32[2,128,1536]{2,1,0:T(8,128)S(1)}, bf16[2,128,1536]{2,1,0:T(8,128)(2,1)S(1)}) custom-call(s32[5]{0:T(128)S(1)} %stack.23.place_ref, bf16[4,128,1536]{2,1,0:T(8,128)(2,1)} %get-tuple-element.82.rest_0_.refs_0_.refs_2_, bf16[4,128,1536]{2,1,0:T(8,128)(2,1)S(1)} %collective-permute-done.10.refs_1_.refs_3_, ...), custom_call_target="tpu_custom_call" | custom-call | flops 20000000000 | bytes 20000000 | tf_op jit(solution)/shard_map/pallas_call | solution.py:277
  139.7 3.8 %shard_map.151 = (bf16[2,128,1536]{2,1,0:T(8,128)(2,1)S(1)}, bf16[2,128,1536]{2,1,0:T(8,128)(2,1)S(1)}) custom-call(s32[5]{0:T(128)S(1)} %stack.23.place_ref, bf16[1152,256]{1,0:T(8,128)(2,1)S(1)} %copy-done.6, bf16[1152,256]{1,0:T(8,128)(2,1)S(1)} %collective-permute-done.8.refs_1_.refs_7_, bf16[1152,1536]{1,0:T(8,128)(2,1)S(1)} %copy-done.7, ...), custom_call_target="tpu_custom_call" | custom-call | flops 1 | bytes 1 | tf_op jit(solution)/shard_map/pallas_call | solution.py:239
  143.5 3.0 %collective-permute-start.13 = (bf16[2,128,1536]{2,1,0:T(8,128)(2,1)S(1)}, bf16[2,128,1536]{2,1,0:T(8,128)(2,1)S(1)}, u32[]{:S(2)}, u32[]{:S(2)}) collective-permute-start(bf16[2,128,1536]{2,1,0:T(8,128)(2,1)S(1)} %get-tuple-element.49.refs_8_), channel_id=1, source_target_pairs={{0,2},{2,0},{4,6},{6,4},{8,10},{10,8},{12,14},{14,12},{16,18},{18,... | collective-permute-start | bytes 2359304 | tf_op jit(solution)/shard_map/ppermute | solution.py:457
  146.5 4.0 %shard_map.152 = (bf16[1152,2048]{1,0:T(8,128)(2,1)S(1)}, f32[8,128]{1,0:T(8,128)S(1)}) custom-call(s32[5]{0:T(128)S(1)} %stack.23.place_ref, bf16[1152,256]{1,0:T(8,128)(2,1)} %shard_map.143.rest_0_.refs_0_, bf16[1152,256]{1,0:T(8,128)(2,1)} %collective-permute-done.2.refs_1_, bf16[1152,256]{1,0:T(8,128)(2,1)} %shard_map.144.rest_0_.refs_2_, ...), custom_call_target="tpu_custom_call" | custom-call | flops 20000000000 | bytes 20000000 | tf_op jit(solution)/shard_map/pallas_call | solution.py:390
  155.0 5.3 %shard_map.156 = (bf16[1152,1536]{1,0:T(8,128)(2,1)}, f32[8,128]{1,0:T(8,128)S(1)}) custom-call(bf16[1152,2048]{1,0:T(8,128)(2,1)S(1)} %get-tuple-element.50.attention_ref, bf16[2048,1536]{1,0:T(8,128)(2,1)S(1)} %bitcast.25, f32[1,1536]{1,0:T(1,128)S(1)} %convert_element_type.19.gate_ref, bf16[2,128,1536]{2,1,0:T(8,128)(2,1)S(1)} %shard_map.155.refs_0_), custom_call_target="tpu_custom_call" | custom-call | flops 1 | bytes 1 | tf_op jit(solution)/shard_map/pallas_call | solution.py:423
  160.3 4.3 %collective-permute-done.15.refs_1_.refs_3_ = bf16[2,128,1536]{2,1,0:T(8,128)(2,1)S(1)} collective-permute-done((bf16[2,128,1536]{2,1,0:T(8,128)(2,1)S(1)}, bf16[2,128,1536]{2,1,0:T(8,128)(2,1)S(1)}, u32[]{:S(2)}, u32[]{:S(2)}) %collective-permute-start.15) | collective-permute-done | bytes 786464 | tf_op jit(solution)/shard_map/ppermute | solution.py:457
  165.3 4.5 %collective-permute-start.18 = (bf16[1,128,1536]{2,1,0:T(8,128)(2,1)S(1)}, bf16[1,128,1536]{2,1,0:T(8,128)(2,1)S(1)}, u32[]{:S(2)}, u32[]{:S(2)}) collective-permute-start(bf16[1,128,1536]{2,1,0:T(8,128)(2,1)S(1)} %get-tuple-element.64), channel_id=1, source_target_pairs={{2,18},{4,20},{26,10},{28,12},{3,19},{5,21},{27,11},{29,13}} | collective-permute-start | bytes 1179656 | tf_op jit(solution)/shard_map/ppermute | solution.py:457
  170.6 3.1 %collective-permute-start.20 = (bf16[1,128,1536]{2,1,0:T(8,128)(2,1)S(1)}, bf16[1,128,1536]{2,1,0:T(8,128)(2,1)S(1)}, u32[]{:S(2)}, u32[]{:S(2)}) collective-permute-start(bf16[1,128,1536]{2,1,0:T(8,128)(2,1)S(1)} %get-tuple-element.57.refs_6_), channel_id=1, source_target_pairs={{2,10},{4,12},{26,18},{28,20},{3,11},{5,13},{27,19},{29,21}} | collective-permute-start | bytes 1179656 | tf_op jit(solution)/shard_map/ppermute | solution.py:457
  174.5 2.8 %collective-permute-start.17 = (bf16[1,128,1536]{2,1,0:T(8,128)(2,1)S(1)}, bf16[1,128,1536]{2,1,0:T(8,128)(2,1)S(1)}, u32[]{:S(2)}, u32[]{:S(2)}) collective-permute-start(bf16[1,128,1536]{2,1,0:T(8,128)(2,1)S(1)} %get-tuple-element.58.refs_1_), channel_id=1, source_target_pairs={{2,26},{4,28},{26,2},{28,4},{3,27},{5,29},{27,3},{29,5}} | collective-permute-start | bytes 1179656 | tf_op jit(solution)/shard_map/ppermute | solution.py:457
  177.3 5.3 %shard_map.159 = (bf16[1152,1536]{1,0:T(8,128)(2,1)}, f32[8,128]{1,0:T(8,128)S(1)}) custom-call(bf16[1152,2048]{1,0:T(8,128)(2,1)S(1)} %get-tuple-element.50.attention_ref, bf16[2048,1536]{1,0:T(8,128)(2,1)S(1)} %bitcast.25, f32[1,1536]{1,0:T(1,128)S(1)} %convert_element_type.19.gate_ref, ...), custom_call_target="tpu_custom_call", output_to_operand_aliasing={{0}: (3, {})} | custom-call | flops 20000000000 | bytes 20000000 | tf_op jit(solution)/shard_map/pallas_call | solution.py:423
  182.6 3.3 %collective-permute-done.17.refs_2_ = bf16[1,128,1536]{2,1,0:T(8,128)(2,1)S(1)} collective-permute-done((bf16[1,128,1536]{2,1,0:T(8,128)(2,1)S(1)}, bf16[1,128,1536]{2,1,0:T(8,128)(2,1)S(1)}, u32[]{:S(2)}, u32[]{:S(2)}) %collective-permute-start.17) | collective-permute-done | bytes 393248 | tf_op jit(solution)/shard_map/ppermute | solution.py:457
  (86 shorter events, 28.3 us)
Async XLA Ops:
  7.2 76.7 %all-gather.2.cloned.1.call-start = ((), (), s32[]{:S(2)}) async-start(), calls=%async_computation | async-start | bytes 6684672 | tf_op jit(solution)/shard_map/all_gather | solution.py:472
  10.6 4.7 %copy-start = (bf16[576,2048]{1,0:T(8,128)(2,1)S(1)}, bf16[576,2048]{1,0:T(8,128)(2,1)}, u32[]{:S(2)}) copy-start(bf16[576,2048]{1,0:T(8,128)(2,1)} %q_ref.15) | copy-start | bytes 7077892
  10.6 22.7 %collective-permute-start.1 = (bf16[3,576,256]{2,1,0:T(8,128)(2,1)}, bf16[3,576,256]{2,1,0:T(8,128)(2,1)S(1)}, u32[]{:S(2)}, u32[]{:S(2)}) collective-permute-start(bf16[3,576,256]{2,1,0:T(8,128)(2,1)} %shard_map.140.rest_0_), channel_id=1, source_target_pairs={{0,1},{1,0},{2,3},{3,2},{4,5},{5,4},{6,7},{7,6},{8,9},{9,8},{10,11... | collective-permute-start | bytes 2654216 | tf_op jit(solution)/shard_map/ppermute | solution.py:484
  14.9 37.5 %collective-permute-start.3 = (bf16[3,576,256]{2,1,0:T(8,128)(2,1)}, bf16[3,576,256]{2,1,0:T(8,128)(2,1)S(1)}, u32[]{:S(2)}, u32[]{:S(2)}) collective-permute-start(bf16[3,576,256]{2,1,0:T(8,128)(2,1)} %shard_map.141.rest_0_), channel_id=1, source_target_pairs={{0,1},{1,0},{2,3},{3,2},{4,5},{5,4},{6,7},{7,6},{8,9},{9,8},{10,11... | collective-permute-start | bytes 2654216 | tf_op jit(solution)/shard_map/ppermute | solution.py:484
  19.9 3.0 %copy-start.10 = (s32[1152]{0:T(1024)S(1)}, s32[1152]{0:T(1024)}, u32[]{:S(2)}) copy-start(s32[1152]{0:T(1024)} %constant.80) | copy-start | bytes 13828
  19.9 3.0 %copy-start.11 = (s32[1152]{0:T(1024)S(1)}, s32[1152]{0:T(1024)}, u32[]{:S(2)}) copy-start(s32[1152]{0:T(1024)} %constant.82) | copy-start | bytes 13828
  19.9 3.0 %copy-start.12 = (s32[1152]{0:T(1024)S(1)}, s32[1152]{0:T(1024)}, u32[]{:S(2)}) copy-start(s32[1152]{0:T(1024)} %constant.84) | copy-start | bytes 13828
  21.1 50.2 %collective-permute-start.5 = (bf16[3,576,256]{2,1,0:T(8,128)(2,1)S(1)}, bf16[3,576,256]{2,1,0:T(8,128)(2,1)S(1)}, u32[]{:S(2)}, u32[]{:S(2)}) collective-permute-start(bf16[3,576,256]{2,1,0:T(8,128)(2,1)S(1)} %shard_map.142.rest_0_), channel_id=1, source_target_pairs={{0,1},{1,0},{2,3},{3,2},{4,5},{5,4},{6,7},{7,6},{8,9},{9,8},{10,11... | collective-permute-start | bytes 2654216 | tf_op jit(solution)/shard_map/ppermute | solution.py:484
  23.7 47.6 %copy-start.3 = (f32[16,24,1152]{2,1,0:T(8,128)}, f32[16,24,1152]{2,1,0:T(8,128)S(1)}, u32[]{:S(2)}) copy-start(f32[16,24,1152]{2,1,0:T(8,128)S(1)} %and_select_fusion.bias_ref) | copy-start | bytes 5308420
  40.6 19.0 %copy-start.9 = (bf16[1,1536]{1,0:T(2,128)(2,1)S(1)}, bf16[1,1536]{1,0:T(2,128)(2,1)}, u32[]{:S(2)}) copy-start(bf16[1,1536]{1,0:T(2,128)(2,1)} %param.20) | copy-start | bytes 9220
  60.8 23.3 %collective-permute-start.4 = (bf16[1152,256]{1,0:T(8,128)(2,1)}, bf16[1152,256]{1,0:T(8,128)(2,1)}, u32[]{:S(2)}, u32[]{:S(2)}) collective-permute-start(bf16[1152,256]{1,0:T(8,128)(2,1)} %shard_map.144.rest_0_.refs_2_), channel_id=1, source_target_pairs={{0,1},{1,0},{2,3},{3,2},{4,5},{5,4},{6,7},{7,6},{8,9},{9,8},{10,11... | collective-permute-start | bytes 1769480 | tf_op jit(solution)/shard_map/ppermute | solution.py:484
  62.4 34.3 %collective-permute-start.2 = (bf16[1152,256]{1,0:T(8,128)(2,1)}, bf16[1152,256]{1,0:T(8,128)(2,1)}, u32[]{:S(2)}, u32[]{:S(2)}) collective-permute-start(bf16[1152,256]{1,0:T(8,128)(2,1)} %shard_map.143.rest_0_.refs_0_), channel_id=1, source_target_pairs={{0,1},{1,0},{2,3},{3,2},{4,5},{5,4},{6,7},{7,6},{8,9},{9,8},{10,11... | collective-permute-start | bytes 1769480 | tf_op jit(solution)/shard_map/ppermute | solution.py:484
  62.9 52.8 %collective-permute-start.7 = (bf16[3,576,256]{2,1,0:T(8,128)(2,1)S(1)}, bf16[3,576,256]{2,1,0:T(8,128)(2,1)}, u32[]{:S(2)}, u32[]{:S(2)}) collective-permute-start(bf16[3,576,256]{2,1,0:T(8,128)(2,1)S(1)} %shard_map.145.rest_1_), channel_id=1, source_target_pairs={{0,1},{1,0},{2,3},{3,2},{4,5},{5,4},{6,7},{7,6},{8,9},{9,8},{10,11... | collective-permute-start | bytes 2654216 | tf_op jit(solution)/shard_map/ppermute | solution.py:484
  71.3 8.8 %copy-start.8 = (bf16[1152,1536]{1,0:T(8,128)(2,1)S(1)}, bf16[1152,1536]{1,0:T(8,128)(2,1)}, u32[]{:S(2)}) copy-start(bf16[1152,1536]{1,0:T(8,128)(2,1)} %param.21) | copy-start | bytes 10616836
  78.6 49.6 %collective-permute-start.6 = (bf16[1152,256]{1,0:T(8,128)(2,1)}, bf16[1152,256]{1,0:T(8,128)(2,1)S(1)}, u32[]{:S(2)}, u32[]{:S(2)}) collective-permute-start(bf16[1152,256]{1,0:T(8,128)(2,1)} %shard_map.146.refs_0_.refs_4_), channel_id=1, source_target_pairs={{0,1},{1,0},{2,3},{3,2},{4,5},{5,4},{6,7},{7,6},{8,9},{9,8},{10,11... | collective-permute-start | bytes 1769480 | tf_op jit(solution)/shard_map/ppermute | solution.py:484
  104.7 3.5 %collective-permute-start = (bf16[4,128,1536]{2,1,0:T(8,128)(2,1)S(1)}, bf16[4,128,1536]{2,1,0:T(8,128)(2,1)S(1)}, u32[]{:S(2)}, u32[]{:S(2)}) collective-permute-start(bf16[4,128,1536]{2,1,0:T(8,128)(2,1)S(1)} %get-tuple-element.22), channel_id=1, source_target_pairs={{0,2},{2,0},{4,6},{6,4},{8,10},{10,8},{12,14},{14,12},{16,18},{18,... | collective-permute-start | bytes 4718600 | tf_op jit(solution)/shard_map/cond/branch_1_fun/ppermute | solution.py:457
  110.0 24.7 %collective-permute-start.10 = (bf16[4,128,1536]{2,1,0:T(8,128)(2,1)}, bf16[4,128,1536]{2,1,0:T(8,128)(2,1)S(1)}, u32[]{:S(2)}, u32[]{:S(2)}) collective-permute-start(bf16[4,128,1536]{2,1,0:T(8,128)(2,1)} %get-tuple-element.82.rest_0_.refs_0_.refs_2_), channel_id=1, source_target_pairs={{2,6},{4,0},{10,14},{12,8},{18,22},{20,16},{26,30},{28,24},{3,7},{... | collective-permute-start | bytes 4718600 | tf_op jit(solution)/shard_map/ppermute | solution.py:457
  123.7 16.0 %collective-permute-start.8 = (bf16[1152,256]{1,0:T(8,128)(2,1)}, bf16[1152,256]{1,0:T(8,128)(2,1)S(1)}, u32[]{:S(2)}, u32[]{:S(2)}) collective-permute-start(bf16[1152,256]{1,0:T(8,128)(2,1)} %shard_map.147.refs_3_.refs_0_.refs_6_), channel_id=1, source_target_pairs={{0,1},{1,0},{2,3},{3,2},{4,5},{5,4},{6,7},{7,6},{8,9},{9,8},{10,11... | collective-permute-start | bytes 1769480 | tf_op jit(solution)/shard_map/ppermute | solution.py:484
  134.6 3.4 %collective-permute-start.9 = (bf16[2,128,1536]{2,1,0:T(8,128)(2,1)S(1)}, bf16[2,128,1536]{2,1,0:T(8,128)(2,1)S(1)}, u32[]{:S(2)}, u32[]{:S(2)}) collective-permute-start(bf16[2,128,1536]{2,1,0:T(8,128)(2,1)S(1)} %get-tuple-element.47.refs_4_), channel_id=1, source_target_pairs={{0,2},{2,0},{4,6},{6,4},{8,10},{10,8},{12,14},{14,12},{16,18},{18,... | collective-permute-start | bytes 2359304 | tf_op jit(solution)/shard_map/ppermute | solution.py:457
  134.7 5.0 %copy-start.7 = (bf16[1152,1536]{1,0:T(8,128)(2,1)S(1)}, bf16[1152,1536]{1,0:T(8,128)(2,1)}, u32[]{:S(2)}) copy-start(bf16[1152,1536]{1,0:T(8,128)(2,1)} %multiply_convert_fusion.refs_2_) | copy-start | bytes 10616836
  137.1 14.9 %collective-permute-start.12 = (bf16[2,128,1536]{2,1,0:T(8,128)(2,1)S(1)}, bf16[2,128,1536]{2,1,0:T(8,128)(2,1)S(1)}, u32[]{:S(2)}, u32[]{:S(2)}) collective-permute-start(bf16[2,128,1536]{2,1,0:T(8,128)(2,1)S(1)} %get-tuple-element.48.refs_2_), channel_id=1, source_target_pairs={{0,8},{6,14},{8,0},{14,6},{16,24},{22,30},{24,16},{30,22},{1,9},{7... | collective-permute-start | bytes 2359304 | tf_op jit(solution)/shard_map/ppermute | solution.py:457
  138.2 14.6 %collective-permute-start.11 = (bf16[2,128,1536]{2,1,0:T(8,128)(2,1)S(1)}, bf16[2,128,1536]{2,1,0:T(8,128)(2,1)S(1)}, u32[]{:S(2)}, u32[]{:S(2)}) collective-permute-start(bf16[2,128,1536]{2,1,0:T(8,128)(2,1)S(1)} %shard_map.150.refs_3_.refs_0_), channel_id=1, source_target_pairs={{0,4},{6,2},{8,12},{14,10},{16,20},{22,18},{24,28},{30,26},{1,5},{... | collective-permute-start | bytes 2359304 | tf_op jit(solution)/shard_map/ppermute | solution.py:457
  139.7 15.3 %slice-start = ((s8[6291456]{0:T(1024)(128)(4,1)}), s8[4194304]{0:T(1024)(128)(4,1)S(1)}, s32[]{:S(2)}) async-start(s8[6291456]{0:T(1024)(128)(4,1)} %bitcast.24), calls=%async_computation.1 | async-start | bytes 8388608
  143.5 11.5 %slice-start.1 = ((s8[6291456]{0:T(1024)(128)(4,1)}), s8[2097152]{0:T(1024)(128)(4,1)S(1)}, s32[]{:S(2)}) async-start(s8[6291456]{0:T(1024)(128)(4,1)} %bitcast.24), calls=%async_computation.2 | async-start | bytes 4194304
  143.5 6.9 %collective-permute-start.13 = (bf16[2,128,1536]{2,1,0:T(8,128)(2,1)S(1)}, bf16[2,128,1536]{2,1,0:T(8,128)(2,1)S(1)}, u32[]{:S(2)}, u32[]{:S(2)}) collective-permute-start(bf16[2,128,1536]{2,1,0:T(8,128)(2,1)S(1)} %get-tuple-element.49.refs_8_), channel_id=1, source_target_pairs={{0,2},{2,0},{4,6},{6,4},{8,10},{10,8},{12,14},{14,12},{16,18},{18,... | collective-permute-start | bytes 2359304 | tf_op jit(solution)/shard_map/ppermute | solution.py:457
  150.7 13.9 %collective-permute-start.15 = (bf16[2,128,1536]{2,1,0:T(8,128)(2,1)S(1)}, bf16[2,128,1536]{2,1,0:T(8,128)(2,1)S(1)}, u32[]{:S(2)}, u32[]{:S(2)}) collective-permute-start(bf16[2,128,1536]{2,1,0:T(8,128)(2,1)S(1)} %shard_map.153.refs_4_.refs_0_.refs_2_), channel_id=1, source_target_pairs={{0,4},{6,2},{8,12},{14,10},{16,20},{22,18},{24,28},{30,26},{1,5},{... | collective-permute-start | bytes 2359304 | tf_op jit(solution)/shard_map/ppermute | solution.py:457
  153.0 20.7 %collective-permute-start.14 = (bf16[2,128,1536]{2,1,0:T(8,128)(2,1)S(1)}, bf16[2,128,1536]{2,1,0:T(8,128)(2,1)S(1)}, u32[]{:S(2)}, u32[]{:S(2)}) collective-permute-start(bf16[2,128,1536]{2,1,0:T(8,128)(2,1)S(1)} %shard_map.155.refs_0_), channel_id=1, source_target_pairs={{10,2},{12,4},{18,26},{20,28},{11,3},{13,5},{19,27},{21,29}} | collective-permute-start | bytes 2359304 | tf_op jit(solution)/shard_map/ppermute | solution.py:457
  154.3 28.3 %collective-permute-start.16 = (bf16[1,128,1536]{2,1,0:T(8,128)(2,1)S(1)}, bf16[1,128,1536]{2,1,0:T(8,128)(2,1)S(1)}, u32[]{:S(2)}, u32[]{:S(2)}) collective-permute-start(bf16[1,128,1536]{2,1,0:T(8,128)(2,1)S(1)} %get-tuple-element.54.refs_2_), channel_id=1, source_target_pairs={{0,16},{6,22},{8,24},{14,30},{16,0},{22,6},{24,8},{30,14},{1,17},{... | collective-permute-start | bytes 1179656 | tf_op jit(solution)/shard_map/ppermute | solution.py:457
  165.3 20.6 %collective-permute-start.18 = (bf16[1,128,1536]{2,1,0:T(8,128)(2,1)S(1)}, bf16[1,128,1536]{2,1,0:T(8,128)(2,1)S(1)}, u32[]{:S(2)}, u32[]{:S(2)}) collective-permute-start(bf16[1,128,1536]{2,1,0:T(8,128)(2,1)S(1)} %get-tuple-element.64), channel_id=1, source_target_pairs={{2,18},{4,20},{26,10},{28,12},{3,19},{5,21},{27,11},{29,13}} | collective-permute-start | bytes 1179656 | tf_op jit(solution)/shard_map/ppermute | solution.py:457
  169.9 16.1 %collective-permute-start.19 = (bf16[1,128,1536]{2,1,0:T(8,128)(2,1)S(1)}, bf16[1,128,1536]{2,1,0:T(8,128)(2,1)S(1)}, u32[]{:S(2)}, u32[]{:S(2)}) collective-permute-start(bf16[1,128,1536]{2,1,0:T(8,128)(2,1)S(1)} %get-tuple-element.64), channel_id=1, source_target_pairs={{10,18},{12,20},{18,10},{20,12},{11,19},{13,21},{19,11},{21,13}} | collective-permute-start | bytes 1179656 | tf_op jit(solution)/shard_map/ppermute | solution.py:457
  170.6 15.4 %collective-permute-start.20 = (bf16[1,128,1536]{2,1,0:T(8,128)(2,1)S(1)}, bf16[1,128,1536]{2,1,0:T(8,128)(2,1)S(1)}, u32[]{:S(2)}, u32[]{:S(2)}) collective-permute-start(bf16[1,128,1536]{2,1,0:T(8,128)(2,1)S(1)} %get-tuple-element.57.refs_6_), channel_id=1, source_target_pairs={{2,10},{4,12},{26,18},{28,20},{3,11},{5,13},{27,19},{29,21}} | collective-permute-start | bytes 1179656 | tf_op jit(solution)/shard_map/ppermute | solution.py:457
  174.5 11.5 %collective-permute-start.17 = (bf16[1,128,1536]{2,1,0:T(8,128)(2,1)S(1)}, bf16[1,128,1536]{2,1,0:T(8,128)(2,1)S(1)}, u32[]{:S(2)}, u32[]{:S(2)}) collective-permute-start(bf16[1,128,1536]{2,1,0:T(8,128)(2,1)S(1)} %get-tuple-element.58.refs_1_), channel_id=1, source_target_pairs={{2,26},{4,28},{26,2},{28,4},{3,27},{5,29},{27,3},{29,5}} | collective-permute-start | bytes 1179656 | tf_op jit(solution)/shard_map/ppermute | solution.py:457
  (9 other events, 19.5 us)
Sparse Core Ops, SparseCore 0:
  10.3 62.1 all-gather.1

commit v2 on v1

--- a/solution.py
+++ b/solution.py
@@ -544,9 +544,10 @@
     gate = gate_row[None]
     out, done = project(columns, weight, gate, range(3), (), (sent_b,))
     kept_c, near_c, far_c = reach_step(place, [total_c, across_c], (done,))
-    reached_c = dp_send(far_c, 8, outer), dp_send(far_c, 12, inner), dp_send(near_c, 4, outer)
-    kept_b, sent_b = level_step(place, HIGH, [total_b, across_b, low_b], (near_c,))
+    reached_c = dp_send(far_c, 8, outer), dp_send(far_c, 12, inner)
+    kept_b, sent_b = level_step(place, HIGH, [total_b, across_b, low_b], (far_c,))
     high_b = dp_send(sent_b, 12, outer)
+    reached_c += (dp_send(after(near_c, sent_b), 4, outer),)
     last = range(3, PROJECT_STEPS)
     block_out, done = project(columns, weight, gate, last, (out,), (sent_b,), LONG_COST)
     final_a = total_step([kept_a, high_a], (done,), jnp.float32)

time: 195 us -> 196 us (level)
  transfers between devices with their start and end apart: 22 -> 22, of which waited for: 12 -> 13; matrix products, arithmetic and copies ran while one was open for 2% -> 2% of each run, Pallas kernels for 39% -> 39%
where the time goes in v2:
time: 196 us; the launch traced here: 195 us
  Pallas kernels  77.9 us (40%)
  waiting for transfers between devices  59.7 us (30%)
  starting transfers between devices  32.2 us (16%)
  between operations  15 us (8%)
  local copies, waits for them, and re-layouts  6.27 us (3%)
  other arithmetic  3.61 us (2%)
    ppermute x8, waiting for transfers between devices, exchange(): return lax.ppermute(mine, 'seq', swap)  47.8 us
    pallas_call x4, Pallas kernels, attend_pair(): pl.pallas_call(pair_kernel, grid_spec=pltpu.PrefetchScalarGridSpec(num_sc...  29.9 us
    ppermute x13, starting transfers between devices, dp_send(): lax.ppermute(value, 'dp', [(i, i ^ flip) for i in range(HEADS) if sender(...  21.9 us
    pallas_call x3, Pallas kernels, batch_gradient(): pl.pallas_call(functools.partial(gradient_kernel, by_call=by_call), grid_...  17.2 us
    ppermute x13, waiting for transfers between devices, dp_send(): lax.ppermute(value, 'dp', [(i, i ^ flip) for i in range(HEADS) if sender(...  11.2 us
    pallas_call x2, Pallas kernels, project(): pl.pallas_call(kernel, grid=(steps,), in_specs=[pl.BlockSpec((rows, depth...  10.5 us
    ppermute x8, starting transfers between devices, exchange(): return lax.ppermute(mine, 'seq', swap)  10.3 us
    pallas_call x4, Pallas kernels, pack_partner(): pl.pallas_call(pack_kernel, grid_spec=pltpu.PrefetchScalarGridSpec(num_sc...  7.59 us
  transfers between devices with their start and end apart: 22, of which 13 were waited for; matrix products, arithmetic and copies ran while one was open for 2% of the time, Pallas kernels for 39%

profile of v2, /device:TPU:2, one launch (start us, length us, event | category | flops | bytes accessed | tf_op | source)
XLA Modules:
  0.0 194.7 jit_solution(3449918900746369168)
XLA Ops:
  8.0 2.6 %shard_map.140.rest_0_ = bf16[3,576,256]{2,1,0:T(8,128)(2,1)} custom-call(s32[5]{0:T(128)S(1)} %stack.23.place_ref, bf16[576,2048]{1,0:T(8,128)(2,1)} %q_ref.15, bf16[576,2048]{1,0:T(8,128)(2,1)} %k_ref.15, bf16[576,2048]{1,0:T(8,128)(2,1)} %v_ref.15), custom_call_target="tpu_custom_call" | custom-call | flops 1 | bytes 1 | tf_op jit(solution)/shard_map/pallas_call | solution.py:186
  12.1 2.7 %shard_map.141.rest_0_ = bf16[3,576,256]{2,1,0:T(8,128)(2,1)} custom-call(s32[5]{0:T(128)S(1)} %stack.23.place_ref, bf16[576,2048]{1,0:T(8,128)(2,1)} %q_ref.15, bf16[576,2048]{1,0:T(8,128)(2,1)} %k_ref.15, bf16[576,2048]{1,0:T(8,128)(2,1)} %v_ref.15, bf16[3,576,256]{2,1,0:T(8,128)(2,1)} %shard_map.140.rest_0_), custom_call_target="tpu_custom_call" | custom-call | flops 1 | bytes 1 | tf_op jit(solution)/shard_map/pallas_call | solution.py:186
  15.4 1.7 copy-done.1
  17.0 1.7 copy-done.2
  21.1 1.6 collective-permute-start.5
  23.7 9.6 %collective-permute-done.1.other_ref = bf16[3,576,256]{2,1,0:T(8,128)(2,1)S(1)} collective-permute-done((bf16[3,576,256]{2,1,0:T(8,128)(2,1)}, bf16[3,576,256]{2,1,0:T(8,128)(2,1)S(1)}, u32[]{:S(2)}, u32[]{:S(2)}) %collective-permute-start.1) | collective-permute-done | bytes 884768 | tf_op jit(solution)/shard_map/ppermute | solution.py:484
  33.4 7.3 %shard_map.143.rest_0_.refs_0_ = bf16[1152,256]{1,0:T(8,128)(2,1)} custom-call(s32[5]{0:T(128)S(1)} %stack.23.place_ref, bf16[576,2048]{1,0:T(8,128)(2,1)S(1)} %copy-done, bf16[576,2048]{1,0:T(8,128)(2,1)S(1)} %copy-done.1, bf16[576,2048]{1,0:T(8,128)(2,1)S(1)} %copy-done.2, bf16[3,576,256]{2,1,0:T(8,128)(2,1)S(1)} %collective-permute-done.1.other_ref, ...), custom_call_target="tpu_custom_call" | custom-call | flops 1 | bytes 1 | tf_op jit(solution)/shard_map/pallas_call | solution.py:117
  40.6 11.7 %collective-permute-done.3.other_ref = bf16[3,576,256]{2,1,0:T(8,128)(2,1)S(1)} collective-permute-done((bf16[3,576,256]{2,1,0:T(8,128)(2,1)}, bf16[3,576,256]{2,1,0:T(8,128)(2,1)S(1)}, u32[]{:S(2)}, u32[]{:S(2)}) %collective-permute-start.3) | collective-permute-done | bytes 884768 | tf_op jit(solution)/shard_map/ppermute | solution.py:484
  52.3 7.3 %shard_map.144.rest_0_.refs_2_ = bf16[1152,256]{1,0:T(8,128)(2,1)} custom-call(s32[5]{0:T(128)S(1)} %stack.23.place_ref, bf16[576,2048]{1,0:T(8,128)(2,1)S(1)} %copy-done, bf16[576,2048]{1,0:T(8,128)(2,1)S(1)} %copy-done.1, bf16[576,2048]{1,0:T(8,128)(2,1)S(1)} %copy-done.2, bf16[3,576,256]{2,1,0:T(8,128)(2,1)S(1)} %collective-permute-done.3.other_ref, ...), custom_call_target="tpu_custom_call" | custom-call | flops 1 | bytes 1 | tf_op jit(solution)/shard_map/pallas_call | solution.py:117
  64.4 6.9 %collective-permute-done.5.other_ref = bf16[3,576,256]{2,1,0:T(8,128)(2,1)S(1)} collective-permute-done((bf16[3,576,256]{2,1,0:T(8,128)(2,1)S(1)}, bf16[3,576,256]{2,1,0:T(8,128)(2,1)S(1)}, u32[]{:S(2)}, u32[]{:S(2)}) %collective-permute-start.5) | collective-permute-done | bytes 884768 | tf_op jit(solution)/shard_map/ppermute | solution.py:484
  71.3 7.3 %shard_map.146.refs_0_.refs_4_ = bf16[1152,256]{1,0:T(8,128)(2,1)} custom-call(s32[5]{0:T(128)S(1)} %stack.23.place_ref, bf16[576,2048]{1,0:T(8,128)(2,1)S(1)} %copy-done, bf16[576,2048]{1,0:T(8,128)(2,1)S(1)} %copy-done.1, bf16[576,2048]{1,0:T(8,128)(2,1)S(1)} %copy-done.2, bf16[3,576,256]{2,1,0:T(8,128)(2,1)S(1)} %collective-permute-done.5.other_ref, ...), custom_call_target="tpu_custom_call" | custom-call | flops 1 | bytes 1 | tf_op jit(solution)/shard_map/pallas_call | solution.py:117
  80.1 2.6 %multiply_convert_fusion.refs_2_ = bf16[1152,1536]{1,0:T(8,128)(2,1)} fusion(bf16[1152,1536]{1,0:T(8,128)(2,1)S(1)} %copy-done.8, f32[1536]{0:T(1024)S(1)} %convert_reduce_fusion), kind=kLoop, calls=%fused_computation | loop fusion | flops 5308416 | bytes 7084032 | tf_op jit(solution)/shard_map/convert_element_type | solution.py:474
  84.0 12.6 %collective-permute-done.2.refs_1_ = bf16[1152,256]{1,0:T(8,128)(2,1)} collective-permute-done((bf16[1152,256]{1,0:T(8,128)(2,1)}, bf16[1152,256]{1,0:T(8,128)(2,1)}, u32[]{:S(2)}, u32[]{:S(2)}) %collective-permute-start.2) | collective-permute-done | bytes 589856 | tf_op jit(solution)/shard_map/ppermute | solution.py:484
  96.7 13.3 %conditional.1 = (bf16[4,128,1536]{2,1,0:T(8,128)(2,1)}) conditional(s32[]{:T(128)} %bitcast.14, () %tuple.16, (s32[5]{0:T(128)S(1)}, bf16[1152,256]{1,0:T(8,128)(2,1)}, bf16[1152,256]{1,0:T(8,128)(2,1)}, bf16[1152,256]{1,0:T(8,128)(2,1)}, bf16[1152,256]{1,0:T(8,128)(2,1)}, /*index=5*/bf16[1152,1536]{1,0:T(8,128)(2,1)}) %tuple.18), branch_computations={%region_0.1_spmd, %region_1.2_spmd} | conditional | flops 2 | bytes 6291506 | solution.py:492
  96.7 8.0 %branch_1_fun.2 = (bf16[4,128,1536]{2,1,0:T(8,128)(2,1)S(1)}, bf16[4,128,1536]{2,1,0:T(8,128)(2,1)S(1)}) custom-call(s32[5]{0:T(128)S(1)} %get-tuple-element.5.place_ref, bf16[1152,256]{1,0:T(8,128)(2,1)} %get-tuple-element.16.refs_0_, bf16[1152,256]{1,0:T(8,128)(2,1)} %get-tuple-element.17.refs_1_, bf16[1152,256]{1,0:T(8,128)(2,1)} %get-tuple-element.18.refs_2_, ...), custom_call_target="tpu_custom_call" | custom-call | flops 1 | bytes 1 | tf_op jit(solution)/shard_map/cond/branch_1_fun/pallas_call | solution.py:239
  104.8 3.4 %collective-permute-done.refs_1_ = bf16[4,128,1536]{2,1,0:T(8,128)(2,1)S(1)} collective-permute-done((bf16[4,128,1536]{2,1,0:T(8,128)(2,1)S(1)}, bf16[4,128,1536]{2,1,0:T(8,128)(2,1)S(1)}, u32[]{:S(2)}, u32[]{:S(2)}) %collective-permute-start) | collective-permute-done | bytes 1572896 | tf_op jit(solution)/shard_map/cond/branch_1_fun/ppermute | solution.py:457
  108.1 1.9 branch_1_fun.3
  110.0 2.0 %collective-permute-start.10 = (bf16[4,128,1536]{2,1,0:T(8,128)(2,1)}, bf16[4,128,1536]{2,1,0:T(8,128)(2,1)S(1)}, u32[]{:S(2)}, u32[]{:S(2)}) collective-permute-start(bf16[4,128,1536]{2,1,0:T(8,128)(2,1)} %get-tuple-element.84.rest_0_.refs_0_.refs_2_), channel_id=1, source_target_pairs={{2,6},{4,0},{10,14},{12,8},{18,22},{20,16},{26,30},{28,24},{3,7},{... | collective-permute-start | bytes 4718600 | tf_op jit(solution)/shard_map/ppermute | solution.py:457
  112.0 3.6 %collective-permute-done.7.other_ref = bf16[3,576,256]{2,1,0:T(8,128)(2,1)} collective-permute-done((bf16[3,576,256]{2,1,0:T(8,128)(2,1)S(1)}, bf16[3,576,256]{2,1,0:T(8,128)(2,1)}, u32[]{:S(2)}, u32[]{:S(2)}) %collective-permute-start.7) | collective-permute-done | bytes 884768 | tf_op jit(solution)/shard_map/ppermute | solution.py:484
  115.6 8.1 %shard_map.147.refs_3_.refs_0_.refs_6_ = bf16[1152,256]{1,0:T(8,128)(2,1)} custom-call(s32[5]{0:T(128)S(1)} %stack.23.place_ref, bf16[576,2048]{1,0:T(8,128)(2,1)} %q_ref.15, bf16[576,2048]{1,0:T(8,128)(2,1)} %k_ref.15, bf16[576,2048]{1,0:T(8,128)(2,1)} %v_ref.15, bf16[3,576,256]{2,1,0:T(8,128)(2,1)} %collective-permute-done.7.other_ref, ...), custom_call_target="tpu_custom_call" | custom-call | flops 1 | bytes 1 | tf_op jit(solution)/shard_map/pallas_call | solution.py:117
  125.2 2.9 %collective-permute-done.6.refs_1_.refs_5_ = bf16[1152,256]{1,0:T(8,128)(2,1)S(1)} collective-permute-done((bf16[1152,256]{1,0:T(8,128)(2,1)}, bf16[1152,256]{1,0:T(8,128)(2,1)S(1)}, u32[]{:S(2)}, u32[]{:S(2)}) %collective-permute-start.6) | collective-permute-done | bytes 589856 | tf_op jit(solution)/shard_map/ppermute | solution.py:484
  129.2 5.4 %shard_map.148 = (bf16[2,128,1536]{2,1,0:T(8,128)(2,1)S(1)}, bf16[2,128,1536]{2,1,0:T(8,128)(2,1)S(1)}) custom-call(s32[5]{0:T(128)S(1)} %stack.23.place_ref, bf16[1152,256]{1,0:T(8,128)(2,1)} %shard_map.146.refs_0_.refs_4_, bf16[1152,256]{1,0:T(8,128)(2,1)S(1)} %collective-permute-done.6.refs_1_.refs_5_, bf16[1152,1536]{1,0:T(8,128)(2,1)} %multiply_convert_fusion.refs_2_, ...), custom_call_target="tpu_custom_call" | custom-call | flops 20000000000 | bytes 20000000 | tf_op jit(solution)/shard_map/pallas_call | solution.py:239
  134.7 2.4 %shard_map.149 = (f32[2,128,1536]{2,1,0:T(8,128)S(1)}, bf16[2,128,1536]{2,1,0:T(8,128)(2,1)S(1)}) custom-call(s32[5]{0:T(128)S(1)} %stack.23.place_ref, bf16[4,128,1536]{2,1,0:T(8,128)(2,1)} %get-tuple-element.84.rest_0_.refs_0_.refs_2_, bf16[4,128,1536]{2,1,0:T(8,128)(2,1)S(1)} %collective-permute-done.10.refs_1_.refs_3_, ...), custom_call_target="tpu_custom_call" | custom-call | flops 20000000000 | bytes 20000000 | tf_op jit(solution)/shard_map/pallas_call | solution.py:277
  139.7 3.8 %shard_map.151 = (bf16[2,128,1536]{2,1,0:T(8,128)(2,1)S(1)}, bf16[2,128,1536]{2,1,0:T(8,128)(2,1)S(1)}) custom-call(s32[5]{0:T(128)S(1)} %stack.23.place_ref, bf16[1152,256]{1,0:T(8,128)(2,1)S(1)} %copy-done.6, bf16[1152,256]{1,0:T(8,128)(2,1)S(1)} %collective-permute-done.8.refs_1_.refs_7_, bf16[1152,1536]{1,0:T(8,128)(2,1)S(1)} %copy-done.7, ...), custom_call_target="tpu_custom_call" | custom-call | flops 1 | bytes 1 | tf_op jit(solution)/shard_map/pallas_call | solution.py:239
  143.5 3.0 %collective-permute-start.13 = (bf16[2,128,1536]{2,1,0:T(8,128)(2,1)S(1)}, bf16[2,128,1536]{2,1,0:T(8,128)(2,1)S(1)}, u32[]{:S(2)}, u32[]{:S(2)}) collective-permute-start(bf16[2,128,1536]{2,1,0:T(8,128)(2,1)S(1)} %get-tuple-element.50.refs_8_), channel_id=1, source_target_pairs={{0,2},{2,0},{4,6},{6,4},{8,10},{10,8},{12,14},{14,12},{16,18},{18,... | collective-permute-start | bytes 2359304 | tf_op jit(solution)/shard_map/ppermute | solution.py:457
  146.5 4.0 %shard_map.152 = (bf16[1152,2048]{1,0:T(8,128)(2,1)S(1)}, f32[8,128]{1,0:T(8,128)S(1)}) custom-call(s32[5]{0:T(128)S(1)} %stack.23.place_ref, bf16[1152,256]{1,0:T(8,128)(2,1)} %shard_map.143.rest_0_.refs_0_, bf16[1152,256]{1,0:T(8,128)(2,1)} %collective-permute-done.2.refs_1_, bf16[1152,256]{1,0:T(8,128)(2,1)} %shard_map.144.rest_0_.refs_2_, ...), custom_call_target="tpu_custom_call" | custom-call | flops 20000000000 | bytes 20000000 | tf_op jit(solution)/shard_map/pallas_call | solution.py:390
  155.0 5.3 %shard_map.156 = (bf16[1152,1536]{1,0:T(8,128)(2,1)}, f32[8,128]{1,0:T(8,128)S(1)}) custom-call(bf16[1152,2048]{1,0:T(8,128)(2,1)S(1)} %get-tuple-element.51.attention_ref, bf16[2048,1536]{1,0:T(8,128)(2,1)S(1)} %bitcast.25, f32[1,1536]{1,0:T(1,128)S(1)} %convert_element_type.19.gate_ref, bf16[2,128,1536]{2,1,0:T(8,128)(2,1)S(1)} %shard_map.155.refs_0_), custom_call_target="tpu_custom_call" | custom-call | flops 1 | bytes 1 | tf_op jit(solution)/shard_map/pallas_call | solution.py:423
  160.3 4.3 %collective-permute-done.15.refs_1_.refs_3_ = bf16[2,128,1536]{2,1,0:T(8,128)(2,1)S(1)} collective-permute-done((bf16[2,128,1536]{2,1,0:T(8,128)(2,1)S(1)}, bf16[2,128,1536]{2,1,0:T(8,128)(2,1)S(1)}, u32[]{:S(2)}, u32[]{:S(2)}) %collective-permute-start.15) | collective-permute-done | bytes 786464 | tf_op jit(solution)/shard_map/ppermute | solution.py:457
  165.3 4.5 %collective-permute-start.18 = (bf16[1,128,1536]{2,1,0:T(8,128)(2,1)S(1)}, bf16[1,128,1536]{2,1,0:T(8,128)(2,1)S(1)}, u32[]{:S(2)}, u32[]{:S(2)}) collective-permute-start(bf16[1,128,1536]{2,1,0:T(8,128)(2,1)S(1)} %get-tuple-element.58.refs_6_), channel_id=1, source_target_pairs={{2,18},{4,20},{26,10},{28,12},{3,19},{5,21},{27,11},{29,13}} | collective-permute-start | bytes 1179656 | tf_op jit(solution)/shard_map/ppermute | solution.py:457
  171.9 4.8 %collective-permute-start.17 = (bf16[1,128,1536]{2,1,0:T(8,128)(2,1)S(1)}, bf16[1,128,1536]{2,1,0:T(8,128)(2,1)S(1)}, u32[]{:S(2)}, u32[]{:S(2)}) collective-permute-start(bf16[1,128,1536]{2,1,0:T(8,128)(2,1)S(1)} %get-tuple-element.59.refs_1_), channel_id=1, source_target_pairs={{2,26},{4,28},{26,2},{28,4},{3,27},{5,29},{27,3},{29,5}} | collective-permute-start | bytes 1179656 | tf_op jit(solution)/shard_map/ppermute | solution.py:457
  178.1 5.3 %shard_map.159 = (bf16[1152,1536]{1,0:T(8,128)(2,1)}, f32[8,128]{1,0:T(8,128)S(1)}) custom-call(bf16[1152,2048]{1,0:T(8,128)(2,1)S(1)} %get-tuple-element.51.attention_ref, bf16[2048,1536]{1,0:T(8,128)(2,1)S(1)} %bitcast.25, f32[1,1536]{1,0:T(1,128)S(1)} %convert_element_type.19.gate_ref, ...), custom_call_target="tpu_custom_call", output_to_operand_aliasing={{0}: (3, {})} | custom-call | flops 20000000000 | bytes 20000000 | tf_op jit(solution)/shard_map/pallas_call | solution.py:423
  183.4 2.9 %collective-permute-done.20.refs_6_ = bf16[1,128,1536]{2,1,0:T(8,128)(2,1)S(1)} collective-permute-done((bf16[1,128,1536]{2,1,0:T(8,128)(2,1)S(1)}, bf16[1,128,1536]{2,1,0:T(8,128)(2,1)S(1)}, u32[]{:S(2)}, u32[]{:S(2)}) %collective-permute-start.20) | collective-permute-done | bytes 393248 | tf_op jit(solution)/shard_map/ppermute | solution.py:457
  (86 shorter events, 28.6 us)
Async XLA Ops:
  7.2 76.7 %all-gather.2.cloned.1.call-start = ((), (), s32[]{:S(2)}) async-start(), calls=%async_computation | async-start | bytes 6684672 | tf_op jit(solution)/shard_map/all_gather | solution.py:472
  10.6 4.7 %copy-start = (bf16[576,2048]{1,0:T(8,128)(2,1)S(1)}, bf16[576,2048]{1,0:T(8,128)(2,1)}, u32[]{:S(2)}) copy-start(bf16[576,2048]{1,0:T(8,128)(2,1)} %q_ref.15) | copy-start | bytes 7077892
  10.6 22.7 %collective-permute-start.1 = (bf16[3,576,256]{2,1,0:T(8,128)(2,1)}, bf16[3,576,256]{2,1,0:T(8,128)(2,1)S(1)}, u32[]{:S(2)}, u32[]{:S(2)}) collective-permute-start(bf16[3,576,256]{2,1,0:T(8,128)(2,1)} %shard_map.140.rest_0_), channel_id=1, source_target_pairs={{0,1},{1,0},{2,3},{3,2},{4,5},{5,4},{6,7},{7,6},{8,9},{9,8},{10,11... | collective-permute-start | bytes 2654216 | tf_op jit(solution)/shard_map/ppermute | solution.py:484
  14.9 37.5 %collective-permute-start.3 = (bf16[3,576,256]{2,1,0:T(8,128)(2,1)}, bf16[3,576,256]{2,1,0:T(8,128)(2,1)S(1)}, u32[]{:S(2)}, u32[]{:S(2)}) collective-permute-start(bf16[3,576,256]{2,1,0:T(8,128)(2,1)} %shard_map.141.rest_0_), channel_id=1, source_target_pairs={{0,1},{1,0},{2,3},{3,2},{4,5},{5,4},{6,7},{7,6},{8,9},{9,8},{10,11... | collective-permute-start | bytes 2654216 | tf_op jit(solution)/shard_map/ppermute | solution.py:484
  19.9 3.0 %copy-start.10 = (s32[1152]{0:T(1024)S(1)}, s32[1152]{0:T(1024)}, u32[]{:S(2)}) copy-start(s32[1152]{0:T(1024)} %constant.80) | copy-start | bytes 13828
  19.9 3.0 %copy-start.11 = (s32[1152]{0:T(1024)S(1)}, s32[1152]{0:T(1024)}, u32[]{:S(2)}) copy-start(s32[1152]{0:T(1024)} %constant.82) | copy-start | bytes 13828
  19.9 3.0 %copy-start.12 = (s32[1152]{0:T(1024)S(1)}, s32[1152]{0:T(1024)}, u32[]{:S(2)}) copy-start(s32[1152]{0:T(1024)} %constant.84) | copy-start | bytes 13828
  21.1 50.2 %collective-permute-start.5 = (bf16[3,576,256]{2,1,0:T(8,128)(2,1)S(1)}, bf16[3,576,256]{2,1,0:T(8,128)(2,1)S(1)}, u32[]{:S(2)}, u32[]{:S(2)}) collective-permute-start(bf16[3,576,256]{2,1,0:T(8,128)(2,1)S(1)} %shard_map.142.rest_0_), channel_id=1, source_target_pairs={{0,1},{1,0},{2,3},{3,2},{4,5},{5,4},{6,7},{7,6},{8,9},{9,8},{10,11... | collective-permute-start | bytes 2654216 | tf_op jit(solution)/shard_map/ppermute | solution.py:484
  23.7 47.6 %copy-start.3 = (f32[16,24,1152]{2,1,0:T(8,128)}, f32[16,24,1152]{2,1,0:T(8,128)S(1)}, u32[]{:S(2)}) copy-start(f32[16,24,1152]{2,1,0:T(8,128)S(1)} %and_select_fusion.bias_ref) | copy-start | bytes 5308420
  40.6 19.0 %copy-start.9 = (bf16[1,1536]{1,0:T(2,128)(2,1)S(1)}, bf16[1,1536]{1,0:T(2,128)(2,1)}, u32[]{:S(2)}) copy-start(bf16[1,1536]{1,0:T(2,128)(2,1)} %param.20) | copy-start | bytes 9220
  60.8 23.3 %collective-permute-start.4 = (bf16[1152,256]{1,0:T(8,128)(2,1)}, bf16[1152,256]{1,0:T(8,128)(2,1)}, u32[]{:S(2)}, u32[]{:S(2)}) collective-permute-start(bf16[1152,256]{1,0:T(8,128)(2,1)} %shard_map.144.rest_0_.refs_2_), channel_id=1, source_target_pairs={{0,1},{1,0},{2,3},{3,2},{4,5},{5,4},{6,7},{7,6},{8,9},{9,8},{10,11... | collective-permute-start | bytes 1769480 | tf_op jit(solution)/shard_map/ppermute | solution.py:484
  62.4 34.3 %collective-permute-start.2 = (bf16[1152,256]{1,0:T(8,128)(2,1)}, bf16[1152,256]{1,0:T(8,128)(2,1)}, u32[]{:S(2)}, u32[]{:S(2)}) collective-permute-start(bf16[1152,256]{1,0:T(8,128)(2,1)} %shard_map.143.rest_0_.refs_0_), channel_id=1, source_target_pairs={{0,1},{1,0},{2,3},{3,2},{4,5},{5,4},{6,7},{7,6},{8,9},{9,8},{10,11... | collective-permute-start | bytes 1769480 | tf_op jit(solution)/shard_map/ppermute | solution.py:484
  62.9 52.8 %collective-permute-start.7 = (bf16[3,576,256]{2,1,0:T(8,128)(2,1)S(1)}, bf16[3,576,256]{2,1,0:T(8,128)(2,1)}, u32[]{:S(2)}, u32[]{:S(2)}) collective-permute-start(bf16[3,576,256]{2,1,0:T(8,128)(2,1)S(1)} %shard_map.145.rest_1_), channel_id=1, source_target_pairs={{0,1},{1,0},{2,3},{3,2},{4,5},{5,4},{6,7},{7,6},{8,9},{9,8},{10,11... | collective-permute-start | bytes 2654216 | tf_op jit(solution)/shard_map/ppermute | solution.py:484
  71.3 8.8 %copy-start.8 = (bf16[1152,1536]{1,0:T(8,128)(2,1)S(1)}, bf16[1152,1536]{1,0:T(8,128)(2,1)}, u32[]{:S(2)}) copy-start(bf16[1152,1536]{1,0:T(8,128)(2,1)} %param.21) | copy-start | bytes 10616836
  78.6 49.6 %collective-permute-start.6 = (bf16[1152,256]{1,0:T(8,128)(2,1)}, bf16[1152,256]{1,0:T(8,128)(2,1)S(1)}, u32[]{:S(2)}, u32[]{:S(2)}) collective-permute-start(bf16[1152,256]{1,0:T(8,128)(2,1)} %shard_map.146.refs_0_.refs_4_), channel_id=1, source_target_pairs={{0,1},{1,0},{2,3},{3,2},{4,5},{5,4},{6,7},{7,6},{8,9},{9,8},{10,11... | collective-permute-start | bytes 1769480 | tf_op jit(solution)/shard_map/ppermute | solution.py:484
  104.7 3.5 %collective-permute-start = (bf16[4,128,1536]{2,1,0:T(8,128)(2,1)S(1)}, bf16[4,128,1536]{2,1,0:T(8,128)(2,1)S(1)}, u32[]{:S(2)}, u32[]{:S(2)}) collective-permute-start(bf16[4,128,1536]{2,1,0:T(8,128)(2,1)S(1)} %get-tuple-element.22), channel_id=1, source_target_pairs={{0,2},{2,0},{4,6},{6,4},{8,10},{10,8},{12,14},{14,12},{16,18},{18,... | collective-permute-start | bytes 4718600 | tf_op jit(solution)/shard_map/cond/branch_1_fun/ppermute | solution.py:457
  110.0 24.7 %collective-permute-start.10 = (bf16[4,128,1536]{2,1,0:T(8,128)(2,1)}, bf16[4,128,1536]{2,1,0:T(8,128)(2,1)S(1)}, u32[]{:S(2)}, u32[]{:S(2)}) collective-permute-start(bf16[4,128,1536]{2,1,0:T(8,128)(2,1)} %get-tuple-element.84.rest_0_.refs_0_.refs_2_), channel_id=1, source_target_pairs={{2,6},{4,0},{10,14},{12,8},{18,22},{20,16},{26,30},{28,24},{3,7},{... | collective-permute-start | bytes 4718600 | tf_op jit(solution)/shard_map/ppermute | solution.py:457
  123.7 16.0 %collective-permute-start.8 = (bf16[1152,256]{1,0:T(8,128)(2,1)}, bf16[1152,256]{1,0:T(8,128)(2,1)S(1)}, u32[]{:S(2)}, u32[]{:S(2)}) collective-permute-start(bf16[1152,256]{1,0:T(8,128)(2,1)} %shard_map.147.refs_3_.refs_0_.refs_6_), channel_id=1, source_target_pairs={{0,1},{1,0},{2,3},{3,2},{4,5},{5,4},{6,7},{7,6},{8,9},{9,8},{10,11... | collective-permute-start | bytes 1769480 | tf_op jit(solution)/shard_map/ppermute | solution.py:484
  134.6 3.4 %collective-permute-start.9 = (bf16[2,128,1536]{2,1,0:T(8,128)(2,1)S(1)}, bf16[2,128,1536]{2,1,0:T(8,128)(2,1)S(1)}, u32[]{:S(2)}, u32[]{:S(2)}) collective-permute-start(bf16[2,128,1536]{2,1,0:T(8,128)(2,1)S(1)} %get-tuple-element.48.refs_4_), channel_id=1, source_target_pairs={{0,2},{2,0},{4,6},{6,4},{8,10},{10,8},{12,14},{14,12},{16,18},{18,... | collective-permute-start | bytes 2359304 | tf_op jit(solution)/shard_map/ppermute | solution.py:457
  134.7 5.0 %copy-start.7 = (bf16[1152,1536]{1,0:T(8,128)(2,1)S(1)}, bf16[1152,1536]{1,0:T(8,128)(2,1)}, u32[]{:S(2)}) copy-start(bf16[1152,1536]{1,0:T(8,128)(2,1)} %multiply_convert_fusion.refs_2_) | copy-start | bytes 10616836
  137.1 14.9 %collective-permute-start.12 = (bf16[2,128,1536]{2,1,0:T(8,128)(2,1)S(1)}, bf16[2,128,1536]{2,1,0:T(8,128)(2,1)S(1)}, u32[]{:S(2)}, u32[]{:S(2)}) collective-permute-start(bf16[2,128,1536]{2,1,0:T(8,128)(2,1)S(1)} %get-tuple-element.49.refs_2_), channel_id=1, source_target_pairs={{0,8},{6,14},{8,0},{14,6},{16,24},{22,30},{24,16},{30,22},{1,9},{7... | collective-permute-start | bytes 2359304 | tf_op jit(solution)/shard_map/ppermute | solution.py:457
  138.2 14.6 %collective-permute-start.11 = (bf16[2,128,1536]{2,1,0:T(8,128)(2,1)S(1)}, bf16[2,128,1536]{2,1,0:T(8,128)(2,1)S(1)}, u32[]{:S(2)}, u32[]{:S(2)}) collective-permute-start(bf16[2,128,1536]{2,1,0:T(8,128)(2,1)S(1)} %shard_map.150.refs_3_.refs_0_), channel_id=1, source_target_pairs={{0,4},{6,2},{8,12},{14,10},{16,20},{22,18},{24,28},{30,26},{1,5},{... | collective-permute-start | bytes 2359304 | tf_op jit(solution)/shard_map/ppermute | solution.py:457
  139.7 15.3 %slice-start = ((s8[6291456]{0:T(1024)(128)(4,1)}), s8[4194304]{0:T(1024)(128)(4,1)S(1)}, s32[]{:S(2)}) async-start(s8[6291456]{0:T(1024)(128)(4,1)} %bitcast.24), calls=%async_computation.1 | async-start | bytes 8388608
  143.5 11.5 %slice-start.1 = ((s8[6291456]{0:T(1024)(128)(4,1)}), s8[2097152]{0:T(1024)(128)(4,1)S(1)}, s32[]{:S(2)}) async-start(s8[6291456]{0:T(1024)(128)(4,1)} %bitcast.24), calls=%async_computation.2 | async-start | bytes 4194304
  143.5 6.9 %collective-permute-start.13 = (bf16[2,128,1536]{2,1,0:T(8,128)(2,1)S(1)}, bf16[2,128,1536]{2,1,0:T(8,128)(2,1)S(1)}, u32[]{:S(2)}, u32[]{:S(2)}) collective-permute-start(bf16[2,128,1536]{2,1,0:T(8,128)(2,1)S(1)} %get-tuple-element.50.refs_8_), channel_id=1, source_target_pairs={{0,2},{2,0},{4,6},{6,4},{8,10},{10,8},{12,14},{14,12},{16,18},{18,... | collective-permute-start | bytes 2359304 | tf_op jit(solution)/shard_map/ppermute | solution.py:457
  150.7 13.9 %collective-permute-start.15 = (bf16[2,128,1536]{2,1,0:T(8,128)(2,1)S(1)}, bf16[2,128,1536]{2,1,0:T(8,128)(2,1)S(1)}, u32[]{:S(2)}, u32[]{:S(2)}) collective-permute-start(bf16[2,128,1536]{2,1,0:T(8,128)(2,1)S(1)} %shard_map.153.refs_4_.refs_0_.refs_2_), channel_id=1, source_target_pairs={{0,4},{6,2},{8,12},{14,10},{16,20},{22,18},{24,28},{30,26},{1,5},{... | collective-permute-start | bytes 2359304 | tf_op jit(solution)/shard_map/ppermute | solution.py:457
  153.0 18.1 %collective-permute-start.14 = (bf16[2,128,1536]{2,1,0:T(8,128)(2,1)S(1)}, bf16[2,128,1536]{2,1,0:T(8,128)(2,1)S(1)}, u32[]{:S(2)}, u32[]{:S(2)}) collective-permute-start(bf16[2,128,1536]{2,1,0:T(8,128)(2,1)S(1)} %shard_map.155.refs_0_), channel_id=1, source_target_pairs={{10,2},{12,4},{18,26},{20,28},{11,3},{13,5},{19,27},{21,29}} | collective-permute-start | bytes 2359304 | tf_op jit(solution)/shard_map/ppermute | solution.py:457
  154.3 29.0 %collective-permute-start.16 = (bf16[1,128,1536]{2,1,0:T(8,128)(2,1)S(1)}, bf16[1,128,1536]{2,1,0:T(8,128)(2,1)S(1)}, u32[]{:S(2)}, u32[]{:S(2)}) collective-permute-start(bf16[1,128,1536]{2,1,0:T(8,128)(2,1)S(1)} %get-tuple-element.55.refs_2_), channel_id=1, source_target_pairs={{0,16},{6,22},{8,24},{14,30},{16,0},{22,6},{24,8},{30,14},{1,17},{... | collective-permute-start | bytes 1179656 | tf_op jit(solution)/shard_map/ppermute | solution.py:457
  165.3 21.0 %collective-permute-start.18 = (bf16[1,128,1536]{2,1,0:T(8,128)(2,1)S(1)}, bf16[1,128,1536]{2,1,0:T(8,128)(2,1)S(1)}, u32[]{:S(2)}, u32[]{:S(2)}) collective-permute-start(bf16[1,128,1536]{2,1,0:T(8,128)(2,1)S(1)} %get-tuple-element.58.refs_6_), channel_id=1, source_target_pairs={{2,18},{4,20},{26,10},{28,12},{3,19},{5,21},{27,11},{29,13}} | collective-permute-start | bytes 1179656 | tf_op jit(solution)/shard_map/ppermute | solution.py:457
  169.9 16.4 %collective-permute-start.19 = (bf16[1,128,1536]{2,1,0:T(8,128)(2,1)S(1)}, bf16[1,128,1536]{2,1,0:T(8,128)(2,1)S(1)}, u32[]{:S(2)}, u32[]{:S(2)}) collective-permute-start(bf16[1,128,1536]{2,1,0:T(8,128)(2,1)S(1)} %get-tuple-element.58.refs_6_), channel_id=1, source_target_pairs={{10,18},{12,20},{18,10},{20,12},{11,19},{13,21},{19,11},{21,13}} | collective-permute-start | bytes 1179656 | tf_op jit(solution)/shard_map/ppermute | solution.py:457
  171.9 14.4 %collective-permute-start.17 = (bf16[1,128,1536]{2,1,0:T(8,128)(2,1)S(1)}, bf16[1,128,1536]{2,1,0:T(8,128)(2,1)S(1)}, u32[]{:S(2)}, u32[]{:S(2)}) collective-permute-start(bf16[1,128,1536]{2,1,0:T(8,128)(2,1)S(1)} %get-tuple-element.59.refs_1_), channel_id=1, source_target_pairs={{2,26},{4,28},{26,2},{28,4},{3,27},{5,29},{27,3},{29,5}} | collective-permute-start | bytes 1179656 | tf_op jit(solution)/shard_map/ppermute | solution.py:457
  176.7 9.5 %collective-permute-start.20 = (bf16[1,128,1536]{2,1,0:T(8,128)(2,1)S(1)}, bf16[1,128,1536]{2,1,0:T(8,128)(2,1)S(1)}, u32[]{:S(2)}, u32[]{:S(2)}) collective-permute-start(bf16[1,128,1536]{2,1,0:T(8,128)(2,1)S(1)} %get-tuple-element.66), channel_id=1, source_target_pairs={{2,10},{4,12},{26,18},{28,20},{3,11},{5,13},{27,19},{29,21}} | collective-permute-start | bytes 1179656 | tf_op jit(solution)/shard_map/ppermute | solution.py:457
  (9 other events, 19.5 us)
Sparse Core Ops, SparseCore 0:
  10.3 62.1 all-gather.1

commit v3 on v1

--- a/solution.py
+++ b/solution.py
@@ -348,7 +348,7 @@
     def kernel(place_ref, *refs):
         alike = place_ref[CORE] == place_ref[X]
         outer = place_ref[LOW] == place_ref[HIGH]
-        owned = (alike, ~alike & outer, ~alike & ~outer)
+        owned = (alike, ~alike & ~outer, ~alike & outer)
         at = 0
         for batch, mine in zip(batches, owned):
             chosen = refs[at : at + len(batch)]
@@ -467,7 +467,7 @@
     place = lax.optimization_barrier(place.astype(jnp.int32))
     local_heads = HEADS // 2
     swap = [(0, 1), (1, 0)]
-    calls = [(0, 0, 4), (3, 0, 4), (1, 4, 1), (5, -4, 1)]
+    calls = [(0, 0, 4), (3, 0, 4), (5, -4, 1), (1, 4, 1)]
     bias = window_bias(windows)
     weight = lax.all_gather(out_weight, "dp", axis=0, tiled=True)
     gate_row = gate_scale[0].astype(jnp.float32)
@@ -540,13 +540,13 @@
     kept_a, sent_a = level_step(place, HIGH, [kept_a, low_a], (total_c,))
     high_a = dp_send(sent_a, 8, same_bits)
     sent_b = total_step([total_b, across_b], (sent_a,))
-    low_b = dp_send(sent_b, 4, inner)
+    low_b = dp_send(sent_b, 4, outer)
     gate = gate_row[None]
     out, done = project(columns, weight, gate, range(3), (), (sent_b,))
     kept_c, near_c, far_c = reach_step(place, [total_c, across_c], (done,))
-    reached_c = dp_send(far_c, 8, outer), dp_send(far_c, 12, inner), dp_send(near_c, 4, outer)
+    reached_c = dp_send(far_c, 8, inner), dp_send(far_c, 12, outer), dp_send(near_c, 4, inner)
     kept_b, sent_b = level_step(place, HIGH, [total_b, across_b, low_b], (near_c,))
-    high_b = dp_send(sent_b, 12, outer)
+    high_b = dp_send(sent_b, 12, inner)
     last = range(3, PROJECT_STEPS)
     block_out, done = project(columns, weight, gate, last, (out,), (sent_b,), LONG_COST)
     final_a = total_step([kept_a, high_a], (done,), jnp.float32)

time: 195 us -> 193 us (0.990)
  transfers between devices with their start and end apart: 22 -> 22, of which waited for: 12 -> 13; matrix products, arithmetic and copies ran while one was open for 2% -> 2% of each run, Pallas kernels for 39% -> 40%
where the time goes in v3:
time: 193 us
  Pallas kernels  78 us (40%)
  waiting for transfers between devices  59.8 us (31%)
  starting transfers between devices  30 us (16%)
  between operations  15 us (8%)
  local copies, waits for them, and re-layouts  6.27 us (3%)
  other arithmetic  3.61 us (2%)
    ppermute x8, waiting for transfers between devices, exchange(): return lax.ppermute(mine, 'seq', swap)  47.8 us
    pallas_call x4, Pallas kernels, attend_pair(): pl.pallas_call(pair_kernel, grid_spec=pltpu.PrefetchScalarGridSpec(num_sc...  29.9 us
    ppermute x13, starting transfers between devices, dp_send(): lax.ppermute(value, 'dp', [(i, i ^ flip) for i in range(HEADS) if sender(...  19.7 us
    pallas_call x3, Pallas kernels, batch_gradient(): pl.pallas_call(functools.partial(gradient_kernel, by_call=by_call), grid_...  17.2 us
    ppermute x13, waiting for transfers between devices, dp_send(): lax.ppermute(value, 'dp', [(i, i ^ flip) for i in range(HEADS) if sender(...  11.4 us
    pallas_call x2, Pallas kernels, project(): pl.pallas_call(kernel, grid=(steps,), in_specs=[pl.BlockSpec((rows, depth...  10.5 us
    ppermute x8, starting transfers between devices, exchange(): return lax.ppermute(mine, 'seq', swap)  10.3 us
    pallas_call x4, Pallas kernels, pack_partner(): pl.pallas_call(pack_kernel, grid_spec=pltpu.PrefetchScalarGridSpec(num_sc...  7.59 us
  transfers between devices with their start and end apart: 22, of which 13 were waited for; matrix products, arithmetic and copies ran while one was open for 2% of the time, Pallas kernels for 40%

profile of v3, /device:TPU:2, one launch (start us, length us, event | category | flops | bytes accessed | tf_op | source)
XLA Modules:
  0.0 192.8 jit_solution(15141126517120406196)
XLA Ops:
  8.0 2.6 %shard_map.140.rest_0_ = bf16[3,576,256]{2,1,0:T(8,128)(2,1)} custom-call(s32[5]{0:T(128)S(1)} %stack.23.place_ref, bf16[576,2048]{1,0:T(8,128)(2,1)} %q_ref.15, bf16[576,2048]{1,0:T(8,128)(2,1)} %k_ref.15, bf16[576,2048]{1,0:T(8,128)(2,1)} %v_ref.15), custom_call_target="tpu_custom_call" | custom-call | flops 1 | bytes 1 | tf_op jit(solution)/shard_map/pallas_call | solution.py:186
  12.1 2.7 %shard_map.141.rest_0_ = bf16[3,576,256]{2,1,0:T(8,128)(2,1)} custom-call(s32[5]{0:T(128)S(1)} %stack.23.place_ref, bf16[576,2048]{1,0:T(8,128)(2,1)} %q_ref.15, bf16[576,2048]{1,0:T(8,128)(2,1)} %k_ref.15, bf16[576,2048]{1,0:T(8,128)(2,1)} %v_ref.15, bf16[3,576,256]{2,1,0:T(8,128)(2,1)} %shard_map.140.rest_0_), custom_call_target="tpu_custom_call" | custom-call | flops 1 | bytes 1 | tf_op jit(solution)/shard_map/pallas_call | solution.py:186
  15.4 1.7 copy-done.1
  17.0 1.7 copy-done.2
  21.1 1.6 collective-permute-start.5
  23.7 9.7 %collective-permute-done.1.other_ref = bf16[3,576,256]{2,1,0:T(8,128)(2,1)S(1)} collective-permute-done((bf16[3,576,256]{2,1,0:T(8,128)(2,1)}, bf16[3,576,256]{2,1,0:T(8,128)(2,1)S(1)}, u32[]{:S(2)}, u32[]{:S(2)}) %collective-permute-start.1) | collective-permute-done | bytes 884768 | tf_op jit(solution)/shard_map/ppermute | solution.py:484
  33.4 7.3 %shard_map.143.rest_0_.refs_0_ = bf16[1152,256]{1,0:T(8,128)(2,1)} custom-call(s32[5]{0:T(128)S(1)} %stack.23.place_ref, bf16[576,2048]{1,0:T(8,128)(2,1)S(1)} %copy-done, bf16[576,2048]{1,0:T(8,128)(2,1)S(1)} %copy-done.1, bf16[576,2048]{1,0:T(8,128)(2,1)S(1)} %copy-done.2, bf16[3,576,256]{2,1,0:T(8,128)(2,1)S(1)} %collective-permute-done.1.other_ref, ...), custom_call_target="tpu_custom_call" | custom-call | flops 1 | bytes 1 | tf_op jit(solution)/shard_map/pallas_call | solution.py:117
  40.6 11.7 %collective-permute-done.3.other_ref = bf16[3,576,256]{2,1,0:T(8,128)(2,1)S(1)} collective-permute-done((bf16[3,576,256]{2,1,0:T(8,128)(2,1)}, bf16[3,576,256]{2,1,0:T(8,128)(2,1)S(1)}, u32[]{:S(2)}, u32[]{:S(2)}) %collective-permute-start.3) | collective-permute-done | bytes 884768 | tf_op jit(solution)/shard_map/ppermute | solution.py:484
  52.3 7.3 %shard_map.144.rest_0_.refs_2_ = bf16[1152,256]{1,0:T(8,128)(2,1)} custom-call(s32[5]{0:T(128)S(1)} %stack.23.place_ref, bf16[576,2048]{1,0:T(8,128)(2,1)S(1)} %copy-done, bf16[576,2048]{1,0:T(8,128)(2,1)S(1)} %copy-done.1, bf16[576,2048]{1,0:T(8,128)(2,1)S(1)} %copy-done.2, bf16[3,576,256]{2,1,0:T(8,128)(2,1)S(1)} %collective-permute-done.3.other_ref, ...), custom_call_target="tpu_custom_call" | custom-call | flops 1 | bytes 1 | tf_op jit(solution)/shard_map/pallas_call | solution.py:117
  64.4 6.9 %collective-permute-done.5.other_ref = bf16[3,576,256]{2,1,0:T(8,128)(2,1)S(1)} collective-permute-done((bf16[3,576,256]{2,1,0:T(8,128)(2,1)S(1)}, bf16[3,576,256]{2,1,0:T(8,128)(2,1)S(1)}, u32[]{:S(2)}, u32[]{:S(2)}) %collective-permute-start.5) | collective-permute-done | bytes 884768 | tf_op jit(solution)/shard_map/ppermute | solution.py:484
  71.3 7.3 %shard_map.146.refs_0_.refs_4_ = bf16[1152,256]{1,0:T(8,128)(2,1)} custom-call(s32[5]{0:T(128)S(1)} %stack.23.place_ref, bf16[576,2048]{1,0:T(8,128)(2,1)S(1)} %copy-done, bf16[576,2048]{1,0:T(8,128)(2,1)S(1)} %copy-done.1, bf16[576,2048]{1,0:T(8,128)(2,1)S(1)} %copy-done.2, bf16[3,576,256]{2,1,0:T(8,128)(2,1)S(1)} %collective-permute-done.5.other_ref, ...), custom_call_target="tpu_custom_call" | custom-call | flops 1 | bytes 1 | tf_op jit(solution)/shard_map/pallas_call | solution.py:117
  80.1 2.6 %multiply_convert_fusion.refs_2_ = bf16[1152,1536]{1,0:T(8,128)(2,1)} fusion(bf16[1152,1536]{1,0:T(8,128)(2,1)S(1)} %copy-done.8, f32[1536]{0:T(1024)S(1)} %convert_reduce_fusion), kind=kLoop, calls=%fused_computation | loop fusion | flops 5308416 | bytes 7084032 | tf_op jit(solution)/shard_map/convert_element_type | solution.py:474
  84.0 12.6 %collective-permute-done.2.refs_1_ = bf16[1152,256]{1,0:T(8,128)(2,1)} collective-permute-done((bf16[1152,256]{1,0:T(8,128)(2,1)}, bf16[1152,256]{1,0:T(8,128)(2,1)}, u32[]{:S(2)}, u32[]{:S(2)}) %collective-permute-start.2) | collective-permute-done | bytes 589856 | tf_op jit(solution)/shard_map/ppermute | solution.py:484
  96.7 13.3 %conditional.1 = (bf16[4,128,1536]{2,1,0:T(8,128)(2,1)}) conditional(s32[]{:T(128)} %bitcast.14, () %tuple.15, (s32[5]{0:T(128)S(1)}, bf16[1152,256]{1,0:T(8,128)(2,1)}, bf16[1152,256]{1,0:T(8,128)(2,1)}, bf16[1152,256]{1,0:T(8,128)(2,1)}, bf16[1152,256]{1,0:T(8,128)(2,1)}, /*index=5*/bf16[1152,1536]{1,0:T(8,128)(2,1)}) %tuple.17), branch_computations={%region_0.1_spmd, %region_1.2_spmd} | conditional | flops 2 | bytes 6291506 | solution.py:492
  96.7 8.0 %branch_1_fun.2 = (bf16[4,128,1536]{2,1,0:T(8,128)(2,1)S(1)}, bf16[4,128,1536]{2,1,0:T(8,128)(2,1)S(1)}) custom-call(s32[5]{0:T(128)S(1)} %get-tuple-element.5.place_ref, bf16[1152,256]{1,0:T(8,128)(2,1)} %get-tuple-element.16.refs_0_, bf16[1152,256]{1,0:T(8,128)(2,1)} %get-tuple-element.17.refs_1_, bf16[1152,256]{1,0:T(8,128)(2,1)} %get-tuple-element.18.refs_2_, ...), custom_call_target="tpu_custom_call" | custom-call | flops 1 | bytes 1 | tf_op jit(solution)/shard_map/cond/branch_1_fun/pallas_call | solution.py:239
  104.8 3.4 %collective-permute-done.refs_1_ = bf16[4,128,1536]{2,1,0:T(8,128)(2,1)S(1)} collective-permute-done((bf16[4,128,1536]{2,1,0:T(8,128)(2,1)S(1)}, bf16[4,128,1536]{2,1,0:T(8,128)(2,1)S(1)}, u32[]{:S(2)}, u32[]{:S(2)}) %collective-permute-start) | collective-permute-done | bytes 1572896 | tf_op jit(solution)/shard_map/cond/branch_1_fun/ppermute | solution.py:457
  108.1 1.9 branch_1_fun.3
  110.0 2.0 %collective-permute-start.10 = (bf16[4,128,1536]{2,1,0:T(8,128)(2,1)}, bf16[4,128,1536]{2,1,0:T(8,128)(2,1)S(1)}, u32[]{:S(2)}, u32[]{:S(2)}) collective-permute-start(bf16[4,128,1536]{2,1,0:T(8,128)(2,1)} %get-tuple-element.82.rest_0_.refs_0_.refs_2_), channel_id=1, source_target_pairs={{2,6},{4,0},{10,14},{12,8},{18,22},{20,16},{26,30},{28,24},{3,7},{... | collective-permute-start | bytes 4718600 | tf_op jit(solution)/shard_map/ppermute | solution.py:457
  112.0 3.6 %collective-permute-done.7.other_ref = bf16[3,576,256]{2,1,0:T(8,128)(2,1)} collective-permute-done((bf16[3,576,256]{2,1,0:T(8,128)(2,1)S(1)}, bf16[3,576,256]{2,1,0:T(8,128)(2,1)}, u32[]{:S(2)}, u32[]{:S(2)}) %collective-permute-start.7) | collective-permute-done | bytes 884768 | tf_op jit(solution)/shard_map/ppermute | solution.py:484
  115.6 8.1 %shard_map.147.refs_3_.refs_0_.refs_6_ = bf16[1152,256]{1,0:T(8,128)(2,1)} custom-call(s32[5]{0:T(128)S(1)} %stack.23.place_ref, bf16[576,2048]{1,0:T(8,128)(2,1)} %q_ref.15, bf16[576,2048]{1,0:T(8,128)(2,1)} %k_ref.15, bf16[576,2048]{1,0:T(8,128)(2,1)} %v_ref.15, bf16[3,576,256]{2,1,0:T(8,128)(2,1)} %collective-permute-done.7.other_ref, ...), custom_call_target="tpu_custom_call" | custom-call | flops 1 | bytes 1 | tf_op jit(solution)/shard_map/pallas_call | solution.py:117
  125.2 2.9 %collective-permute-done.6.refs_1_.refs_5_ = bf16[1152,256]{1,0:T(8,128)(2,1)S(1)} collective-permute-done((bf16[1152,256]{1,0:T(8,128)(2,1)}, bf16[1152,256]{1,0:T(8,128)(2,1)S(1)}, u32[]{:S(2)}, u32[]{:S(2)}) %collective-permute-start.6) | collective-permute-done | bytes 589856 | tf_op jit(solution)/shard_map/ppermute | solution.py:484
  129.2 5.4 %shard_map.148 = (bf16[2,128,1536]{2,1,0:T(8,128)(2,1)S(1)}, bf16[2,128,1536]{2,1,0:T(8,128)(2,1)S(1)}) custom-call(s32[5]{0:T(128)S(1)} %stack.23.place_ref, bf16[1152,256]{1,0:T(8,128)(2,1)} %shard_map.146.refs_0_.refs_4_, bf16[1152,256]{1,0:T(8,128)(2,1)S(1)} %collective-permute-done.6.refs_1_.refs_5_, bf16[1152,1536]{1,0:T(8,128)(2,1)} %multiply_convert_fusion.refs_2_, ...), custom_call_target="tpu_custom_call" | custom-call | flops 20000000000 | bytes 20000000 | tf_op jit(solution)/shard_map/pallas_call | solution.py:239
  134.7 2.4 %shard_map.149 = (f32[2,128,1536]{2,1,0:T(8,128)S(1)}, bf16[2,128,1536]{2,1,0:T(8,128)(2,1)S(1)}) custom-call(s32[5]{0:T(128)S(1)} %stack.23.place_ref, bf16[4,128,1536]{2,1,0:T(8,128)(2,1)} %get-tuple-element.82.rest_0_.refs_0_.refs_2_, bf16[4,128,1536]{2,1,0:T(8,128)(2,1)S(1)} %collective-permute-done.10.refs_1_.refs_3_, ...), custom_call_target="tpu_custom_call" | custom-call | flops 20000000000 | bytes 20000000 | tf_op jit(solution)/shard_map/pallas_call | solution.py:277
  139.7 3.8 %shard_map.151 = (bf16[2,128,1536]{2,1,0:T(8,128)(2,1)S(1)}, bf16[2,128,1536]{2,1,0:T(8,128)(2,1)S(1)}) custom-call(s32[5]{0:T(128)S(1)} %stack.23.place_ref, bf16[1152,256]{1,0:T(8,128)(2,1)S(1)} %copy-done.6, bf16[1152,256]{1,0:T(8,128)(2,1)S(1)} %collective-permute-done.8.refs_1_.refs_7_, bf16[1152,1536]{1,0:T(8,128)(2,1)S(1)} %copy-done.7, ...), custom_call_target="tpu_custom_call" | custom-call | flops 1 | bytes 1 | tf_op jit(solution)/shard_map/pallas_call | solution.py:239
  143.5 3.0 %collective-permute-start.13 = (bf16[2,128,1536]{2,1,0:T(8,128)(2,1)S(1)}, bf16[2,128,1536]{2,1,0:T(8,128)(2,1)S(1)}, u32[]{:S(2)}, u32[]{:S(2)}) collective-permute-start(bf16[2,128,1536]{2,1,0:T(8,128)(2,1)S(1)} %get-tuple-element.49.refs_8_), channel_id=1, source_target_pairs={{0,2},{2,0},{4,6},{6,4},{8,10},{10,8},{12,14},{14,12},{16,18},{18,... | collective-permute-start | bytes 2359304 | tf_op jit(solution)/shard_map/ppermute | solution.py:457
  146.5 4.0 %shard_map.152 = (bf16[1152,2048]{1,0:T(8,128)(2,1)S(1)}, f32[8,128]{1,0:T(8,128)S(1)}) custom-call(s32[5]{0:T(128)S(1)} %stack.23.place_ref, bf16[1152,256]{1,0:T(8,128)(2,1)} %shard_map.143.rest_0_.refs_0_, bf16[1152,256]{1,0:T(8,128)(2,1)} %collective-permute-done.2.refs_1_, bf16[1152,256]{1,0:T(8,128)(2,1)} %shard_map.144.rest_0_.refs_2_, ...), custom_call_target="tpu_custom_call" | custom-call | flops 20000000000 | bytes 20000000 | tf_op jit(solution)/shard_map/pallas_call | solution.py:390
  153.0 2.9 %collective-permute-start.14 = (bf16[2,128,1536]{2,1,0:T(8,128)(2,1)S(1)}, bf16[2,128,1536]{2,1,0:T(8,128)(2,1)S(1)}, u32[]{:S(2)}, u32[]{:S(2)}) collective-permute-start(bf16[2,128,1536]{2,1,0:T(8,128)(2,1)S(1)} %shard_map.155.refs_0_), channel_id=1, source_target_pairs={{2,10},{4,12},{26,18},{28,20},{3,11},{5,13},{27,19},{29,21}} | collective-permute-start | bytes 2359304 | tf_op jit(solution)/shard_map/ppermute | solution.py:457
  156.6 5.3 %shard_map.156 = (bf16[1152,1536]{1,0:T(8,128)(2,1)}, f32[8,128]{1,0:T(8,128)S(1)}) custom-call(bf16[1152,2048]{1,0:T(8,128)(2,1)S(1)} %get-tuple-element.50.attention_ref, bf16[2048,1536]{1,0:T(8,128)(2,1)S(1)} %bitcast.25, f32[1,1536]{1,0:T(1,128)S(1)} %convert_element_type.19.gate_ref, bf16[2,128,1536]{2,1,0:T(8,128)(2,1)S(1)} %shard_map.155.refs_0_), custom_call_target="tpu_custom_call" | custom-call | flops 1 | bytes 1 | tf_op jit(solution)/shard_map/pallas_call | solution.py:423
  161.8 2.7 %collective-permute-done.15.refs_1_.refs_3_ = bf16[2,128,1536]{2,1,0:T(8,128)(2,1)S(1)} collective-permute-done((bf16[2,128,1536]{2,1,0:T(8,128)(2,1)S(1)}, bf16[2,128,1536]{2,1,0:T(8,128)(2,1)S(1)}, u32[]{:S(2)}, u32[]{:S(2)}) %collective-permute-start.15) | collective-permute-done | bytes 786464 | tf_op jit(solution)/shard_map/ppermute | solution.py:457
  166.6 4.4 %collective-permute-start.19 = (bf16[1,128,1536]{2,1,0:T(8,128)(2,1)S(1)}, bf16[1,128,1536]{2,1,0:T(8,128)(2,1)S(1)}, u32[]{:S(2)}, u32[]{:S(2)}) collective-permute-start(bf16[1,128,1536]{2,1,0:T(8,128)(2,1)S(1)} %get-tuple-element.64), channel_id=1, source_target_pairs={{2,26},{4,28},{26,2},{28,4},{3,27},{5,29},{27,3},{29,5}} | collective-permute-start | bytes 1179656 | tf_op jit(solution)/shard_map/ppermute | solution.py:457
  173.9 5.3 %shard_map.159 = (bf16[1152,1536]{1,0:T(8,128)(2,1)}, f32[8,128]{1,0:T(8,128)S(1)}) custom-call(bf16[1152,2048]{1,0:T(8,128)(2,1)S(1)} %get-tuple-element.50.attention_ref, bf16[2048,1536]{1,0:T(8,128)(2,1)S(1)} %bitcast.25, f32[1,1536]{1,0:T(1,128)S(1)} %convert_element_type.19.gate_ref, ...), custom_call_target="tpu_custom_call", output_to_operand_aliasing={{0}: (3, {})} | custom-call | flops 20000000000 | bytes 20000000 | tf_op jit(solution)/shard_map/pallas_call | solution.py:423
  180.2 4.1 %collective-permute-done.20.refs_6_ = bf16[1,128,1536]{2,1,0:T(8,128)(2,1)S(1)} collective-permute-done((bf16[1,128,1536]{2,1,0:T(8,128)(2,1)S(1)}, bf16[1,128,1536]{2,1,0:T(8,128)(2,1)S(1)}, u32[]{:S(2)}, u32[]{:S(2)}) %collective-permute-start.20) | collective-permute-done | bytes 393248 | tf_op jit(solution)/shard_map/ppermute | solution.py:457
  (86 shorter events, 29.1 us)
Async XLA Ops:
  7.2 76.7 %all-gather.2.cloned.1.call-start = ((), (), s32[]{:S(2)}) async-start(), calls=%async_computation | async-start | bytes 6684672 | tf_op jit(solution)/shard_map/all_gather | solution.py:472
  10.6 4.7 %copy-start = (bf16[576,2048]{1,0:T(8,128)(2,1)S(1)}, bf16[576,2048]{1,0:T(8,128)(2,1)}, u32[]{:S(2)}) copy-start(bf16[576,2048]{1,0:T(8,128)(2,1)} %q_ref.15) | copy-start | bytes 7077892
  10.6 22.7 %collective-permute-start.1 = (bf16[3,576,256]{2,1,0:T(8,128)(2,1)}, bf16[3,576,256]{2,1,0:T(8,128)(2,1)S(1)}, u32[]{:S(2)}, u32[]{:S(2)}) collective-permute-start(bf16[3,576,256]{2,1,0:T(8,128)(2,1)} %shard_map.140.rest_0_), channel_id=1, source_target_pairs={{0,1},{1,0},{2,3},{3,2},{4,5},{5,4},{6,7},{7,6},{8,9},{9,8},{10,11... | collective-permute-start | bytes 2654216 | tf_op jit(solution)/shard_map/ppermute | solution.py:484
  14.9 37.5 %collective-permute-start.3 = (bf16[3,576,256]{2,1,0:T(8,128)(2,1)}, bf16[3,576,256]{2,1,0:T(8,128)(2,1)S(1)}, u32[]{:S(2)}, u32[]{:S(2)}) collective-permute-start(bf16[3,576,256]{2,1,0:T(8,128)(2,1)} %shard_map.141.rest_0_), channel_id=1, source_target_pairs={{0,1},{1,0},{2,3},{3,2},{4,5},{5,4},{6,7},{7,6},{8,9},{9,8},{10,11... | collective-permute-start | bytes 2654216 | tf_op jit(solution)/shard_map/ppermute | solution.py:484
  19.9 3.0 %copy-start.10 = (s32[1152]{0:T(1024)S(1)}, s32[1152]{0:T(1024)}, u32[]{:S(2)}) copy-start(s32[1152]{0:T(1024)} %constant.80) | copy-start | bytes 13828
  19.9 3.0 %copy-start.11 = (s32[1152]{0:T(1024)S(1)}, s32[1152]{0:T(1024)}, u32[]{:S(2)}) copy-start(s32[1152]{0:T(1024)} %constant.82) | copy-start | bytes 13828
  19.9 3.0 %copy-start.12 = (s32[1152]{0:T(1024)S(1)}, s32[1152]{0:T(1024)}, u32[]{:S(2)}) copy-start(s32[1152]{0:T(1024)} %constant.84) | copy-start | bytes 13828
  21.1 50.2 %collective-permute-start.5 = (bf16[3,576,256]{2,1,0:T(8,128)(2,1)S(1)}, bf16[3,576,256]{2,1,0:T(8,128)(2,1)S(1)}, u32[]{:S(2)}, u32[]{:S(2)}) collective-permute-start(bf16[3,576,256]{2,1,0:T(8,128)(2,1)S(1)} %shard_map.142.rest_0_), channel_id=1, source_target_pairs={{0,1},{1,0},{2,3},{3,2},{4,5},{5,4},{6,7},{7,6},{8,9},{9,8},{10,11... | collective-permute-start | bytes 2654216 | tf_op jit(solution)/shard_map/ppermute | solution.py:484
  23.7 47.6 %copy-start.3 = (f32[16,24,1152]{2,1,0:T(8,128)}, f32[16,24,1152]{2,1,0:T(8,128)S(1)}, u32[]{:S(2)}) copy-start(f32[16,24,1152]{2,1,0:T(8,128)S(1)} %and_select_fusion.bias_ref) | copy-start | bytes 5308420
  40.6 19.0 %copy-start.9 = (bf16[1,1536]{1,0:T(2,128)(2,1)S(1)}, bf16[1,1536]{1,0:T(2,128)(2,1)}, u32[]{:S(2)}) copy-start(bf16[1,1536]{1,0:T(2,128)(2,1)} %param.20) | copy-start | bytes 9220
  60.8 23.3 %collective-permute-start.4 = (bf16[1152,256]{1,0:T(8,128)(2,1)}, bf16[1152,256]{1,0:T(8,128)(2,1)}, u32[]{:S(2)}, u32[]{:S(2)}) collective-permute-start(bf16[1152,256]{1,0:T(8,128)(2,1)} %shard_map.144.rest_0_.refs_2_), channel_id=1, source_target_pairs={{0,1},{1,0},{2,3},{3,2},{4,5},{5,4},{6,7},{7,6},{8,9},{9,8},{10,11... | collective-permute-start | bytes 1769480 | tf_op jit(solution)/shard_map/ppermute | solution.py:484
  62.4 34.3 %collective-permute-start.2 = (bf16[1152,256]{1,0:T(8,128)(2,1)}, bf16[1152,256]{1,0:T(8,128)(2,1)}, u32[]{:S(2)}, u32[]{:S(2)}) collective-permute-start(bf16[1152,256]{1,0:T(8,128)(2,1)} %shard_map.143.rest_0_.refs_0_), channel_id=1, source_target_pairs={{0,1},{1,0},{2,3},{3,2},{4,5},{5,4},{6,7},{7,6},{8,9},{9,8},{10,11... | collective-permute-start | bytes 1769480 | tf_op jit(solution)/shard_map/ppermute | solution.py:484
  62.9 52.8 %collective-permute-start.7 = (bf16[3,576,256]{2,1,0:T(8,128)(2,1)S(1)}, bf16[3,576,256]{2,1,0:T(8,128)(2,1)}, u32[]{:S(2)}, u32[]{:S(2)}) collective-permute-start(bf16[3,576,256]{2,1,0:T(8,128)(2,1)S(1)} %shard_map.145.rest_1_), channel_id=1, source_target_pairs={{0,1},{1,0},{2,3},{3,2},{4,5},{5,4},{6,7},{7,6},{8,9},{9,8},{10,11... | collective-permute-start | bytes 2654216 | tf_op jit(solution)/shard_map/ppermute | solution.py:484
  71.3 8.8 %copy-start.8 = (bf16[1152,1536]{1,0:T(8,128)(2,1)S(1)}, bf16[1152,1536]{1,0:T(8,128)(2,1)}, u32[]{:S(2)}) copy-start(bf16[1152,1536]{1,0:T(8,128)(2,1)} %param.21) | copy-start | bytes 10616836
  78.6 49.6 %collective-permute-start.6 = (bf16[1152,256]{1,0:T(8,128)(2,1)}, bf16[1152,256]{1,0:T(8,128)(2,1)S(1)}, u32[]{:S(2)}, u32[]{:S(2)}) collective-permute-start(bf16[1152,256]{1,0:T(8,128)(2,1)} %shard_map.146.refs_0_.refs_4_), channel_id=1, source_target_pairs={{0,1},{1,0},{2,3},{3,2},{4,5},{5,4},{6,7},{7,6},{8,9},{9,8},{10,11... | collective-permute-start | bytes 1769480 | tf_op jit(solution)/shard_map/ppermute | solution.py:484
  104.7 3.5 %collective-permute-start = (bf16[4,128,1536]{2,1,0:T(8,128)(2,1)S(1)}, bf16[4,128,1536]{2,1,0:T(8,128)(2,1)S(1)}, u32[]{:S(2)}, u32[]{:S(2)}) collective-permute-start(bf16[4,128,1536]{2,1,0:T(8,128)(2,1)S(1)} %get-tuple-element.22), channel_id=1, source_target_pairs={{0,2},{2,0},{4,6},{6,4},{8,10},{10,8},{12,14},{14,12},{16,18},{18,... | collective-permute-start | bytes 4718600 | tf_op jit(solution)/shard_map/cond/branch_1_fun/ppermute | solution.py:457
  110.0 24.7 %collective-permute-start.10 = (bf16[4,128,1536]{2,1,0:T(8,128)(2,1)}, bf16[4,128,1536]{2,1,0:T(8,128)(2,1)S(1)}, u32[]{:S(2)}, u32[]{:S(2)}) collective-permute-start(bf16[4,128,1536]{2,1,0:T(8,128)(2,1)} %get-tuple-element.82.rest_0_.refs_0_.refs_2_), channel_id=1, source_target_pairs={{2,6},{4,0},{10,14},{12,8},{18,22},{20,16},{26,30},{28,24},{3,7},{... | collective-permute-start | bytes 4718600 | tf_op jit(solution)/shard_map/ppermute | solution.py:457
  123.7 16.0 %collective-permute-start.8 = (bf16[1152,256]{1,0:T(8,128)(2,1)}, bf16[1152,256]{1,0:T(8,128)(2,1)S(1)}, u32[]{:S(2)}, u32[]{:S(2)}) collective-permute-start(bf16[1152,256]{1,0:T(8,128)(2,1)} %shard_map.147.refs_3_.refs_0_.refs_6_), channel_id=1, source_target_pairs={{0,1},{1,0},{2,3},{3,2},{4,5},{5,4},{6,7},{7,6},{8,9},{9,8},{10,11... | collective-permute-start | bytes 1769480 | tf_op jit(solution)/shard_map/ppermute | solution.py:484
  134.6 3.4 %collective-permute-start.9 = (bf16[2,128,1536]{2,1,0:T(8,128)(2,1)S(1)}, bf16[2,128,1536]{2,1,0:T(8,128)(2,1)S(1)}, u32[]{:S(2)}, u32[]{:S(2)}) collective-permute-start(bf16[2,128,1536]{2,1,0:T(8,128)(2,1)S(1)} %get-tuple-element.47.refs_4_), channel_id=1, source_target_pairs={{0,2},{2,0},{4,6},{6,4},{8,10},{10,8},{12,14},{14,12},{16,18},{18,... | collective-permute-start | bytes 2359304 | tf_op jit(solution)/shard_map/ppermute | solution.py:457
  134.7 5.0 %copy-start.7 = (bf16[1152,1536]{1,0:T(8,128)(2,1)S(1)}, bf16[1152,1536]{1,0:T(8,128)(2,1)}, u32[]{:S(2)}) copy-start(bf16[1152,1536]{1,0:T(8,128)(2,1)} %multiply_convert_fusion.refs_2_) | copy-start | bytes 10616836
  137.1 14.9 %collective-permute-start.12 = (bf16[2,128,1536]{2,1,0:T(8,128)(2,1)S(1)}, bf16[2,128,1536]{2,1,0:T(8,128)(2,1)S(1)}, u32[]{:S(2)}, u32[]{:S(2)}) collective-permute-start(bf16[2,128,1536]{2,1,0:T(8,128)(2,1)S(1)} %get-tuple-element.48.refs_2_), channel_id=1, source_target_pairs={{0,8},{6,14},{8,0},{14,6},{16,24},{22,30},{24,16},{30,22},{1,9},{7... | collective-permute-start | bytes 2359304 | tf_op jit(solution)/shard_map/ppermute | solution.py:457
  138.2 14.6 %collective-permute-start.11 = (bf16[2,128,1536]{2,1,0:T(8,128)(2,1)S(1)}, bf16[2,128,1536]{2,1,0:T(8,128)(2,1)S(1)}, u32[]{:S(2)}, u32[]{:S(2)}) collective-permute-start(bf16[2,128,1536]{2,1,0:T(8,128)(2,1)S(1)} %shard_map.150.refs_3_.refs_0_), channel_id=1, source_target_pairs={{0,4},{6,2},{8,12},{14,10},{16,20},{22,18},{24,28},{30,26},{1,5},{... | collective-permute-start | bytes 2359304 | tf_op jit(solution)/shard_map/ppermute | solution.py:457
  139.7 16.9 %slice-start = ((s8[6291456]{0:T(1024)(128)(4,1)}), s8[4194304]{0:T(1024)(128)(4,1)S(1)}, s32[]{:S(2)}) async-start(s8[6291456]{0:T(1024)(128)(4,1)} %bitcast.24), calls=%async_computation.1 | async-start | bytes 8388608
  143.5 13.1 %slice-start.1 = ((s8[6291456]{0:T(1024)(128)(4,1)}), s8[2097152]{0:T(1024)(128)(4,1)S(1)}, s32[]{:S(2)}) async-start(s8[6291456]{0:T(1024)(128)(4,1)} %bitcast.24), calls=%async_computation.2 | async-start | bytes 4194304
  143.5 6.9 %collective-permute-start.13 = (bf16[2,128,1536]{2,1,0:T(8,128)(2,1)S(1)}, bf16[2,128,1536]{2,1,0:T(8,128)(2,1)S(1)}, u32[]{:S(2)}, u32[]{:S(2)}) collective-permute-start(bf16[2,128,1536]{2,1,0:T(8,128)(2,1)S(1)} %get-tuple-element.49.refs_8_), channel_id=1, source_target_pairs={{0,2},{2,0},{4,6},{6,4},{8,10},{10,8},{12,14},{14,12},{16,18},{18,... | collective-permute-start | bytes 2359304 | tf_op jit(solution)/shard_map/ppermute | solution.py:457
  150.7 13.9 %collective-permute-start.15 = (bf16[2,128,1536]{2,1,0:T(8,128)(2,1)S(1)}, bf16[2,128,1536]{2,1,0:T(8,128)(2,1)S(1)}, u32[]{:S(2)}, u32[]{:S(2)}) collective-permute-start(bf16[2,128,1536]{2,1,0:T(8,128)(2,1)S(1)} %shard_map.153.refs_4_.refs_0_.refs_2_), channel_id=1, source_target_pairs={{0,4},{6,2},{8,12},{14,10},{16,20},{22,18},{24,28},{30,26},{1,5},{... | collective-permute-start | bytes 2359304 | tf_op jit(solution)/shard_map/ppermute | solution.py:457
  153.0 19.3 %collective-permute-start.14 = (bf16[2,128,1536]{2,1,0:T(8,128)(2,1)S(1)}, bf16[2,128,1536]{2,1,0:T(8,128)(2,1)S(1)}, u32[]{:S(2)}, u32[]{:S(2)}) collective-permute-start(bf16[2,128,1536]{2,1,0:T(8,128)(2,1)S(1)} %shard_map.155.refs_0_), channel_id=1, source_target_pairs={{2,10},{4,12},{26,18},{28,20},{3,11},{5,13},{27,19},{29,21}} | collective-permute-start | bytes 2359304 | tf_op jit(solution)/shard_map/ppermute | solution.py:457
  155.9 23.2 %collective-permute-start.16 = (bf16[1,128,1536]{2,1,0:T(8,128)(2,1)S(1)}, bf16[1,128,1536]{2,1,0:T(8,128)(2,1)S(1)}, u32[]{:S(2)}, u32[]{:S(2)}) collective-permute-start(bf16[1,128,1536]{2,1,0:T(8,128)(2,1)S(1)} %get-tuple-element.54.refs_2_), channel_id=1, source_target_pairs={{0,16},{6,22},{8,24},{14,30},{16,0},{22,6},{24,8},{30,14},{1,17},{... | collective-permute-start | bytes 1179656 | tf_op jit(solution)/shard_map/ppermute | solution.py:457
  165.3 14.9 %collective-permute-start.18 = (bf16[1,128,1536]{2,1,0:T(8,128)(2,1)S(1)}, bf16[1,128,1536]{2,1,0:T(8,128)(2,1)S(1)}, u32[]{:S(2)}, u32[]{:S(2)}) collective-permute-start(bf16[1,128,1536]{2,1,0:T(8,128)(2,1)S(1)} %get-tuple-element.64), channel_id=1, source_target_pairs={{10,26},{12,28},{18,2},{20,4},{11,27},{13,29},{19,3},{21,5}} | collective-permute-start | bytes 1179656 | tf_op jit(solution)/shard_map/ppermute | solution.py:457
  166.6 13.6 %collective-permute-start.19 = (bf16[1,128,1536]{2,1,0:T(8,128)(2,1)S(1)}, bf16[1,128,1536]{2,1,0:T(8,128)(2,1)S(1)}, u32[]{:S(2)}, u32[]{:S(2)}) collective-permute-start(bf16[1,128,1536]{2,1,0:T(8,128)(2,1)S(1)} %get-tuple-element.64), channel_id=1, source_target_pairs={{2,26},{4,28},{26,2},{28,4},{3,27},{5,29},{27,3},{29,5}} | collective-permute-start | bytes 1179656 | tf_op jit(solution)/shard_map/ppermute | solution.py:457
  171.0 13.3 %collective-permute-start.20 = (bf16[1,128,1536]{2,1,0:T(8,128)(2,1)S(1)}, bf16[1,128,1536]{2,1,0:T(8,128)(2,1)S(1)}, u32[]{:S(2)}, u32[]{:S(2)}) collective-permute-start(bf16[1,128,1536]{2,1,0:T(8,128)(2,1)S(1)} %get-tuple-element.57.refs_6_), channel_id=1, source_target_pairs={{10,2},{12,4},{18,26},{20,28},{11,3},{13,5},{19,27},{21,29}} | collective-permute-start | bytes 1179656 | tf_op jit(solution)/shard_map/ppermute | solution.py:457
  173.2 6.0 %collective-permute-start.17 = (bf16[1,128,1536]{2,1,0:T(8,128)(2,1)S(1)}, bf16[1,128,1536]{2,1,0:T(8,128)(2,1)S(1)}, u32[]{:S(2)}, u32[]{:S(2)}) collective-permute-start(bf16[1,128,1536]{2,1,0:T(8,128)(2,1)S(1)} %get-tuple-element.58.refs_1_), channel_id=1, source_target_pairs={{10,18},{12,20},{18,10},{20,12},{11,19},{13,21},{19,11},{21,13}} | collective-permute-start | bytes 1179656 | tf_op jit(solution)/shard_map/ppermute | solution.py:457
  (9 other events, 19.5 us)
Sparse Core Ops, SparseCore 0:
  10.3 62.1 all-gather.1

commit v4 on v3

--- a/solution.py
+++ b/solution.py
@@ -544,7 +544,7 @@
     gate = gate_row[None]
     out, done = project(columns, weight, gate, range(3), (), (sent_b,))
     kept_c, near_c, far_c = reach_step(place, [total_c, across_c], (done,))
-    reached_c = dp_send(far_c, 8, inner), dp_send(far_c, 12, outer), dp_send(near_c, 4, inner)
+    reached_c = dp_send(near_c, 4, inner), dp_send(far_c, 8, inner), dp_send(far_c, 12, outer)
     kept_b, sent_b = level_step(place, HIGH, [total_b, across_b, low_b], (near_c,))
     high_b = dp_send(sent_b, 12, inner)
     last = range(3, PROJECT_STEPS)

time: 193 us -> 193 us (level)
  transfers between devices with their start and end apart: 22 -> 22, of which waited for: 13 -> 12; matrix products, arithmetic and copies ran while one was open for 2% -> 2% of each run, Pallas kernels for 40% -> 40%
where the time goes in v4:
time: 193 us
  Pallas kernels  78 us (40%)
  waiting for transfers between devices  59.8 us (31%)
  starting transfers between devices  30 us (16%)
  between operations  15 us (8%)
  local copies, waits for them, and re-layouts  6.27 us (3%)
  other arithmetic  3.61 us (2%)
    ppermute x8, waiting for transfers between devices, exchange(): return lax.ppermute(mine, 'seq', swap)  47.8 us
    pallas_call x4, Pallas kernels, attend_pair(): pl.pallas_call(pair_kernel, grid_spec=pltpu.PrefetchScalarGridSpec(num_sc...  29.9 us
    ppermute x13, starting transfers between devices, dp_send(): lax.ppermute(value, 'dp', [(i, i ^ flip) for i in range(HEADS) if sender(...  19.7 us
    pallas_call x3, Pallas kernels, batch_gradient(): pl.pallas_call(functools.partial(gradient_kernel, by_call=by_call), grid_...  17.2 us
    ppermute x13, waiting for transfers between devices, dp_send(): lax.ppermute(value, 'dp', [(i, i ^ flip) for i in range(HEADS) if sender(...  11.4 us
    pallas_call x2, Pallas kernels, project(): pl.pallas_call(kernel, grid=(steps,), in_specs=[pl.BlockSpec((rows, depth...  10.5 us
    ppermute x8, starting transfers between devices, exchange(): return lax.ppermute(mine, 'seq', swap)  10.3 us
    pallas_call x4, Pallas kernels, pack_partner(): pl.pallas_call(pack_kernel, grid_spec=pltpu.PrefetchScalarGridSpec(num_sc...  7.59 us
  transfers between devices with their start and end apart: 22, of which 12 were waited for; matrix products, arithmetic and copies ran while one was open for 2% of the time, Pallas kernels for 40%

profile of v4, /device:TPU:2, one launch (start us, length us, event | category | flops | bytes accessed | tf_op | source)
XLA Modules:
  0.0 192.8 jit_solution(16823328312999735786)
XLA Ops:
  8.0 2.6 %shard_map.140.rest_0_ = bf16[3,576,256]{2,1,0:T(8,128)(2,1)} custom-call(s32[5]{0:T(128)S(1)} %stack.23.place_ref, bf16[576,2048]{1,0:T(8,128)(2,1)} %q_ref.15, bf16[576,2048]{1,0:T(8,128)(2,1)} %k_ref.15, bf16[576,2048]{1,0:T(8,128)(2,1)} %v_ref.15), custom_call_target="tpu_custom_call" | custom-call | flops 1 | bytes 1 | tf_op jit(solution)/shard_map/pallas_call | solution.py:186
  12.1 2.7 %shard_map.141.rest_0_ = bf16[3,576,256]{2,1,0:T(8,128)(2,1)} custom-call(s32[5]{0:T(128)S(1)} %stack.23.place_ref, bf16[576,2048]{1,0:T(8,128)(2,1)} %q_ref.15, bf16[576,2048]{1,0:T(8,128)(2,1)} %k_ref.15, bf16[576,2048]{1,0:T(8,128)(2,1)} %v_ref.15, bf16[3,576,256]{2,1,0:T(8,128)(2,1)} %shard_map.140.rest_0_), custom_call_target="tpu_custom_call" | custom-call | flops 1 | bytes 1 | tf_op jit(solution)/shard_map/pallas_call | solution.py:186
  15.4 1.7 copy-done.1
  17.0 1.7 copy-done.2
  21.1 1.6 collective-permute-start.5
  23.7 9.7 %collective-permute-done.1.other_ref = bf16[3,576,256]{2,1,0:T(8,128)(2,1)S(1)} collective-permute-done((bf16[3,576,256]{2,1,0:T(8,128)(2,1)}, bf16[3,576,256]{2,1,0:T(8,128)(2,1)S(1)}, u32[]{:S(2)}, u32[]{:S(2)}) %collective-permute-start.1) | collective-permute-done | bytes 884768 | tf_op jit(solution)/shard_map/ppermute | solution.py:484
  33.4 7.3 %shard_map.143.rest_0_.refs_0_ = bf16[1152,256]{1,0:T(8,128)(2,1)} custom-call(s32[5]{0:T(128)S(1)} %stack.23.place_ref, bf16[576,2048]{1,0:T(8,128)(2,1)S(1)} %copy-done, bf16[576,2048]{1,0:T(8,128)(2,1)S(1)} %copy-done.1, bf16[576,2048]{1,0:T(8,128)(2,1)S(1)} %copy-done.2, bf16[3,576,256]{2,1,0:T(8,128)(2,1)S(1)} %collective-permute-done.1.other_ref, ...), custom_call_target="tpu_custom_call" | custom-call | flops 1 | bytes 1 | tf_op jit(solution)/shard_map/pallas_call | solution.py:117
  40.6 11.7 %collective-permute-done.3.other_ref = bf16[3,576,256]{2,1,0:T(8,128)(2,1)S(1)} collective-permute-done((bf16[3,576,256]{2,1,0:T(8,128)(2,1)}, bf16[3,576,256]{2,1,0:T(8,128)(2,1)S(1)}, u32[]{:S(2)}, u32[]{:S(2)}) %collective-permute-start.3) | collective-permute-done | bytes 884768 | tf_op jit(solution)/shard_map/ppermute | solution.py:484
  52.3 7.3 %shard_map.144.rest_0_.refs_2_ = bf16[1152,256]{1,0:T(8,128)(2,1)} custom-call(s32[5]{0:T(128)S(1)} %stack.23.place_ref, bf16[576,2048]{1,0:T(8,128)(2,1)S(1)} %copy-done, bf16[576,2048]{1,0:T(8,128)(2,1)S(1)} %copy-done.1, bf16[576,2048]{1,0:T(8,128)(2,1)S(1)} %copy-done.2, bf16[3,576,256]{2,1,0:T(8,128)(2,1)S(1)} %collective-permute-done.3.other_ref, ...), custom_call_target="tpu_custom_call" | custom-call | flops 1 | bytes 1 | tf_op jit(solution)/shard_map/pallas_call | solution.py:117
  64.4 6.9 %collective-permute-done.5.other_ref = bf16[3,576,256]{2,1,0:T(8,128)(2,1)S(1)} collective-permute-done((bf16[3,576,256]{2,1,0:T(8,128)(2,1)S(1)}, bf16[3,576,256]{2,1,0:T(8,128)(2,1)S(1)}, u32[]{:S(2)}, u32[]{:S(2)}) %collective-permute-start.5) | collective-permute-done | bytes 884768 | tf_op jit(solution)/shard_map/ppermute | solution.py:484
  71.3 7.3 %shard_map.146.refs_0_.refs_4_ = bf16[1152,256]{1,0:T(8,128)(2,1)} custom-call(s32[5]{0:T(128)S(1)} %stack.23.place_ref, bf16[576,2048]{1,0:T(8,128)(2,1)S(1)} %copy-done, bf16[576,2048]{1,0:T(8,128)(2,1)S(1)} %copy-done.1, bf16[576,2048]{1,0:T(8,128)(2,1)S(1)} %copy-done.2, bf16[3,576,256]{2,1,0:T(8,128)(2,1)S(1)} %collective-permute-done.5.other_ref, ...), custom_call_target="tpu_custom_call" | custom-call | flops 1 | bytes 1 | tf_op jit(solution)/shard_map/pallas_call | solution.py:117
  80.1 2.6 %multiply_convert_fusion.refs_2_ = bf16[1152,1536]{1,0:T(8,128)(2,1)} fusion(bf16[1152,1536]{1,0:T(8,128)(2,1)S(1)} %copy-done.8, f32[1536]{0:T(1024)S(1)} %convert_reduce_fusion), kind=kLoop, calls=%fused_computation | loop fusion | flops 5308416 | bytes 7084032 | tf_op jit(solution)/shard_map/convert_element_type | solution.py:474
  84.0 12.6 %collective-permute-done.2.refs_1_ = bf16[1152,256]{1,0:T(8,128)(2,1)} collective-permute-done((bf16[1152,256]{1,0:T(8,128)(2,1)}, bf16[1152,256]{1,0:T(8,128)(2,1)}, u32[]{:S(2)}, u32[]{:S(2)}) %collective-permute-start.2) | collective-permute-done | bytes 589856 | tf_op jit(solution)/shard_map/ppermute | solution.py:484
  96.7 13.3 %conditional.1 = (bf16[4,128,1536]{2,1,0:T(8,128)(2,1)}) conditional(s32[]{:T(128)} %bitcast.14, () %tuple.15, (s32[5]{0:T(128)S(1)}, bf16[1152,256]{1,0:T(8,128)(2,1)}, bf16[1152,256]{1,0:T(8,128)(2,1)}, bf16[1152,256]{1,0:T(8,128)(2,1)}, bf16[1152,256]{1,0:T(8,128)(2,1)}, /*index=5*/bf16[1152,1536]{1,0:T(8,128)(2,1)}) %tuple.17), branch_computations={%region_0.1_spmd, %region_1.2_spmd} | conditional | flops 2 | bytes 6291506 | solution.py:492
  96.7 8.0 %branch_1_fun.2 = (bf16[4,128,1536]{2,1,0:T(8,128)(2,1)S(1)}, bf16[4,128,1536]{2,1,0:T(8,128)(2,1)S(1)}) custom-call(s32[5]{0:T(128)S(1)} %get-tuple-element.5.place_ref, bf16[1152,256]{1,0:T(8,128)(2,1)} %get-tuple-element.16.refs_0_, bf16[1152,256]{1,0:T(8,128)(2,1)} %get-tuple-element.17.refs_1_, bf16[1152,256]{1,0:T(8,128)(2,1)} %get-tuple-element.18.refs_2_, ...), custom_call_target="tpu_custom_call" | custom-call | flops 1 | bytes 1 | tf_op jit(solution)/shard_map/cond/branch_1_fun/pallas_call | solution.py:239
  104.8 3.4 %collective-permute-done.refs_1_ = bf16[4,128,1536]{2,1,0:T(8,128)(2,1)S(1)} collective-permute-done((bf16[4,128,1536]{2,1,0:T(8,128)(2,1)S(1)}, bf16[4,128,1536]{2,1,0:T(8,128)(2,1)S(1)}, u32[]{:S(2)}, u32[]{:S(2)}) %collective-permute-start) | collective-permute-done | bytes 1572896 | tf_op jit(solution)/shard_map/cond/branch_1_fun/ppermute | solution.py:457
  108.1 1.9 branch_1_fun.3
  110.0 2.0 %collective-permute-start.10 = (bf16[4,128,1536]{2,1,0:T(8,128)(2,1)}, bf16[4,128,1536]{2,1,0:T(8,128)(2,1)S(1)}, u32[]{:S(2)}, u32[]{:S(2)}) collective-permute-start(bf16[4,128,1536]{2,1,0:T(8,128)(2,1)} %get-tuple-element.82.rest_0_.refs_0_.refs_2_), channel_id=1, source_target_pairs={{2,6},{4,0},{10,14},{12,8},{18,22},{20,16},{26,30},{28,24},{3,7},{... | collective-permute-start | bytes 4718600 | tf_op jit(solution)/shard_map/ppermute | solution.py:457
  112.0 3.6 %collective-permute-done.7.other_ref = bf16[3,576,256]{2,1,0:T(8,128)(2,1)} collective-permute-done((bf16[3,576,256]{2,1,0:T(8,128)(2,1)S(1)}, bf16[3,576,256]{2,1,0:T(8,128)(2,1)}, u32[]{:S(2)}, u32[]{:S(2)}) %collective-permute-start.7) | collective-permute-done | bytes 884768 | tf_op jit(solution)/shard_map/ppermute | solution.py:484
  115.6 8.1 %shard_map.147.refs_3_.refs_0_.refs_6_ = bf16[1152,256]{1,0:T(8,128)(2,1)} custom-call(s32[5]{0:T(128)S(1)} %stack.23.place_ref, bf16[576,2048]{1,0:T(8,128)(2,1)} %q_ref.15, bf16[576,2048]{1,0:T(8,128)(2,1)} %k_ref.15, bf16[576,2048]{1,0:T(8,128)(2,1)} %v_ref.15, bf16[3,576,256]{2,1,0:T(8,128)(2,1)} %collective-permute-done.7.other_ref, ...), custom_call_target="tpu_custom_call" | custom-call | flops 1 | bytes 1 | tf_op jit(solution)/shard_map/pallas_call | solution.py:117
  125.2 2.9 %collective-permute-done.6.refs_1_.refs_5_ = bf16[1152,256]{1,0:T(8,128)(2,1)S(1)} collective-permute-done((bf16[1152,256]{1,0:T(8,128)(2,1)}, bf16[1152,256]{1,0:T(8,128)(2,1)S(1)}, u32[]{:S(2)}, u32[]{:S(2)}) %collective-permute-start.6) | collective-permute-done | bytes 589856 | tf_op jit(solution)/shard_map/ppermute | solution.py:484
  129.2 5.4 %shard_map.148 = (bf16[2,128,1536]{2,1,0:T(8,128)(2,1)S(1)}, bf16[2,128,1536]{2,1,0:T(8,128)(2,1)S(1)}) custom-call(s32[5]{0:T(128)S(1)} %stack.23.place_ref, bf16[1152,256]{1,0:T(8,128)(2,1)} %shard_map.146.refs_0_.refs_4_, bf16[1152,256]{1,0:T(8,128)(2,1)S(1)} %collective-permute-done.6.refs_1_.refs_5_, bf16[1152,1536]{1,0:T(8,128)(2,1)} %multiply_convert_fusion.refs_2_, ...), custom_call_target="tpu_custom_call" | custom-call | flops 20000000000 | bytes 20000000 | tf_op jit(solution)/shard_map/pallas_call | solution.py:239
  134.7 2.4 %shard_map.149 = (f32[2,128,1536]{2,1,0:T(8,128)S(1)}, bf16[2,128,1536]{2,1,0:T(8,128)(2,1)S(1)}) custom-call(s32[5]{0:T(128)S(1)} %stack.23.place_ref, bf16[4,128,1536]{2,1,0:T(8,128)(2,1)} %get-tuple-element.82.rest_0_.refs_0_.refs_2_, bf16[4,128,1536]{2,1,0:T(8,128)(2,1)S(1)} %collective-permute-done.10.refs_1_.refs_3_, ...), custom_call_target="tpu_custom_call" | custom-call | flops 20000000000 | bytes 20000000 | tf_op jit(solution)/shard_map/pallas_call | solution.py:277
  139.7 3.8 %shard_map.151 = (bf16[2,128,1536]{2,1,0:T(8,128)(2,1)S(1)}, bf16[2,128,1536]{2,1,0:T(8,128)(2,1)S(1)}) custom-call(s32[5]{0:T(128)S(1)} %stack.23.place_ref, bf16[1152,256]{1,0:T(8,128)(2,1)S(1)} %copy-done.6, bf16[1152,256]{1,0:T(8,128)(2,1)S(1)} %collective-permute-done.8.refs_1_.refs_7_, bf16[1152,1536]{1,0:T(8,128)(2,1)S(1)} %copy-done.7, ...), custom_call_target="tpu_custom_call" | custom-call | flops 1 | bytes 1 | tf_op jit(solution)/shard_map/pallas_call | solution.py:239
  143.5 3.0 %collective-permute-start.13 = (bf16[2,128,1536]{2,1,0:T(8,128)(2,1)S(1)}, bf16[2,128,1536]{2,1,0:T(8,128)(2,1)S(1)}, u32[]{:S(2)}, u32[]{:S(2)}) collective-permute-start(bf16[2,128,1536]{2,1,0:T(8,128)(2,1)S(1)} %get-tuple-element.49.refs_8_), channel_id=1, source_target_pairs={{0,2},{2,0},{4,6},{6,4},{8,10},{10,8},{12,14},{14,12},{16,18},{18,... | collective-permute-start | bytes 2359304 | tf_op jit(solution)/shard_map/ppermute | solution.py:457
  146.5 4.0 %shard_map.152 = (bf16[1152,2048]{1,0:T(8,128)(2,1)S(1)}, f32[8,128]{1,0:T(8,128)S(1)}) custom-call(s32[5]{0:T(128)S(1)} %stack.23.place_ref, bf16[1152,256]{1,0:T(8,128)(2,1)} %shard_map.143.rest_0_.refs_0_, bf16[1152,256]{1,0:T(8,128)(2,1)} %collective-permute-done.2.refs_1_, bf16[1152,256]{1,0:T(8,128)(2,1)} %shard_map.144.rest_0_.refs_2_, ...), custom_call_target="tpu_custom_call" | custom-call | flops 20000000000 | bytes 20000000 | tf_op jit(solution)/shard_map/pallas_call | solution.py:390
  153.0 2.9 %collective-permute-start.14 = (bf16[2,128,1536]{2,1,0:T(8,128)(2,1)S(1)}, bf16[2,128,1536]{2,1,0:T(8,128)(2,1)S(1)}, u32[]{:S(2)}, u32[]{:S(2)}) collective-permute-start(bf16[2,128,1536]{2,1,0:T(8,128)(2,1)S(1)} %shard_map.155.refs_0_), channel_id=1, source_target_pairs={{2,10},{4,12},{26,18},{28,20},{3,11},{5,13},{27,19},{29,21}} | collective-permute-start | bytes 2359304 | tf_op jit(solution)/shard_map/ppermute | solution.py:457
  156.6 5.3 %shard_map.156 = (bf16[1152,1536]{1,0:T(8,128)(2,1)}, f32[8,128]{1,0:T(8,128)S(1)}) custom-call(bf16[1152,2048]{1,0:T(8,128)(2,1)S(1)} %get-tuple-element.50.attention_ref, bf16[2048,1536]{1,0:T(8,128)(2,1)S(1)} %bitcast.25, f32[1,1536]{1,0:T(1,128)S(1)} %convert_element_type.19.gate_ref, bf16[2,128,1536]{2,1,0:T(8,128)(2,1)S(1)} %shard_map.155.refs_0_), custom_call_target="tpu_custom_call" | custom-call | flops 1 | bytes 1 | tf_op jit(solution)/shard_map/pallas_call | solution.py:423
  161.8 2.7 %collective-permute-done.15.refs_1_.refs_3_ = bf16[2,128,1536]{2,1,0:T(8,128)(2,1)S(1)} collective-permute-done((bf16[2,128,1536]{2,1,0:T(8,128)(2,1)S(1)}, bf16[2,128,1536]{2,1,0:T(8,128)(2,1)S(1)}, u32[]{:S(2)}, u32[]{:S(2)}) %collective-permute-start.15) | collective-permute-done | bytes 786464 | tf_op jit(solution)/shard_map/ppermute | solution.py:457
  166.6 4.4 %collective-permute-start.20 = (bf16[1,128,1536]{2,1,0:T(8,128)(2,1)S(1)}, bf16[1,128,1536]{2,1,0:T(8,128)(2,1)S(1)}, u32[]{:S(2)}, u32[]{:S(2)}) collective-permute-start(bf16[1,128,1536]{2,1,0:T(8,128)(2,1)S(1)} %get-tuple-element.64), channel_id=1, source_target_pairs={{2,26},{4,28},{26,2},{28,4},{3,27},{5,29},{27,3},{29,5}} | collective-permute-start | bytes 1179656 | tf_op jit(solution)/shard_map/ppermute | solution.py:457
  173.9 5.3 %shard_map.159 = (bf16[1152,1536]{1,0:T(8,128)(2,1)}, f32[8,128]{1,0:T(8,128)S(1)}) custom-call(bf16[1152,2048]{1,0:T(8,128)(2,1)S(1)} %get-tuple-element.50.attention_ref, bf16[2048,1536]{1,0:T(8,128)(2,1)S(1)} %bitcast.25, f32[1,1536]{1,0:T(1,128)S(1)} %convert_element_type.19.gate_ref, ...), custom_call_target="tpu_custom_call", output_to_operand_aliasing={{0}: (3, {})} | custom-call | flops 20000000000 | bytes 20000000 | tf_op jit(solution)/shard_map/pallas_call | solution.py:423
  179.2 5.1 %collective-permute-done.18.refs_4_ = bf16[1,128,1536]{2,1,0:T(8,128)(2,1)S(1)} collective-permute-done((bf16[1,128,1536]{2,1,0:T(8,128)(2,1)S(1)}, bf16[1,128,1536]{2,1,0:T(8,128)(2,1)S(1)}, u32[]{:S(2)}, u32[]{:S(2)}) %collective-permute-start.18) | collective-permute-done | bytes 393248 | tf_op jit(solution)/shard_map/ppermute | solution.py:457
  (86 shorter events, 28.1 us)
Async XLA Ops:
  7.2 76.7 %all-gather.2.cloned.1.call-start = ((), (), s32[]{:S(2)}) async-start(), calls=%async_computation | async-start | bytes 6684672 | tf_op jit(solution)/shard_map/all_gather | solution.py:472
  10.6 4.7 %copy-start = (bf16[576,2048]{1,0:T(8,128)(2,1)S(1)}, bf16[576,2048]{1,0:T(8,128)(2,1)}, u32[]{:S(2)}) copy-start(bf16[576,2048]{1,0:T(8,128)(2,1)} %q_ref.15) | copy-start | bytes 7077892
  10.6 22.7 %collective-permute-start.1 = (bf16[3,576,256]{2,1,0:T(8,128)(2,1)}, bf16[3,576,256]{2,1,0:T(8,128)(2,1)S(1)}, u32[]{:S(2)}, u32[]{:S(2)}) collective-permute-start(bf16[3,576,256]{2,1,0:T(8,128)(2,1)} %shard_map.140.rest_0_), channel_id=1, source_target_pairs={{0,1},{1,0},{2,3},{3,2},{4,5},{5,4},{6,7},{7,6},{8,9},{9,8},{10,11... | collective-permute-start | bytes 2654216 | tf_op jit(solution)/shard_map/ppermute | solution.py:484
  14.9 37.5 %collective-permute-start.3 = (bf16[3,576,256]{2,1,0:T(8,128)(2,1)}, bf16[3,576,256]{2,1,0:T(8,128)(2,1)S(1)}, u32[]{:S(2)}, u32[]{:S(2)}) collective-permute-start(bf16[3,576,256]{2,1,0:T(8,128)(2,1)} %shard_map.141.rest_0_), channel_id=1, source_target_pairs={{0,1},{1,0},{2,3},{3,2},{4,5},{5,4},{6,7},{7,6},{8,9},{9,8},{10,11... | collective-permute-start | bytes 2654216 | tf_op jit(solution)/shard_map/ppermute | solution.py:484
  19.9 3.0 %copy-start.10 = (s32[1152]{0:T(1024)S(1)}, s32[1152]{0:T(1024)}, u32[]{:S(2)}) copy-start(s32[1152]{0:T(1024)} %constant.80) | copy-start | bytes 13828
  19.9 3.0 %copy-start.11 = (s32[1152]{0:T(1024)S(1)}, s32[1152]{0:T(1024)}, u32[]{:S(2)}) copy-start(s32[1152]{0:T(1024)} %constant.82) | copy-start | bytes 13828
  19.9 3.0 %copy-start.12 = (s32[1152]{0:T(1024)S(1)}, s32[1152]{0:T(1024)}, u32[]{:S(2)}) copy-start(s32[1152]{0:T(1024)} %constant.84) | copy-start | bytes 13828
  21.1 50.2 %collective-permute-start.5 = (bf16[3,576,256]{2,1,0:T(8,128)(2,1)S(1)}, bf16[3,576,256]{2,1,0:T(8,128)(2,1)S(1)}, u32[]{:S(2)}, u32[]{:S(2)}) collective-permute-start(bf16[3,576,256]{2,1,0:T(8,128)(2,1)S(1)} %shard_map.142.rest_0_), channel_id=1, source_target_pairs={{0,1},{1,0},{2,3},{3,2},{4,5},{5,4},{6,7},{7,6},{8,9},{9,8},{10,11... | collective-permute-start | bytes 2654216 | tf_op jit(solution)/shard_map/ppermute | solution.py:484
  23.7 47.6 %copy-start.3 = (f32[16,24,1152]{2,1,0:T(8,128)}, f32[16,24,1152]{2,1,0:T(8,128)S(1)}, u32[]{:S(2)}) copy-start(f32[16,24,1152]{2,1,0:T(8,128)S(1)} %and_select_fusion.bias_ref) | copy-start | bytes 5308420
  40.6 19.0 %copy-start.9 = (bf16[1,1536]{1,0:T(2,128)(2,1)S(1)}, bf16[1,1536]{1,0:T(2,128)(2,1)}, u32[]{:S(2)}) copy-start(bf16[1,1536]{1,0:T(2,128)(2,1)} %param.20) | copy-start | bytes 9220
  60.8 23.3 %collective-permute-start.4 = (bf16[1152,256]{1,0:T(8,128)(2,1)}, bf16[1152,256]{1,0:T(8,128)(2,1)}, u32[]{:S(2)}, u32[]{:S(2)}) collective-permute-start(bf16[1152,256]{1,0:T(8,128)(2,1)} %shard_map.144.rest_0_.refs_2_), channel_id=1, source_target_pairs={{0,1},{1,0},{2,3},{3,2},{4,5},{5,4},{6,7},{7,6},{8,9},{9,8},{10,11... | collective-permute-start | bytes 1769480 | tf_op jit(solution)/shard_map/ppermute | solution.py:484
  62.4 34.3 %collective-permute-start.2 = (bf16[1152,256]{1,0:T(8,128)(2,1)}, bf16[1152,256]{1,0:T(8,128)(2,1)}, u32[]{:S(2)}, u32[]{:S(2)}) collective-permute-start(bf16[1152,256]{1,0:T(8,128)(2,1)} %shard_map.143.rest_0_.refs_0_), channel_id=1, source_target_pairs={{0,1},{1,0},{2,3},{3,2},{4,5},{5,4},{6,7},{7,6},{8,9},{9,8},{10,11... | collective-permute-start | bytes 1769480 | tf_op jit(solution)/shard_map/ppermute | solution.py:484
  62.9 52.8 %collective-permute-start.7 = (bf16[3,576,256]{2,1,0:T(8,128)(2,1)S(1)}, bf16[3,576,256]{2,1,0:T(8,128)(2,1)}, u32[]{:S(2)}, u32[]{:S(2)}) collective-permute-start(bf16[3,576,256]{2,1,0:T(8,128)(2,1)S(1)} %shard_map.145.rest_1_), channel_id=1, source_target_pairs={{0,1},{1,0},{2,3},{3,2},{4,5},{5,4},{6,7},{7,6},{8,9},{9,8},{10,11... | collective-permute-start | bytes 2654216 | tf_op jit(solution)/shard_map/ppermute | solution.py:484
  71.3 8.8 %copy-start.8 = (bf16[1152,1536]{1,0:T(8,128)(2,1)S(1)}, bf16[1152,1536]{1,0:T(8,128)(2,1)}, u32[]{:S(2)}) copy-start(bf16[1152,1536]{1,0:T(8,128)(2,1)} %param.21) | copy-start | bytes 10616836
  78.6 49.6 %collective-permute-start.6 = (bf16[1152,256]{1,0:T(8,128)(2,1)}, bf16[1152,256]{1,0:T(8,128)(2,1)S(1)}, u32[]{:S(2)}, u32[]{:S(2)}) collective-permute-start(bf16[1152,256]{1,0:T(8,128)(2,1)} %shard_map.146.refs_0_.refs_4_), channel_id=1, source_target_pairs={{0,1},{1,0},{2,3},{3,2},{4,5},{5,4},{6,7},{7,6},{8,9},{9,8},{10,11... | collective-permute-start | bytes 1769480 | tf_op jit(solution)/shard_map/ppermute | solution.py:484
  104.7 3.5 %collective-permute-start = (bf16[4,128,1536]{2,1,0:T(8,128)(2,1)S(1)}, bf16[4,128,1536]{2,1,0:T(8,128)(2,1)S(1)}, u32[]{:S(2)}, u32[]{:S(2)}) collective-permute-start(bf16[4,128,1536]{2,1,0:T(8,128)(2,1)S(1)} %get-tuple-element.22), channel_id=1, source_target_pairs={{0,2},{2,0},{4,6},{6,4},{8,10},{10,8},{12,14},{14,12},{16,18},{18,... | collective-permute-start | bytes 4718600 | tf_op jit(solution)/shard_map/cond/branch_1_fun/ppermute | solution.py:457
  110.0 24.7 %collective-permute-start.10 = (bf16[4,128,1536]{2,1,0:T(8,128)(2,1)}, bf16[4,128,1536]{2,1,0:T(8,128)(2,1)S(1)}, u32[]{:S(2)}, u32[]{:S(2)}) collective-permute-start(bf16[4,128,1536]{2,1,0:T(8,128)(2,1)} %get-tuple-element.82.rest_0_.refs_0_.refs_2_), channel_id=1, source_target_pairs={{2,6},{4,0},{10,14},{12,8},{18,22},{20,16},{26,30},{28,24},{3,7},{... | collective-permute-start | bytes 4718600 | tf_op jit(solution)/shard_map/ppermute | solution.py:457
  123.7 16.0 %collective-permute-start.8 = (bf16[1152,256]{1,0:T(8,128)(2,1)}, bf16[1152,256]{1,0:T(8,128)(2,1)S(1)}, u32[]{:S(2)}, u32[]{:S(2)}) collective-permute-start(bf16[1152,256]{1,0:T(8,128)(2,1)} %shard_map.147.refs_3_.refs_0_.refs_6_), channel_id=1, source_target_pairs={{0,1},{1,0},{2,3},{3,2},{4,5},{5,4},{6,7},{7,6},{8,9},{9,8},{10,11... | collective-permute-start | bytes 1769480 | tf_op jit(solution)/shard_map/ppermute | solution.py:484
  134.6 3.4 %collective-permute-start.9 = (bf16[2,128,1536]{2,1,0:T(8,128)(2,1)S(1)}, bf16[2,128,1536]{2,1,0:T(8,128)(2,1)S(1)}, u32[]{:S(2)}, u32[]{:S(2)}) collective-permute-start(bf16[2,128,1536]{2,1,0:T(8,128)(2,1)S(1)} %get-tuple-element.47.refs_4_), channel_id=1, source_target_pairs={{0,2},{2,0},{4,6},{6,4},{8,10},{10,8},{12,14},{14,12},{16,18},{18,... | collective-permute-start | bytes 2359304 | tf_op jit(solution)/shard_map/ppermute | solution.py:457
  134.7 5.0 %copy-start.7 = (bf16[1152,1536]{1,0:T(8,128)(2,1)S(1)}, bf16[1152,1536]{1,0:T(8,128)(2,1)}, u32[]{:S(2)}) copy-start(bf16[1152,1536]{1,0:T(8,128)(2,1)} %multiply_convert_fusion.refs_2_) | copy-start | bytes 10616836
  137.1 14.9 %collective-permute-start.12 = (bf16[2,128,1536]{2,1,0:T(8,128)(2,1)S(1)}, bf16[2,128,1536]{2,1,0:T(8,128)(2,1)S(1)}, u32[]{:S(2)}, u32[]{:S(2)}) collective-permute-start(bf16[2,128,1536]{2,1,0:T(8,128)(2,1)S(1)} %get-tuple-element.48.refs_2_), channel_id=1, source_target_pairs={{0,8},{6,14},{8,0},{14,6},{16,24},{22,30},{24,16},{30,22},{1,9},{7... | collective-permute-start | bytes 2359304 | tf_op jit(solution)/shard_map/ppermute | solution.py:457
  138.2 14.6 %collective-permute-start.11 = (bf16[2,128,1536]{2,1,0:T(8,128)(2,1)S(1)}, bf16[2,128,1536]{2,1,0:T(8,128)(2,1)S(1)}, u32[]{:S(2)}, u32[]{:S(2)}) collective-permute-start(bf16[2,128,1536]{2,1,0:T(8,128)(2,1)S(1)} %shard_map.150.refs_3_.refs_0_), channel_id=1, source_target_pairs={{0,4},{6,2},{8,12},{14,10},{16,20},{22,18},{24,28},{30,26},{1,5},{... | collective-permute-start | bytes 2359304 | tf_op jit(solution)/shard_map/ppermute | solution.py:457
  139.7 16.9 %slice-start = ((s8[6291456]{0:T(1024)(128)(4,1)}), s8[4194304]{0:T(1024)(128)(4,1)S(1)}, s32[]{:S(2)}) async-start(s8[6291456]{0:T(1024)(128)(4,1)} %bitcast.24), calls=%async_computation.1 | async-start | bytes 8388608
  143.5 13.1 %slice-start.1 = ((s8[6291456]{0:T(1024)(128)(4,1)}), s8[2097152]{0:T(1024)(128)(4,1)S(1)}, s32[]{:S(2)}) async-start(s8[6291456]{0:T(1024)(128)(4,1)} %bitcast.24), calls=%async_computation.2 | async-start | bytes 4194304
  143.5 6.9 %collective-permute-start.13 = (bf16[2,128,1536]{2,1,0:T(8,128)(2,1)S(1)}, bf16[2,128,1536]{2,1,0:T(8,128)(2,1)S(1)}, u32[]{:S(2)}, u32[]{:S(2)}) collective-permute-start(bf16[2,128,1536]{2,1,0:T(8,128)(2,1)S(1)} %get-tuple-element.49.refs_8_), channel_id=1, source_target_pairs={{0,2},{2,0},{4,6},{6,4},{8,10},{10,8},{12,14},{14,12},{16,18},{18,... | collective-permute-start | bytes 2359304 | tf_op jit(solution)/shard_map/ppermute | solution.py:457
  150.7 13.9 %collective-permute-start.15 = (bf16[2,128,1536]{2,1,0:T(8,128)(2,1)S(1)}, bf16[2,128,1536]{2,1,0:T(8,128)(2,1)S(1)}, u32[]{:S(2)}, u32[]{:S(2)}) collective-permute-start(bf16[2,128,1536]{2,1,0:T(8,128)(2,1)S(1)} %shard_map.153.refs_4_.refs_0_.refs_2_), channel_id=1, source_target_pairs={{0,4},{6,2},{8,12},{14,10},{16,20},{22,18},{24,28},{30,26},{1,5},{... | collective-permute-start | bytes 2359304 | tf_op jit(solution)/shard_map/ppermute | solution.py:457
  153.0 19.3 %collective-permute-start.14 = (bf16[2,128,1536]{2,1,0:T(8,128)(2,1)S(1)}, bf16[2,128,1536]{2,1,0:T(8,128)(2,1)S(1)}, u32[]{:S(2)}, u32[]{:S(2)}) collective-permute-start(bf16[2,128,1536]{2,1,0:T(8,128)(2,1)S(1)} %shard_map.155.refs_0_), channel_id=1, source_target_pairs={{2,10},{4,12},{26,18},{28,20},{3,11},{5,13},{27,19},{29,21}} | collective-permute-start | bytes 2359304 | tf_op jit(solution)/shard_map/ppermute | solution.py:457
  155.9 23.2 %collective-permute-start.16 = (bf16[1,128,1536]{2,1,0:T(8,128)(2,1)S(1)}, bf16[1,128,1536]{2,1,0:T(8,128)(2,1)S(1)}, u32[]{:S(2)}, u32[]{:S(2)}) collective-permute-start(bf16[1,128,1536]{2,1,0:T(8,128)(2,1)S(1)} %get-tuple-element.54.refs_2_), channel_id=1, source_target_pairs={{0,16},{6,22},{8,24},{14,30},{16,0},{22,6},{24,8},{30,14},{1,17},{... | collective-permute-start | bytes 1179656 | tf_op jit(solution)/shard_map/ppermute | solution.py:457
  165.3 19.0 %collective-permute-start.19 = (bf16[1,128,1536]{2,1,0:T(8,128)(2,1)S(1)}, bf16[1,128,1536]{2,1,0:T(8,128)(2,1)S(1)}, u32[]{:S(2)}, u32[]{:S(2)}) collective-permute-start(bf16[1,128,1536]{2,1,0:T(8,128)(2,1)S(1)} %get-tuple-element.64), channel_id=1, source_target_pairs={{10,26},{12,28},{18,2},{20,4},{11,27},{13,29},{19,3},{21,5}} | collective-permute-start | bytes 1179656 | tf_op jit(solution)/shard_map/ppermute | solution.py:457
  166.6 17.7 %collective-permute-start.20 = (bf16[1,128,1536]{2,1,0:T(8,128)(2,1)S(1)}, bf16[1,128,1536]{2,1,0:T(8,128)(2,1)S(1)}, u32[]{:S(2)}, u32[]{:S(2)}) collective-permute-start(bf16[1,128,1536]{2,1,0:T(8,128)(2,1)S(1)} %get-tuple-element.64), channel_id=1, source_target_pairs={{2,26},{4,28},{26,2},{28,4},{3,27},{5,29},{27,3},{29,5}} | collective-permute-start | bytes 1179656 | tf_op jit(solution)/shard_map/ppermute | solution.py:457
  171.0 13.3 %collective-permute-start.18 = (bf16[1,128,1536]{2,1,0:T(8,128)(2,1)S(1)}, bf16[1,128,1536]{2,1,0:T(8,128)(2,1)S(1)}, u32[]{:S(2)}, u32[]{:S(2)}) collective-permute-start(bf16[1,128,1536]{2,1,0:T(8,128)(2,1)S(1)} %get-tuple-element.57.refs_6_), channel_id=1, source_target_pairs={{10,2},{12,4},{18,26},{20,28},{11,3},{13,5},{19,27},{21,29}} | collective-permute-start | bytes 1179656 | tf_op jit(solution)/shard_map/ppermute | solution.py:457
  173.2 6.0 %collective-permute-start.17 = (bf16[1,128,1536]{2,1,0:T(8,128)(2,1)S(1)}, bf16[1,128,1536]{2,1,0:T(8,128)(2,1)S(1)}, u32[]{:S(2)}, u32[]{:S(2)}) collective-permute-start(bf16[1,128,1536]{2,1,0:T(8,128)(2,1)S(1)} %get-tuple-element.58.refs_1_), channel_id=1, source_target_pairs={{10,18},{12,20},{18,10},{20,12},{11,19},{13,21},{19,11},{21,13}} | collective-permute-start | bytes 1179656 | tf_op jit(solution)/shard_map/ppermute | solution.py:457
  (9 other events, 19.5 us)
Sparse Core Ops, SparseCore 0:
  10.3 62.1 all-gather.1

commit v5 on v3

--- a/solution.py
+++ b/solution.py
@@ -24,7 +24,7 @@
 VMEM_PROJECT = 24 * 1024 * 1024
 PROJECT_STEPS = 6
 GRADIENT_STEPS = 3
-JOIN_STEPS = 4
+JOIN_STEPS = 8
 SEQ, CORE, X, LOW, HIGH = range(5)
 VMEM_WHOLE = 60 * 1024 * 1024
 VMEM_SMALL = 12 * 1024 * 1024

time: 193 us -> 195 us (1.010)
  transfers between devices with their start and end apart: 22 -> 22, of which waited for: 13 -> 12; matrix products, arithmetic and copies ran while one was open for 2% -> 2% of each run, Pallas kernels for 40% -> 40%
where the time goes in v5:
time: 195 us; the launch traced here: 194 us
  Pallas kernels  79.6 us (41%)
  waiting for transfers between devices  60.3 us (31%)
  starting transfers between devices  29.6 us (15%)
  between operations  15 us (8%)
  local copies, waits for them, and re-layouts  6.27 us (3%)
  other arithmetic  3.61 us (2%)
    ppermute x8, waiting for transfers between devices, exchange(): return lax.ppermute(mine, 'seq', swap)  47.8 us
    pallas_call x4, Pallas kernels, attend_pair(): pl.pallas_call(pair_kernel, grid_spec=pltpu.PrefetchScalarGridSpec(num_sc...  29.9 us
    ppermute x13, starting transfers between devices, dp_send(): lax.ppermute(value, 'dp', [(i, i ^ flip) for i in range(HEADS) if sender(...  19.3 us
    pallas_call x3, Pallas kernels, batch_gradient(): pl.pallas_call(functools.partial(gradient_kernel, by_call=by_call), grid_...  17.2 us
    ppermute x13, waiting for transfers between devices, dp_send(): lax.ppermute(value, 'dp', [(i, i ^ flip) for i in range(HEADS) if sender(...  11.8 us
    pallas_call x2, Pallas kernels, project(): pl.pallas_call(kernel, grid=(steps,), in_specs=[pl.BlockSpec((rows, depth...  10.5 us
    ppermute x8, starting transfers between devices, exchange(): return lax.ppermute(mine, 'seq', swap)  10.3 us
    pallas_call x4, Pallas kernels, pack_partner(): pl.pallas_call(pack_kernel, grid_spec=pltpu.PrefetchScalarGridSpec(num_sc...  7.59 us
  transfers between devices with their start and end apart: 22, of which 12 were waited for; matrix products, arithmetic and copies ran while one was open for 2% of the time, Pallas kernels for 40%

profile of v5, /device:TPU:2, one launch (start us, length us, event | category | flops | bytes accessed | tf_op | source)
XLA Modules:
  0.0 194.4 jit_solution(14862203244647415009)
XLA Ops:
  8.0 2.6 %shard_map.140.rest_0_ = bf16[3,576,256]{2,1,0:T(8,128)(2,1)} custom-call(s32[5]{0:T(128)S(1)} %stack.23.place_ref, bf16[576,2048]{1,0:T(8,128)(2,1)} %q_ref.15, bf16[576,2048]{1,0:T(8,128)(2,1)} %k_ref.15, bf16[576,2048]{1,0:T(8,128)(2,1)} %v_ref.15), custom_call_target="tpu_custom_call" | custom-call | flops 1 | bytes 1 | tf_op jit(solution)/shard_map/pallas_call | solution.py:186
  12.1 2.7 %shard_map.141.rest_0_ = bf16[3,576,256]{2,1,0:T(8,128)(2,1)} custom-call(s32[5]{0:T(128)S(1)} %stack.23.place_ref, bf16[576,2048]{1,0:T(8,128)(2,1)} %q_ref.15, bf16[576,2048]{1,0:T(8,128)(2,1)} %k_ref.15, bf16[576,2048]{1,0:T(8,128)(2,1)} %v_ref.15, bf16[3,576,256]{2,1,0:T(8,128)(2,1)} %shard_map.140.rest_0_), custom_call_target="tpu_custom_call" | custom-call | flops 1 | bytes 1 | tf_op jit(solution)/shard_map/pallas_call | solution.py:186
  15.4 1.7 copy-done.1
  17.0 1.7 copy-done.2
  21.1 1.6 collective-permute-start.5
  23.7 9.7 %collective-permute-done.1.other_ref = bf16[3,576,256]{2,1,0:T(8,128)(2,1)S(1)} collective-permute-done((bf16[3,576,256]{2,1,0:T(8,128)(2,1)}, bf16[3,576,256]{2,1,0:T(8,128)(2,1)S(1)}, u32[]{:S(2)}, u32[]{:S(2)}) %collective-permute-start.1) | collective-permute-done | bytes 884768 | tf_op jit(solution)/shard_map/ppermute | solution.py:484
  33.4 7.3 %shard_map.143.rest_0_.refs_0_ = bf16[1152,256]{1,0:T(8,128)(2,1)} custom-call(s32[5]{0:T(128)S(1)} %stack.23.place_ref, bf16[576,2048]{1,0:T(8,128)(2,1)S(1)} %copy-done, bf16[576,2048]{1,0:T(8,128)(2,1)S(1)} %copy-done.1, bf16[576,2048]{1,0:T(8,128)(2,1)S(1)} %copy-done.2, bf16[3,576,256]{2,1,0:T(8,128)(2,1)S(1)} %collective-permute-done.1.other_ref, ...), custom_call_target="tpu_custom_call" | custom-call | flops 1 | bytes 1 | tf_op jit(solution)/shard_map/pallas_call | solution.py:117
  40.6 11.7 %collective-permute-done.3.other_ref = bf16[3,576,256]{2,1,0:T(8,128)(2,1)S(1)} collective-permute-done((bf16[3,576,256]{2,1,0:T(8,128)(2,1)}, bf16[3,576,256]{2,1,0:T(8,128)(2,1)S(1)}, u32[]{:S(2)}, u32[]{:S(2)}) %collective-permute-start.3) | collective-permute-done | bytes 884768 | tf_op jit(solution)/shard_map/ppermute | solution.py:484
  52.3 7.3 %shard_map.144.rest_0_.refs_2_ = bf16[1152,256]{1,0:T(8,128)(2,1)} custom-call(s32[5]{0:T(128)S(1)} %stack.23.place_ref, bf16[576,2048]{1,0:T(8,128)(2,1)S(1)} %copy-done, bf16[576,2048]{1,0:T(8,128)(2,1)S(1)} %copy-done.1, bf16[576,2048]{1,0:T(8,128)(2,1)S(1)} %copy-done.2, bf16[3,576,256]{2,1,0:T(8,128)(2,1)S(1)} %collective-permute-done.3.other_ref, ...), custom_call_target="tpu_custom_call" | custom-call | flops 1 | bytes 1 | tf_op jit(solution)/shard_map/pallas_call | solution.py:117
  64.4 6.9 %collective-permute-done.5.other_ref = bf16[3,576,256]{2,1,0:T(8,128)(2,1)S(1)} collective-permute-done((bf16[3,576,256]{2,1,0:T(8,128)(2,1)S(1)}, bf16[3,576,256]{2,1,0:T(8,128)(2,1)S(1)}, u32[]{:S(2)}, u32[]{:S(2)}) %collective-permute-start.5) | collective-permute-done | bytes 884768 | tf_op jit(solution)/shard_map/ppermute | solution.py:484
  71.3 7.3 %shard_map.146.refs_0_.refs_4_ = bf16[1152,256]{1,0:T(8,128)(2,1)} custom-call(s32[5]{0:T(128)S(1)} %stack.23.place_ref, bf16[576,2048]{1,0:T(8,128)(2,1)S(1)} %copy-done, bf16[576,2048]{1,0:T(8,128)(2,1)S(1)} %copy-done.1, bf16[576,2048]{1,0:T(8,128)(2,1)S(1)} %copy-done.2, bf16[3,576,256]{2,1,0:T(8,128)(2,1)S(1)} %collective-permute-done.5.other_ref, ...), custom_call_target="tpu_custom_call" | custom-call | flops 1 | bytes 1 | tf_op jit(solution)/shard_map/pallas_call | solution.py:117
  80.1 2.6 %multiply_convert_fusion.refs_2_ = bf16[1152,1536]{1,0:T(8,128)(2,1)} fusion(bf16[1152,1536]{1,0:T(8,128)(2,1)S(1)} %copy-done.8, f32[1536]{0:T(1024)S(1)} %convert_reduce_fusion), kind=kLoop, calls=%fused_computation | loop fusion | flops 5308416 | bytes 7084032 | tf_op jit(solution)/shard_map/convert_element_type | solution.py:474
  84.0 12.6 %collective-permute-done.2.refs_1_ = bf16[1152,256]{1,0:T(8,128)(2,1)} collective-permute-done((bf16[1152,256]{1,0:T(8,128)(2,1)}, bf16[1152,256]{1,0:T(8,128)(2,1)}, u32[]{:S(2)}, u32[]{:S(2)}) %collective-permute-start.2) | collective-permute-done | bytes 589856 | tf_op jit(solution)/shard_map/ppermute | solution.py:484
  96.7 13.3 %conditional.1 = (bf16[4,128,1536]{2,1,0:T(8,128)(2,1)}) conditional(s32[]{:T(128)} %bitcast.14, () %tuple.15, (s32[5]{0:T(128)S(1)}, bf16[1152,256]{1,0:T(8,128)(2,1)}, bf16[1152,256]{1,0:T(8,128)(2,1)}, bf16[1152,256]{1,0:T(8,128)(2,1)}, bf16[1152,256]{1,0:T(8,128)(2,1)}, /*index=5*/bf16[1152,1536]{1,0:T(8,128)(2,1)}) %tuple.17), branch_computations={%region_0.1_spmd, %region_1.2_spmd} | conditional | flops 2 | bytes 6291506 | solution.py:492
  96.7 8.0 %branch_1_fun.2 = (bf16[4,128,1536]{2,1,0:T(8,128)(2,1)S(1)}, bf16[4,128,1536]{2,1,0:T(8,128)(2,1)S(1)}) custom-call(s32[5]{0:T(128)S(1)} %get-tuple-element.5.place_ref, bf16[1152,256]{1,0:T(8,128)(2,1)} %get-tuple-element.16.refs_0_, bf16[1152,256]{1,0:T(8,128)(2,1)} %get-tuple-element.17.refs_1_, bf16[1152,256]{1,0:T(8,128)(2,1)} %get-tuple-element.18.refs_2_, ...), custom_call_target="tpu_custom_call" | custom-call | flops 1 | bytes 1 | tf_op jit(solution)/shard_map/cond/branch_1_fun/pallas_call | solution.py:239
  104.8 3.4 %collective-permute-done.refs_1_ = bf16[4,128,1536]{2,1,0:T(8,128)(2,1)S(1)} collective-permute-done((bf16[4,128,1536]{2,1,0:T(8,128)(2,1)S(1)}, bf16[4,128,1536]{2,1,0:T(8,128)(2,1)S(1)}, u32[]{:S(2)}, u32[]{:S(2)}) %collective-permute-start) | collective-permute-done | bytes 1572896 | tf_op jit(solution)/shard_map/cond/branch_1_fun/ppermute | solution.py:457
  108.1 1.9 branch_1_fun.3
  110.0 2.0 %collective-permute-start.10 = (bf16[4,128,1536]{2,1,0:T(8,128)(2,1)}, bf16[4,128,1536]{2,1,0:T(8,128)(2,1)S(1)}, u32[]{:S(2)}, u32[]{:S(2)}) collective-permute-start(bf16[4,128,1536]{2,1,0:T(8,128)(2,1)} %get-tuple-element.82.rest_0_.refs_0_.refs_2_), channel_id=1, source_target_pairs={{2,6},{4,0},{10,14},{12,8},{18,22},{20,16},{26,30},{28,24},{3,7},{... | collective-permute-start | bytes 4718600 | tf_op jit(solution)/shard_map/ppermute | solution.py:457
  112.0 3.6 %collective-permute-done.7.other_ref = bf16[3,576,256]{2,1,0:T(8,128)(2,1)} collective-permute-done((bf16[3,576,256]{2,1,0:T(8,128)(2,1)S(1)}, bf16[3,576,256]{2,1,0:T(8,128)(2,1)}, u32[]{:S(2)}, u32[]{:S(2)}) %collective-permute-start.7) | collective-permute-done | bytes 884768 | tf_op jit(solution)/shard_map/ppermute | solution.py:484
  115.6 8.1 %shard_map.147.refs_3_.refs_0_.refs_6_ = bf16[1152,256]{1,0:T(8,128)(2,1)} custom-call(s32[5]{0:T(128)S(1)} %stack.23.place_ref, bf16[576,2048]{1,0:T(8,128)(2,1)} %q_ref.15, bf16[576,2048]{1,0:T(8,128)(2,1)} %k_ref.15, bf16[576,2048]{1,0:T(8,128)(2,1)} %v_ref.15, bf16[3,576,256]{2,1,0:T(8,128)(2,1)} %collective-permute-done.7.other_ref, ...), custom_call_target="tpu_custom_call" | custom-call | flops 1 | bytes 1 | tf_op jit(solution)/shard_map/pallas_call | solution.py:117
  125.2 2.9 %collective-permute-done.6.refs_1_.refs_5_ = bf16[1152,256]{1,0:T(8,128)(2,1)S(1)} collective-permute-done((bf16[1152,256]{1,0:T(8,128)(2,1)}, bf16[1152,256]{1,0:T(8,128)(2,1)S(1)}, u32[]{:S(2)}, u32[]{:S(2)}) %collective-permute-start.6) | collective-permute-done | bytes 589856 | tf_op jit(solution)/shard_map/ppermute | solution.py:484
  129.2 5.4 %shard_map.148 = (bf16[2,128,1536]{2,1,0:T(8,128)(2,1)S(1)}, bf16[2,128,1536]{2,1,0:T(8,128)(2,1)S(1)}) custom-call(s32[5]{0:T(128)S(1)} %stack.23.place_ref, bf16[1152,256]{1,0:T(8,128)(2,1)} %shard_map.146.refs_0_.refs_4_, bf16[1152,256]{1,0:T(8,128)(2,1)S(1)} %collective-permute-done.6.refs_1_.refs_5_, bf16[1152,1536]{1,0:T(8,128)(2,1)} %multiply_convert_fusion.refs_2_, ...), custom_call_target="tpu_custom_call" | custom-call | flops 20000000000 | bytes 20000000 | tf_op jit(solution)/shard_map/pallas_call | solution.py:239
  134.7 2.4 %shard_map.149 = (f32[2,128,1536]{2,1,0:T(8,128)S(1)}, bf16[2,128,1536]{2,1,0:T(8,128)(2,1)S(1)}) custom-call(s32[5]{0:T(128)S(1)} %stack.23.place_ref, bf16[4,128,1536]{2,1,0:T(8,128)(2,1)} %get-tuple-element.82.rest_0_.refs_0_.refs_2_, bf16[4,128,1536]{2,1,0:T(8,128)(2,1)S(1)} %collective-permute-done.10.refs_1_.refs_3_, ...), custom_call_target="tpu_custom_call" | custom-call | flops 20000000000 | bytes 20000000 | tf_op jit(solution)/shard_map/pallas_call | solution.py:277
  139.7 3.8 %shard_map.151 = (bf16[2,128,1536]{2,1,0:T(8,128)(2,1)S(1)}, bf16[2,128,1536]{2,1,0:T(8,128)(2,1)S(1)}) custom-call(s32[5]{0:T(128)S(1)} %stack.23.place_ref, bf16[1152,256]{1,0:T(8,128)(2,1)S(1)} %copy-done.6, bf16[1152,256]{1,0:T(8,128)(2,1)S(1)} %collective-permute-done.8.refs_1_.refs_7_, bf16[1152,1536]{1,0:T(8,128)(2,1)S(1)} %copy-done.7, ...), custom_call_target="tpu_custom_call" | custom-call | flops 1 | bytes 1 | tf_op jit(solution)/shard_map/pallas_call | solution.py:239
  143.5 3.0 %collective-permute-start.13 = (bf16[2,128,1536]{2,1,0:T(8,128)(2,1)S(1)}, bf16[2,128,1536]{2,1,0:T(8,128)(2,1)S(1)}, u32[]{:S(2)}, u32[]{:S(2)}) collective-permute-start(bf16[2,128,1536]{2,1,0:T(8,128)(2,1)S(1)} %get-tuple-element.49.refs_8_), channel_id=1, source_target_pairs={{0,2},{2,0},{4,6},{6,4},{8,10},{10,8},{12,14},{14,12},{16,18},{18,... | collective-permute-start | bytes 2359304 | tf_op jit(solution)/shard_map/ppermute | solution.py:457
  146.5 5.6 %shard_map.152 = (bf16[1152,2048]{1,0:T(8,128)(2,1)S(1)}, f32[8,128]{1,0:T(8,128)S(1)}) custom-call(s32[5]{0:T(128)S(1)} %stack.23.place_ref, bf16[1152,256]{1,0:T(8,128)(2,1)} %shard_map.143.rest_0_.refs_0_, bf16[1152,256]{1,0:T(8,128)(2,1)} %collective-permute-done.2.refs_1_, bf16[1152,256]{1,0:T(8,128)(2,1)} %shard_map.144.rest_0_.refs_2_, ...), custom_call_target="tpu_custom_call" | custom-call | flops 20000000000 | bytes 20000000 | tf_op jit(solution)/shard_map/pallas_call | solution.py:390
  154.5 2.4 %collective-permute-start.14 = (bf16[2,128,1536]{2,1,0:T(8,128)(2,1)S(1)}, bf16[2,128,1536]{2,1,0:T(8,128)(2,1)S(1)}, u32[]{:S(2)}, u32[]{:S(2)}) collective-permute-start(bf16[2,128,1536]{2,1,0:T(8,128)(2,1)S(1)} %shard_map.155.refs_0_), channel_id=1, source_target_pairs={{2,10},{4,12},{26,18},{28,20},{3,11},{5,13},{27,19},{29,21}} | collective-permute-start | bytes 2359304 | tf_op jit(solution)/shard_map/ppermute | solution.py:457
  157.7 5.3 %shard_map.156 = (bf16[1152,1536]{1,0:T(8,128)(2,1)}, f32[8,128]{1,0:T(8,128)S(1)}) custom-call(bf16[1152,2048]{1,0:T(8,128)(2,1)S(1)} %get-tuple-element.50.attention_ref, bf16[2048,1536]{1,0:T(8,128)(2,1)S(1)} %bitcast.25, f32[1,1536]{1,0:T(1,128)S(1)} %convert_element_type.19.gate_ref, bf16[2,128,1536]{2,1,0:T(8,128)(2,1)S(1)} %shard_map.155.refs_0_), custom_call_target="tpu_custom_call" | custom-call | flops 1 | bytes 1 | tf_op jit(solution)/shard_map/pallas_call | solution.py:423
  163.0 3.2 %collective-permute-done.15.refs_1_.refs_3_ = bf16[2,128,1536]{2,1,0:T(8,128)(2,1)S(1)} collective-permute-done((bf16[2,128,1536]{2,1,0:T(8,128)(2,1)S(1)}, bf16[2,128,1536]{2,1,0:T(8,128)(2,1)S(1)}, u32[]{:S(2)}, u32[]{:S(2)}) %collective-permute-start.15) | collective-permute-done | bytes 786464 | tf_op jit(solution)/shard_map/ppermute | solution.py:457
  168.2 4.4 %collective-permute-start.19 = (bf16[1,128,1536]{2,1,0:T(8,128)(2,1)S(1)}, bf16[1,128,1536]{2,1,0:T(8,128)(2,1)S(1)}, u32[]{:S(2)}, u32[]{:S(2)}) collective-permute-start(bf16[1,128,1536]{2,1,0:T(8,128)(2,1)S(1)} %get-tuple-element.64), channel_id=1, source_target_pairs={{2,26},{4,28},{26,2},{28,4},{3,27},{5,29},{27,3},{29,5}} | collective-permute-start | bytes 1179656 | tf_op jit(solution)/shard_map/ppermute | solution.py:457
  175.5 5.3 %shard_map.159 = (bf16[1152,1536]{1,0:T(8,128)(2,1)}, f32[8,128]{1,0:T(8,128)S(1)}) custom-call(bf16[1152,2048]{1,0:T(8,128)(2,1)S(1)} %get-tuple-element.50.attention_ref, bf16[2048,1536]{1,0:T(8,128)(2,1)S(1)} %bitcast.25, f32[1,1536]{1,0:T(1,128)S(1)} %convert_element_type.19.gate_ref, ...), custom_call_target="tpu_custom_call", output_to_operand_aliasing={{0}: (3, {})} | custom-call | flops 20000000000 | bytes 20000000 | tf_op jit(solution)/shard_map/pallas_call | solution.py:423
  181.8 4.1 %collective-permute-done.20.refs_6_ = bf16[1,128,1536]{2,1,0:T(8,128)(2,1)S(1)} collective-permute-done((bf16[1,128,1536]{2,1,0:T(8,128)(2,1)S(1)}, bf16[1,128,1536]{2,1,0:T(8,128)(2,1)S(1)}, u32[]{:S(2)}, u32[]{:S(2)}) %collective-permute-start.20) | collective-permute-done | bytes 393248 | tf_op jit(solution)/shard_map/ppermute | solution.py:457
  (86 shorter events, 29.1 us)
Async XLA Ops:
  7.2 76.7 %all-gather.2.cloned.1.call-start = ((), (), s32[]{:S(2)}) async-start(), calls=%async_computation | async-start | bytes 6684672 | tf_op jit(solution)/shard_map/all_gather | solution.py:472
  10.6 4.7 %copy-start = (bf16[576,2048]{1,0:T(8,128)(2,1)S(1)}, bf16[576,2048]{1,0:T(8,128)(2,1)}, u32[]{:S(2)}) copy-start(bf16[576,2048]{1,0:T(8,128)(2,1)} %q_ref.15) | copy-start | bytes 7077892
  10.6 22.7 %collective-permute-start.1 = (bf16[3,576,256]{2,1,0:T(8,128)(2,1)}, bf16[3,576,256]{2,1,0:T(8,128)(2,1)S(1)}, u32[]{:S(2)}, u32[]{:S(2)}) collective-permute-start(bf16[3,576,256]{2,1,0:T(8,128)(2,1)} %shard_map.140.rest_0_), channel_id=1, source_target_pairs={{0,1},{1,0},{2,3},{3,2},{4,5},{5,4},{6,7},{7,6},{8,9},{9,8},{10,11... | collective-permute-start | bytes 2654216 | tf_op jit(solution)/shard_map/ppermute | solution.py:484
  14.9 37.5 %collective-permute-start.3 = (bf16[3,576,256]{2,1,0:T(8,128)(2,1)}, bf16[3,576,256]{2,1,0:T(8,128)(2,1)S(1)}, u32[]{:S(2)}, u32[]{:S(2)}) collective-permute-start(bf16[3,576,256]{2,1,0:T(8,128)(2,1)} %shard_map.141.rest_0_), channel_id=1, source_target_pairs={{0,1},{1,0},{2,3},{3,2},{4,5},{5,4},{6,7},{7,6},{8,9},{9,8},{10,11... | collective-permute-start | bytes 2654216 | tf_op jit(solution)/shard_map/ppermute | solution.py:484
  19.9 3.0 %copy-start.10 = (s32[1152]{0:T(1024)S(1)}, s32[1152]{0:T(1024)}, u32[]{:S(2)}) copy-start(s32[1152]{0:T(1024)} %constant.80) | copy-start | bytes 13828
  19.9 3.0 %copy-start.11 = (s32[1152]{0:T(1024)S(1)}, s32[1152]{0:T(1024)}, u32[]{:S(2)}) copy-start(s32[1152]{0:T(1024)} %constant.82) | copy-start | bytes 13828
  19.9 3.0 %copy-start.12 = (s32[1152]{0:T(1024)S(1)}, s32[1152]{0:T(1024)}, u32[]{:S(2)}) copy-start(s32[1152]{0:T(1024)} %constant.84) | copy-start | bytes 13828
  21.1 50.2 %collective-permute-start.5 = (bf16[3,576,256]{2,1,0:T(8,128)(2,1)S(1)}, bf16[3,576,256]{2,1,0:T(8,128)(2,1)S(1)}, u32[]{:S(2)}, u32[]{:S(2)}) collective-permute-start(bf16[3,576,256]{2,1,0:T(8,128)(2,1)S(1)} %shard_map.142.rest_0_), channel_id=1, source_target_pairs={{0,1},{1,0},{2,3},{3,2},{4,5},{5,4},{6,7},{7,6},{8,9},{9,8},{10,11... | collective-permute-start | bytes 2654216 | tf_op jit(solution)/shard_map/ppermute | solution.py:484
  23.7 47.6 %copy-start.3 = (f32[16,24,1152]{2,1,0:T(8,128)}, f32[16,24,1152]{2,1,0:T(8,128)S(1)}, u32[]{:S(2)}) copy-start(f32[16,24,1152]{2,1,0:T(8,128)S(1)} %and_select_fusion.bias_ref) | copy-start | bytes 5308420
  40.6 19.0 %copy-start.9 = (bf16[1,1536]{1,0:T(2,128)(2,1)S(1)}, bf16[1,1536]{1,0:T(2,128)(2,1)}, u32[]{:S(2)}) copy-start(bf16[1,1536]{1,0:T(2,128)(2,1)} %param.20) | copy-start | bytes 9220
  60.8 23.3 %collective-permute-start.4 = (bf16[1152,256]{1,0:T(8,128)(2,1)}, bf16[1152,256]{1,0:T(8,128)(2,1)}, u32[]{:S(2)}, u32[]{:S(2)}) collective-permute-start(bf16[1152,256]{1,0:T(8,128)(2,1)} %shard_map.144.rest_0_.refs_2_), channel_id=1, source_target_pairs={{0,1},{1,0},{2,3},{3,2},{4,5},{5,4},{6,7},{7,6},{8,9},{9,8},{10,11... | collective-permute-start | bytes 1769480 | tf_op jit(solution)/shard_map/ppermute | solution.py:484
  62.4 34.3 %collective-permute-start.2 = (bf16[1152,256]{1,0:T(8,128)(2,1)}, bf16[1152,256]{1,0:T(8,128)(2,1)}, u32[]{:S(2)}, u32[]{:S(2)}) collective-permute-start(bf16[1152,256]{1,0:T(8,128)(2,1)} %shard_map.143.rest_0_.refs_0_), channel_id=1, source_target_pairs={{0,1},{1,0},{2,3},{3,2},{4,5},{5,4},{6,7},{7,6},{8,9},{9,8},{10,11... | collective-permute-start | bytes 1769480 | tf_op jit(solution)/shard_map/ppermute | solution.py:484
  62.9 52.8 %collective-permute-start.7 = (bf16[3,576,256]{2,1,0:T(8,128)(2,1)S(1)}, bf16[3,576,256]{2,1,0:T(8,128)(2,1)}, u32[]{:S(2)}, u32[]{:S(2)}) collective-permute-start(bf16[3,576,256]{2,1,0:T(8,128)(2,1)S(1)} %shard_map.145.rest_1_), channel_id=1, source_target_pairs={{0,1},{1,0},{2,3},{3,2},{4,5},{5,4},{6,7},{7,6},{8,9},{9,8},{10,11... | collective-permute-start | bytes 2654216 | tf_op jit(solution)/shard_map/ppermute | solution.py:484
  71.3 8.8 %copy-start.8 = (bf16[1152,1536]{1,0:T(8,128)(2,1)S(1)}, bf16[1152,1536]{1,0:T(8,128)(2,1)}, u32[]{:S(2)}) copy-start(bf16[1152,1536]{1,0:T(8,128)(2,1)} %param.21) | copy-start | bytes 10616836
  78.6 49.6 %collective-permute-start.6 = (bf16[1152,256]{1,0:T(8,128)(2,1)}, bf16[1152,256]{1,0:T(8,128)(2,1)S(1)}, u32[]{:S(2)}, u32[]{:S(2)}) collective-permute-start(bf16[1152,256]{1,0:T(8,128)(2,1)} %shard_map.146.refs_0_.refs_4_), channel_id=1, source_target_pairs={{0,1},{1,0},{2,3},{3,2},{4,5},{5,4},{6,7},{7,6},{8,9},{9,8},{10,11... | collective-permute-start | bytes 1769480 | tf_op jit(solution)/shard_map/ppermute | solution.py:484
  104.7 3.5 %collective-permute-start = (bf16[4,128,1536]{2,1,0:T(8,128)(2,1)S(1)}, bf16[4,128,1536]{2,1,0:T(8,128)(2,1)S(1)}, u32[]{:S(2)}, u32[]{:S(2)}) collective-permute-start(bf16[4,128,1536]{2,1,0:T(8,128)(2,1)S(1)} %get-tuple-element.22), channel_id=1, source_target_pairs={{0,2},{2,0},{4,6},{6,4},{8,10},{10,8},{12,14},{14,12},{16,18},{18,... | collective-permute-start | bytes 4718600 | tf_op jit(solution)/shard_map/cond/branch_1_fun/ppermute | solution.py:457
  110.0 24.7 %collective-permute-start.10 = (bf16[4,128,1536]{2,1,0:T(8,128)(2,1)}, bf16[4,128,1536]{2,1,0:T(8,128)(2,1)S(1)}, u32[]{:S(2)}, u32[]{:S(2)}) collective-permute-start(bf16[4,128,1536]{2,1,0:T(8,128)(2,1)} %get-tuple-element.82.rest_0_.refs_0_.refs_2_), channel_id=1, source_target_pairs={{2,6},{4,0},{10,14},{12,8},{18,22},{20,16},{26,30},{28,24},{3,7},{... | collective-permute-start | bytes 4718600 | tf_op jit(solution)/shard_map/ppermute | solution.py:457
  123.7 16.0 %collective-permute-start.8 = (bf16[1152,256]{1,0:T(8,128)(2,1)}, bf16[1152,256]{1,0:T(8,128)(2,1)S(1)}, u32[]{:S(2)}, u32[]{:S(2)}) collective-permute-start(bf16[1152,256]{1,0:T(8,128)(2,1)} %shard_map.147.refs_3_.refs_0_.refs_6_), channel_id=1, source_target_pairs={{0,1},{1,0},{2,3},{3,2},{4,5},{5,4},{6,7},{7,6},{8,9},{9,8},{10,11... | collective-permute-start | bytes 1769480 | tf_op jit(solution)/shard_map/ppermute | solution.py:484
  134.6 3.4 %collective-permute-start.9 = (bf16[2,128,1536]{2,1,0:T(8,128)(2,1)S(1)}, bf16[2,128,1536]{2,1,0:T(8,128)(2,1)S(1)}, u32[]{:S(2)}, u32[]{:S(2)}) collective-permute-start(bf16[2,128,1536]{2,1,0:T(8,128)(2,1)S(1)} %get-tuple-element.47.refs_4_), channel_id=1, source_target_pairs={{0,2},{2,0},{4,6},{6,4},{8,10},{10,8},{12,14},{14,12},{16,18},{18,... | collective-permute-start | bytes 2359304 | tf_op jit(solution)/shard_map/ppermute | solution.py:457
  134.7 5.0 %copy-start.7 = (bf16[1152,1536]{1,0:T(8,128)(2,1)S(1)}, bf16[1152,1536]{1,0:T(8,128)(2,1)}, u32[]{:S(2)}) copy-start(bf16[1152,1536]{1,0:T(8,128)(2,1)} %multiply_convert_fusion.refs_2_) | copy-start | bytes 10616836
  137.1 16.5 %collective-permute-start.12 = (bf16[2,128,1536]{2,1,0:T(8,128)(2,1)S(1)}, bf16[2,128,1536]{2,1,0:T(8,128)(2,1)S(1)}, u32[]{:S(2)}, u32[]{:S(2)}) collective-permute-start(bf16[2,128,1536]{2,1,0:T(8,128)(2,1)S(1)} %get-tuple-element.48.refs_2_), channel_id=1, source_target_pairs={{0,8},{6,14},{8,0},{14,6},{16,24},{22,30},{24,16},{30,22},{1,9},{7... | collective-permute-start | bytes 2359304 | tf_op jit(solution)/shard_map/ppermute | solution.py:457
  138.2 16.1 %collective-permute-start.11 = (bf16[2,128,1536]{2,1,0:T(8,128)(2,1)S(1)}, bf16[2,128,1536]{2,1,0:T(8,128)(2,1)S(1)}, u32[]{:S(2)}, u32[]{:S(2)}) collective-permute-start(bf16[2,128,1536]{2,1,0:T(8,128)(2,1)S(1)} %shard_map.150.refs_3_.refs_0_), channel_id=1, source_target_pairs={{0,4},{6,2},{8,12},{14,10},{16,20},{22,18},{24,28},{30,26},{1,5},{... | collective-permute-start | bytes 2359304 | tf_op jit(solution)/shard_map/ppermute | solution.py:457
  139.7 18.0 %slice-start = ((s8[6291456]{0:T(1024)(128)(4,1)}), s8[4194304]{0:T(1024)(128)(4,1)S(1)}, s32[]{:S(2)}) async-start(s8[6291456]{0:T(1024)(128)(4,1)} %bitcast.24), calls=%async_computation.1 | async-start | bytes 8388608
  143.5 14.2 %slice-start.1 = ((s8[6291456]{0:T(1024)(128)(4,1)}), s8[2097152]{0:T(1024)(128)(4,1)S(1)}, s32[]{:S(2)}) async-start(s8[6291456]{0:T(1024)(128)(4,1)} %bitcast.24), calls=%async_computation.2 | async-start | bytes 4194304
  143.5 8.6 %collective-permute-start.13 = (bf16[2,128,1536]{2,1,0:T(8,128)(2,1)S(1)}, bf16[2,128,1536]{2,1,0:T(8,128)(2,1)S(1)}, u32[]{:S(2)}, u32[]{:S(2)}) collective-permute-start(bf16[2,128,1536]{2,1,0:T(8,128)(2,1)S(1)} %get-tuple-element.49.refs_8_), channel_id=1, source_target_pairs={{0,2},{2,0},{4,6},{6,4},{8,10},{10,8},{12,14},{14,12},{16,18},{18,... | collective-permute-start | bytes 2359304 | tf_op jit(solution)/shard_map/ppermute | solution.py:457
  152.3 13.9 %collective-permute-start.15 = (bf16[2,128,1536]{2,1,0:T(8,128)(2,1)S(1)}, bf16[2,128,1536]{2,1,0:T(8,128)(2,1)S(1)}, u32[]{:S(2)}, u32[]{:S(2)}) collective-permute-start(bf16[2,128,1536]{2,1,0:T(8,128)(2,1)S(1)} %shard_map.153.refs_4_.refs_0_.refs_2_), channel_id=1, source_target_pairs={{0,4},{6,2},{8,12},{14,10},{16,20},{22,18},{24,28},{30,26},{1,5},{... | collective-permute-start | bytes 2359304 | tf_op jit(solution)/shard_map/ppermute | solution.py:457
  154.5 19.4 %collective-permute-start.14 = (bf16[2,128,1536]{2,1,0:T(8,128)(2,1)S(1)}, bf16[2,128,1536]{2,1,0:T(8,128)(2,1)S(1)}, u32[]{:S(2)}, u32[]{:S(2)}) collective-permute-start(bf16[2,128,1536]{2,1,0:T(8,128)(2,1)S(1)} %shard_map.155.refs_0_), channel_id=1, source_target_pairs={{2,10},{4,12},{26,18},{28,20},{3,11},{5,13},{27,19},{29,21}} | collective-permute-start | bytes 2359304 | tf_op jit(solution)/shard_map/ppermute | solution.py:457
  157.0 23.8 %collective-permute-start.16 = (bf16[1,128,1536]{2,1,0:T(8,128)(2,1)S(1)}, bf16[1,128,1536]{2,1,0:T(8,128)(2,1)S(1)}, u32[]{:S(2)}, u32[]{:S(2)}) collective-permute-start(bf16[1,128,1536]{2,1,0:T(8,128)(2,1)S(1)} %get-tuple-element.54.refs_2_), channel_id=1, source_target_pairs={{0,16},{6,22},{8,24},{14,30},{16,0},{22,6},{24,8},{30,14},{1,17},{... | collective-permute-start | bytes 1179656 | tf_op jit(solution)/shard_map/ppermute | solution.py:457
  166.9 14.9 %collective-permute-start.18 = (bf16[1,128,1536]{2,1,0:T(8,128)(2,1)S(1)}, bf16[1,128,1536]{2,1,0:T(8,128)(2,1)S(1)}, u32[]{:S(2)}, u32[]{:S(2)}) collective-permute-start(bf16[1,128,1536]{2,1,0:T(8,128)(2,1)S(1)} %get-tuple-element.64), channel_id=1, source_target_pairs={{10,26},{12,28},{18,2},{20,4},{11,27},{13,29},{19,3},{21,5}} | collective-permute-start | bytes 1179656 | tf_op jit(solution)/shard_map/ppermute | solution.py:457
  168.2 13.6 %collective-permute-start.19 = (bf16[1,128,1536]{2,1,0:T(8,128)(2,1)S(1)}, bf16[1,128,1536]{2,1,0:T(8,128)(2,1)S(1)}, u32[]{:S(2)}, u32[]{:S(2)}) collective-permute-start(bf16[1,128,1536]{2,1,0:T(8,128)(2,1)S(1)} %get-tuple-element.64), channel_id=1, source_target_pairs={{2,26},{4,28},{26,2},{28,4},{3,27},{5,29},{27,3},{29,5}} | collective-permute-start | bytes 1179656 | tf_op jit(solution)/shard_map/ppermute | solution.py:457
  172.6 13.3 %collective-permute-start.20 = (bf16[1,128,1536]{2,1,0:T(8,128)(2,1)S(1)}, bf16[1,128,1536]{2,1,0:T(8,128)(2,1)S(1)}, u32[]{:S(2)}, u32[]{:S(2)}) collective-permute-start(bf16[1,128,1536]{2,1,0:T(8,128)(2,1)S(1)} %get-tuple-element.57.refs_6_), channel_id=1, source_target_pairs={{10,2},{12,4},{18,26},{20,28},{11,3},{13,5},{19,27},{21,29}} | collective-permute-start | bytes 1179656 | tf_op jit(solution)/shard_map/ppermute | solution.py:457
  174.8 6.0 %collective-permute-start.17 = (bf16[1,128,1536]{2,1,0:T(8,128)(2,1)S(1)}, bf16[1,128,1536]{2,1,0:T(8,128)(2,1)S(1)}, u32[]{:S(2)}, u32[]{:S(2)}) collective-permute-start(bf16[1,128,1536]{2,1,0:T(8,128)(2,1)S(1)} %get-tuple-element.58.refs_1_), channel_id=1, source_target_pairs={{10,18},{12,20},{18,10},{20,12},{11,19},{13,21},{19,11},{21,13}} | collective-permute-start | bytes 1179656 | tf_op jit(solution)/shard_map/ppermute | solution.py:457
  (9 other events, 19.5 us)
Sparse Core Ops, SparseCore 0:
  10.3 62.1 all-gather.1
